TPU v7x, 128 devices: a whole 4x4x4 slice. The times are simulated.
128 devices in a mesh: region: 4 (over x_hi, core), fsdp: 4 (over z), tensor: 8 (over y, x_lo).
Axes of the slice: x: 4 (x_hi: 2, x_lo: 2; x = x_hi * 2 + x_lo), y: 4, z: 4, core: 2. Of those that a mesh axis runs over, the one named last changes fastest.
Arguments:
- gate_pre: bfloat16 [4, 2048, 14336], P('region', 'fsdp', 'tensor'), may hold values from -6 to 6
- up_pre: bfloat16 [4, 2048, 14336], P('region', 'fsdp', 'tensor'), may hold values from -6 to 6
- out_grad: bfloat16 [4, 2048, 4096], P('region', 'tensor', 'fsdp'), may hold values from -6 to 6
- weights: bfloat16 [4, 14336, 4096], P('region', 'tensor', 'fsdp'), may hold values from -6 to 6
- first_moment: bfloat16 [4, 14336, 4096], P('region', 'tensor', 'fsdp'), may hold values from -0.015625 to 0.015625
- second_moment: float32 [4, 14336, 4096], P('region', 'tensor', 'fsdp'), may hold values from 1e-06 to 1e-05
- anchor: float32 [8, 4, 448, 4096], P('tensor', 'region', None, 'fsdp'), may hold values from -6 to 6
- momentum: float32 [8, 4, 448, 4096], P('tensor', 'region', None, 'fsdp'), may hold values from -4 to 4
Outputs:
- new_params: bfloat16 [14336, 4096], P('tensor', 'fsdp')
All inputs are finite; a program needn't handle non-finite values.
Results may differ from a plain program's by a relative error of at most 0.0017.
Values may be sent and summed in bfloat16 or wider, within the bound.
No kernel may reach another device: no remote copies, remote signals or barrier semaphores. Data moves between devices by JAX's collectives and lax.ppermute only.
A program may use at most 192 MiB of HBM per device.

v0:
```python
import jax
import jax.numpy as jnp
from jax import lax
from jax.sharding import PartitionSpec as P

decay_first = 0.9
decay_second = 0.95
inner_rate = 0.25
weight_decay = 0.1
epsilon = 1e-08
outer_rate = 0.7
nesterov = 0.9


def activate(gate_rows, up_rows):
    return (jax.nn.silu(gate_rows.astype(jnp.float32)) * up_rows.astype(jnp.float32)).astype(
        jnp.bfloat16
    )


def local(gate_pre, up_pre, out_grad, weights, first_moment, second_moment, anchor, momentum):
    owner_shape = (anchor.shape[2], anchor.shape[3])
    anchor_local = anchor.reshape(owner_shape)
    momentum_local = momentum.reshape(owner_shape)
    incoming = lax.all_gather(out_grad[0], "tensor", axis=0, tiled=True)
    tok_count = incoming.shape[0]
    hidden = activate(gate_pre[0], up_pre[0])
    summed_grad = lax.dot_general(
        lax.all_gather(hidden, "fsdp", axis=0, tiled=True),
        incoming,
        (((0,), (0,)), ((), ())),
        preferred_element_type=jnp.float32,
    )
    gradient = summed_grad * (1.0 / tok_count)
    first_new = decay_first * first_moment[0].astype(jnp.float32) + (1.0 - decay_first) * gradient
    second_new = decay_second * second_moment[0] + (1.0 - decay_second) * gradient * gradient
    master = weights[0].astype(jnp.float32)
    inner = master - inner_rate * (
        first_new / (jnp.sqrt(second_new) + epsilon) + weight_decay * master
    )
    replicas = lax.axis_size("region")
    owned = lax.psum_scatter(inner, "region", scatter_dimension=0, tiled=True)
    pseudo = anchor_local - owned / replicas
    momentum_new = nesterov * momentum_local + pseudo
    fresh = (anchor_local - outer_rate * (pseudo + nesterov * momentum_new)).astype(jnp.bfloat16)
    return lax.all_gather(fresh, "region", axis=0, tiled=True)


def solution(mesh):
    placed = (
        P("region", "fsdp", "tensor"),
        P("region", "fsdp", "tensor"),
        P("region", "tensor", "fsdp"),
        P("region", "tensor", "fsdp"),
        P("region", "tensor", "fsdp"),
        P("region", "tensor", "fsdp"),
        P("tensor", "region", None, "fsdp"),
        P("tensor", "region", None, "fsdp"),
    )
    return jax.shard_map(
        local, mesh=mesh, in_specs=placed, out_specs=P("tensor", "fsdp"), check_vma=False
    )
```

profile of v0, /device:TPU:1, one launch (start us, length us, event | category | flops | bytes accessed | tf_op | source)
XLA Modules:
  0.0 323.8 jit_solution(2080936046749270988)
XLA Ops:
  6.5 0.0 all-gather.9.cloned.1.call-start
  6.5 0.7 all-gather.9.cloned.1.call-update
  7.3 0.0 all-gather.5.cloned.1.call-start
  7.3 4.4 %fusion.13 = bf16[512,1792]{1,0:T(8,128)(2,1)} fusion(bf16[1,512,1792]{2,1,0:T(8,128)(2,1)} %param.9, bf16[1,512,1792]{2,1,0:T(8,128)(2,1)} %param.8), kind=kLoop, calls=%fused_computation.17 | loop fusion | flops 7340032 | bytes 5505024 | tf_op jit(solution)/shard_map/convert_element_type | solution.py:16
  11.7 0.0 all-gather.5.cloned.1.call-update
  11.7 0.0 reduce-scatter.2.cloned.1.call-start
  11.8 91.0 %all-gather.9.cloned.1.call-done = bf16[1,2048,1024]{2,1,0:T(8,128)(2,1)} async-done(((bf16[1,256,1024]{2,1,0:T(8,128)(2,1)}), bf16[1,2048,1024]{2,1,0:T(8,128)(2,1)}) %all-gather.9.cloned.1.call-update) | async-done | bytes 4194320 | tf_op jit(solution)/shard_map/all_gather | solution.py:25
  102.8 76.5 %all-gather.5.cloned.1.call-done = bf16[2048,1792]{1,0:T(8,128)(2,1)} async-done(((bf16[512,1792]{1,0:T(8,128)(2,1)}), bf16[2048,1792]{1,0:T(8,128)(2,1)}) %all-gather.5.cloned.1.call-update) | async-done | bytes 7340048 | tf_op jit(solution)/shard_map/all_gather | solution.py:29
  179.2 21.4 %convert_subtract_fusion = f32[1792,1024]{1,0:T(8,128)} fusion(f32[1,1792,1024]{2,1,0:T(8,128)} %param.13, bf16[1,1792,1024]{2,1,0:T(8,128)(2,1)} %param.12, bf16[2048,1792]{1,0:T(8,128)(2,1)} %all-gather.5.cloned.1.call-done, bf16[1,2048,1024]{2,1,0:T(8,128)(2,1)} %all-gather.9.cloned.1.call-done, bf16[1,1792,1024]{2,1,0:T(8,128)(2,1)} %param.11), kind=kOutput, calls=%fused_computation | convolution fusion | flops 7545552896 | bytes 33554432 | tf_op jit(solution)/shard_map/dot_general | solution.py:28
  200.6 0.0 copy-start
  200.6 0.0 reduce-scatter.2.cloned.1.call-update
  200.7 0.0 all-gather.7.cloned.1.call-start
  200.7 73.1 %reduce-scatter.2.cloned.1.call-done = f32[448,1024]{1,0:T(8,128)} async-done(((f32[1792,1024]{1,0:T(8,128)}), f32[448,1024]{1,0:T(8,128)}) %reduce-scatter.2.cloned.1.call-update) | async-done | bytes 1835024 | tf_op jit(solution)/shard_map/reduce_scatter | solution.py:42
  273.8 0.0 copy-done
  273.8 3.7 %fusion.18 = bf16[448,1024]{1,0:T(8,128)(2,1)} fusion(f32[1,1,448,1024]{3,2,1,0:T(8,128)S(1)} %copy-done, f32[1,1,448,1024]{3,2,1,0:T(8,128)} %param.15, f32[448,1024]{1,0:T(8,128)} %reduce-scatter.2.cloned.1.call-done), kind=kLoop, calls=%fused_computation.23 | loop fusion | flops 4128768 | bytes 6422528 | tf_op jit(solution)/shard_map/convert_element_type | solution.py:45
  277.4 0.0 all-gather.7.cloned.1.call-update
  277.4 35.5 %all-gather.7.cloned.1.call-done = bf16[1792,1024]{1,0:T(8,128)(2,1)} async-done(((bf16[448,1024]{1,0:T(8,128)(2,1)}), bf16[1792,1024]{1,0:T(8,128)(2,1)}) %all-gather.7.cloned.1.call-update) | async-done | bytes 3670032 | tf_op jit(solution)/shard_map/all_gather | solution.py:46
  313.0 4.2 %copy.10 = bf16[1792,1024]{1,0:T(8,128)(2,1)} copy(bf16[1792,1024]{1,0:T(8,128)(2,1)} %all-gather.7.cloned.1.call-done) | data formatting | bytes 7340032
Async XLA Ops:
  6.5 96.2 %all-gather.9.cloned.1.call-start = ((), (), s32[]{:S(2)}) async-start(), calls=%async_computation.4 | async-start | bytes 4718592 | tf_op jit(solution)/shard_map/all_gather | solution.py:25
  7.3 172.0 %all-gather.5.cloned.1.call-start = ((), (), s32[]{:S(2)}) async-start(), calls=%async_computation.1 | async-start | bytes 9175040 | tf_op jit(solution)/shard_map/all_gather | solution.py:29
  11.7 262.0 %reduce-scatter.2.cloned.1.call-start = ((), (), s32[]{:S(2)}) async-start(), calls=%async_computation.2 | async-start | bytes 9175040 | tf_op jit(solution)/shard_map/reduce_scatter | solution.py:42
  200.6 73.1 %copy-start = (f32[1,1,448,1024]{3,2,1,0:T(8,128)S(1)}, f32[1,1,448,1024]{3,2,1,0:T(8,128)}, u32[]{:S(2)}) copy-start(f32[1,1,448,1024]{3,2,1,0:T(8,128)} %param.14) | copy-start | bytes 5505028
  200.7 112.3 %all-gather.7.cloned.1.call-start = ((), (), s32[]{:S(2)}) async-start(), calls=%async_computation.3 | async-start | bytes 4587520 | tf_op jit(solution)/shard_map/all_gather | solution.py:46
Sparse Core Ops, SparseCore 0:
  9.0 93.7 all-gather.8
  104.4 74.7 all-gather.4
  200.8 72.9 reduce-scatter.1
  277.6 35.3 all-gather.6
where the time goes:
time: 324 us
  waiting for transfers between devices  277 us (85%)
  matrix products  21.4 us (7%)
  between operations  13.1 us (4%)
  other arithmetic  8.06 us (2%)
  local copies, waits for them, and re-layouts  4.25 us (1%)
    all_gather x1, waiting for transfers between devices, local(): incoming = lax.all_gather(out_grad[0], 'tensor', axis=0, tiled=True)  91 us
    all_gather x1, waiting for transfers between devices, local(): lax.all_gather(hidden, 'fsdp', axis=0, tiled=True)  76.5 us
    reduce_scatter x1, waiting for transfers between devices, local(): owned = lax.psum_scatter(inner, 'region', scatter_dimension=0, tiled=True)  73.1 us
    all_gather x1, waiting for transfers between devices, local(): return lax.all_gather(fresh, 'region', axis=0, tiled=True)  35.5 us
    dot_general x1, matrix products, local(): lax.dot_general(lax.all_gather(hidden, 'fsdp', axis=0, tiled=True), incom...  21.4 us
  transfers between devices with their start and end apart: 4, of which 4 were waited for; matrix products, arithmetic and copies ran while one was open for 1% of the time, Pallas kernels for 0%

commit v1 on v0

v1 whole, which is shorter than its diff:
```python
import functools

import jax
import jax.numpy as jnp
from jax import lax
from jax.experimental import pallas as pl
from jax.experimental.pallas import tpu as pltpu
from jax.sharding import PartitionSpec as P

decay_first = 0.9
decay_second = 0.95
inner_rate = 0.25
weight_decay = 0.1
epsilon = 1e-08
outer_rate = 0.7
nesterov = 0.9

SIZES = (128, 128, 128, 64)
OWNERS = 4
VMEM = 48 * 1024 * 1024


def offsets(sizes):
    return [sum(sizes[:i]) for i in range(len(sizes))]


def activate_kernel(gate_ref, up_ref, *chunk_refs):
    gate = gate_ref[...].astype(jnp.float32)
    up = up_ref[...].astype(jnp.float32)
    hidden = (gate / (1.0 + jnp.exp(-gate)) * up).astype(jnp.bfloat16)
    turned = hidden.T
    owned = turned.shape[0] // OWNERS
    start = 0
    for ref in chunk_refs:
        rows = ref.shape[0] // OWNERS
        for o in range(OWNERS):
            ref[o * rows : (o + 1) * rows, :] = turned[o * owned + start : o * owned + start + rows, :]
        start += rows


def activate(gate, up, sizes, block=128):
    tokens, units = gate.shape
    spec = pl.BlockSpec((block, units), lambda i: (i, 0))
    return pl.pallas_call(
        activate_kernel,
        grid=(tokens // block,),
        in_specs=[spec, spec],
        out_specs=[pl.BlockSpec((OWNERS * n, block), lambda i: (0, i)) for n in sizes],
        out_shape=[jax.ShapeDtypeStruct((OWNERS * n, tokens), jnp.bfloat16) for n in sizes],
        compiler_params=pltpu.CompilerParams(vmem_limit_bytes=VMEM),
        cost_estimate=pl.CostEstimate(
            flops=6 * tokens * units, bytes_accessed=6 * tokens * units, transcendentals=tokens * units
        ),
        name="activate",
    )(gate, up)


def inner_kernel(where, *refs):
    pieces, refs = refs[:8], refs[8:]
    own, before, after, far_a, far_b, weights, first, second, keep, send, grads, sems = refs
    d, steps = pl.program_id(0), pl.num_programs(0)
    z, y, x_lo, core = where[0], where[1], where[2], where[3]
    width = weights.shape[2]
    hops = (0, 0, 3, 3, 1, 1, 2, 2)

    def fetch(i, tile):
        block = lax.rem(y + hops[i], 4)
        half = x_lo if i % 2 == 0 else 1 - x_lo
        row = pl.multiple_of(block * 512 + half * 256, 256)
        cols = pl.ds(tile * width, width)
        return pltpu.make_async_copy(
            pieces[i].at[:, cols], grads.at[tile, pl.ds(row, 256), :], sems.at[tile, i]
        )

    tiles = grads.shape[0]

    @pl.when(d == 0)
    def _():
        for tile in range(tiles):
            for i in range(8):
                fetch(i, tile).start()

    for tile in range(tiles):

        @pl.when(d == tile)
        def _(tile=tile):
            for i in range(8):
                fetch(i, tile).wait()

    def block_of(hop):
        row = pl.multiple_of(lax.rem(z + hop, 4) * 512, 512)
        return grads[d, pl.ds(row, 512), :]

    def dot(a, b):
        return jnp.dot(a, b, preferred_element_type=jnp.float32)

    total = dot(own[...], block_of(0)) + dot(before[...], block_of(3)) + dot(after[...], block_of(1))
    far = block_of(2)
    total = total + jnp.concatenate([dot(far_a[...], far), dot(far_b[...], far)], axis=0)
    gradient = total * (1.0 / 2048)
    rows = weights.shape[1]
    gradient = gradient.reshape(OWNERS, rows, width)
    first_new = decay_first * first[...].astype(jnp.float32) + (1.0 - decay_first) * gradient
    second_new = decay_second * second[...] + (1.0 - decay_second) * gradient * gradient
    master = weights[...].astype(jnp.float32)
    inner = master - inner_rate * (first_new / (jnp.sqrt(second_new) + epsilon) + weight_decay * master)
    for c in range(2):

        @pl.when(core == c)
        def _(c=c):
            for h in range(2):
                keep[h] = inner[2 * h + c]
                send[h] = inner[2 * h + 1 - c]


def inner_step(where, pieces, hidden, weights, first, second, start, width=256):
    own, before, after, far_a, far_b = hidden
    rows = own.shape[0] // OWNERS
    columns = weights.shape[2]
    whole = lambda a: pl.BlockSpec(a.shape, lambda d, w: (0, 0))
    tile = pl.BlockSpec((OWNERS, rows, width), lambda d, w: (0, start // rows, d))
    out = pl.BlockSpec((2, rows, width), lambda d, w: (0, 0, d))
    shape = jax.ShapeDtypeStruct((2, rows, columns), jnp.float32)
    count = OWNERS * rows * columns
    return pl.pallas_call(
        inner_kernel,
        grid_spec=pltpu.PrefetchScalarGridSpec(
            num_scalar_prefetch=1,
            grid=(columns // width,),
            in_specs=[pl.BlockSpec(memory_space=pl.ANY)] * 8 + [whole(a) for a in hidden] + [tile] * 3,
            out_specs=[out, out],
            scratch_shapes=[
                pltpu.VMEM((columns // width, 2048, width), jnp.bfloat16),
                pltpu.SemaphoreType.DMA((columns // width, 8)),
            ],
        ),
        out_shape=[shape, shape],
        compiler_params=pltpu.CompilerParams(vmem_limit_bytes=VMEM),
        cost_estimate=pl.CostEstimate(
            flops=2 * 2048 * count, bytes_accessed=12 * count + 2 * 2048 * (columns + OWNERS * rows), transcendentals=count
        ),
        name="inner_step",
    )(where, *pieces, *hidden, weights, first, second)


def shift(x, axis, n, step):
    return lax.ppermute(x, axis, [(i, (i + step) % n) for i in range(n)])


def local(gate_pre, up_pre, out_grad, weights, first_moment, second_moment, anchor, momentum):
    z, t, r = lax.axis_index("fsdp"), lax.axis_index("tensor"), lax.axis_index("region")
    y, x_lo, half, core = t // 2, t % 2, r // 2, r % 2
    where = jnp.stack([z, y, x_lo, core]).astype(jnp.int32)
    along_z = functools.partial(shift, axis="fsdp", n=4)
    along_y = lambda x, step: shift(x, "tensor", 8, 2 * step)
    swap = lambda x, axis, n, bit: lax.ppermute(x, axis, [(i, i ^ bit) for i in range(n)])
    other_core = lambda x: swap(x, "region", 4, 1)
    other_chip = lambda x: swap(x, "region", 4, 2)

    mine = out_grad[0]
    pair = swap(mine, "tensor", 8, 1)
    mine_up, mine_down = along_y(mine, 1), along_y(mine, -1)
    pair_up, pair_down = along_y(pair, 1), along_y(pair, -1)
    mine_far, pair_far = along_y(mine_up, 1), along_y(pair_down, -1)
    pieces = [mine, pair, mine_up, pair_up, mine_down, pair_down, mine_far, pair_far]

    chunks = activate(gate_pre[0], up_pre[0], SIZES)
    gathered = []
    for own in chunks:
        before, after = along_z(own, step=1), along_z(own, step=-1)
        middle = own.shape[0] // 2
        far_a = along_z(before[:middle], step=1)
        far_b = along_z(after[middle:], step=-1)
        gathered.append((own, before, after, far_a, far_b))

    gain = outer_rate * (1.0 + nesterov)
    rest = (1.0 - gain) * anchor[0, 0] - outer_rate * nesterov * nesterov * momentum[0, 0]
    rest = rest.astype(jnp.float16)
    rest_there = other_chip(rest)
    rest = jnp.where(half == 0, jnp.stack([rest, rest_there]), jnp.stack([rest_there, rest]))

    by_owner = lambda a: a[0].reshape(OWNERS, 448, 1024)
    w, m, v = by_owner(weights), by_owner(first_moment), by_owner(second_moment)
    out = jnp.zeros((2, 2, 448, 1024), jnp.bfloat16)
    for hidden, rows, start in zip(gathered, SIZES, offsets(SIZES)):
        keep, send = inner_step(where, pieces, hidden, w, m, v, start)
        both = (keep + other_core(send)).astype(jnp.float16)
        both_there = other_chip(both)
        total = both.astype(jnp.float32) + both_there.astype(jnp.float32)
        fresh = rest[:, start : start + rows].astype(jnp.float32) + (gain / 4) * total
        fresh = fresh.astype(jnp.bfloat16)
        fresh_there = other_core(fresh)
        out = lax.dynamic_update_slice(out, fresh[:, None], (0, core, start, 0))
        out = lax.dynamic_update_slice(out, fresh_there[:, None], (0, 1 - core, start, 0))
    return out.reshape(1792, 1024)


def solution(mesh):
    placed = (
        P("region", "fsdp", "tensor"),
        P("region", "fsdp", "tensor"),
        P("region", "tensor", "fsdp"),
        P("region", "tensor", "fsdp"),
        P("region", "tensor", "fsdp"),
        P("region", "tensor", "fsdp"),
        P("tensor", "region", None, "fsdp"),
        P("tensor", "region", None, "fsdp"),
    )
    return jax.shard_map(
        local, mesh=mesh, in_specs=placed, out_specs=P("tensor", "fsdp"), check_vma=False
    )
```

time: 324 us -> 181 us (0.56)
  waiting for transfers between devices: 277 us -> 42.8 us
  starting transfers between devices: 0.12 us -> 65.1 us
  Pallas kernels: 0 us -> 36.3 us
  matrix products: 21.4 us -> 0 us
  between operations: 13.1 us -> 0.32 us
  local copies, waits for them, and re-layouts: 4.25 us -> 16.1 us
  other arithmetic: 8.06 us -> 19 us
    all_gather x3 -> x0, waiting for transfers between devices: 203 us -> none  [the longest x1 91 us: local(): incoming = lax.all_gather(out_grad[0], 'tensor', axis=0, tiled=True)]
    reduce_scatter x1 -> x0, waiting for transfers between devices: 73.1 us -> none  [local(): owned = lax.psum_scatter(inner, 'region', scatter_dimension=0, tiled=True)]
    ppermute x0 -> x36, starting transfers between devices: none -> 65.1 us  [the longest x22 42.3 us: shift(): return lax.ppermute(x, axis, [(i, (i + step) % n) for i in range(n)])]
    ppermute x0 -> x36, waiting for transfers between devices: none -> 42.8 us  [the longest x22 28.1 us: shift(): return lax.ppermute(x, axis, [(i, (i + step) % n) for i in range(n)])]
    pallas_call x0 -> x5, Pallas kernels: none -> 36.3 us  [the longest x4 33.7 us: inner_step(): pl.pallas_call(inner_kernel, grid_spec=pltpu.PrefetchScalarGridSpec(num_s...]
    dot_general x1 -> x0, matrix products: 21.4 us -> none  [local(): lax.dot_general(lax.all_gather(hidden, 'fsdp', axis=0, tiled=True), incom...]
    dynamic_update_slice x0 -> x4, other arithmetic: none -> 7.54 us  [local(): out = lax.dynamic_update_slice(out, fresh[:, None], (0, core, start, 0))]
    unnamed x3 -> x52, local copies, waits for them, and re-layouts: 4.25 us -> 9.35 us
  transfers between devices with their start and end apart: 4 -> 36, of which waited for: 4 -> 14; matrix products, arithmetic and copies ran while one was open for 1% -> 14% of each run, Pallas kernels for 0% -> 20%
where the time goes in v1:
time: 181 us; the launch traced here: 180 us
  starting transfers between devices  65.1 us (36%)
  waiting for transfers between devices  42.8 us (24%)
  Pallas kernels  36.3 us (20%)
  other arithmetic  19 us (10%)
  local copies, waits for them, and re-layouts  16.1 us (9%)
    ppermute x22, starting transfers between devices, shift(): return lax.ppermute(x, axis, [(i, (i + step) % n) for i in range(n)])  42.3 us
    pallas_call x4, Pallas kernels, inner_step(): pl.pallas_call(inner_kernel, grid_spec=pltpu.PrefetchScalarGridSpec(num_s...  33.7 us
    ppermute x22, waiting for transfers between devices, shift(): return lax.ppermute(x, axis, [(i, (i + step) % n) for i in range(n)])  28.1 us
    ppermute x14, starting transfers between devices, local(): lax.ppermute(x, axis, [(i, i ^ bit) for i in range(n)])  22.9 us
    ppermute x14, waiting for transfers between devices, local(): lax.ppermute(x, axis, [(i, i ^ bit) for i in range(n)])  14.7 us
    unnamed x52, local copies, waits for them, and re-layouts  9.35 us
    dynamic_update_slice x4, other arithmetic, local(): out = lax.dynamic_update_slice(out, fresh[:, None], (0, core, start, 0))  7.54 us
    convert_element_type x4, other arithmetic, local(): both = (keep + other_core(send)).astype(jnp.float16)  5.57 us
  transfers between devices with their start and end apart: 36, of which 14 were waited for; matrix products, arithmetic and copies ran while one was open for 14% of the time, Pallas kernels for 20%

profile of v1, /device:TPU:1, one launch (start us, length us, event | category | flops | bytes accessed | tf_op | source)
XLA Modules:
  0.0 179.6 jit_solution(15344814286801039290)
XLA Ops:
  0.0 2.0 %collective-permute-start.1 = (bf16[256,1024]{1,0:T(8,128)(2,1)}, bf16[256,1024]{1,0:T(8,128)(2,1)S(1)}, u32[]{:S(2)}, u32[]{:S(2)}) collective-permute-start(bf16[256,1024]{1,0:T(8,128)(2,1)} %bitcast.34), channel_id=1, source_target_pairs={{0,1},{1,0},{2,3},{3,2},{4,5},{5,4},{6,7},{7,6},{8,9},{9,8},{10,11... | collective-permute-start | bytes 1572872 | tf_op jit(solution)/shard_map/ppermute | solution.py:156
  2.0 1.3 collective-permute-start.2
  3.3 1.5 copy-done.1
  4.8 1.5 copy-done.2
  6.3 2.5 %activate.1 = (bf16[512,512]{1,0:T(8,128)(2,1)S(1)}, bf16[512,512]{1,0:T(8,128)(2,1)S(1)}, bf16[512,512]{1,0:T(8,128)(2,1)S(1)}, bf16[256,512]{1,0:T(8,128)(2,1)}) custom-call(bf16[512,1792]{1,0:T(8,128)(2,1)S(1)} %bitcast.41, bf16[512,1792]{1,0:T(8,128)(2,1)S(1)} %bitcast.42), custom_call_target="tpu_custom_call" | custom-call | flops 5505024 | bytes 5505024 | tf_op jit(solution)/shard_map/activate/pallas_call | solution.py:44
  8.9 0.8 copy-done.10
  9.7 3.8 %collective-permute-start.9 = (bf16[512,512]{1,0:T(8,128)(2,1)S(1)}, bf16[512,512]{1,0:T(8,128)(2,1)S(1)}, u32[]{:S(2)}, u32[]{:S(2)}) collective-permute-start(bf16[512,512]{1,0:T(8,128)(2,1)S(1)} %get-tuple-element.17.refs_8_), channel_id=1, source_target_pairs={{0,24},{8,0},{16,8},{24,16},{1,25},{9,1},{17,9},{25,17},{2,26},{10... | collective-permute-start | bytes 1572872 | tf_op jit(solution)/shard_map/ppermute | solution.py:147
  13.4 3.1 %collective-permute-start.5 = (bf16[256,1024]{1,0:T(8,128)(2,1)S(1)}, bf16[256,1024]{1,0:T(8,128)(2,1)S(1)}, u32[]{:S(2)}, u32[]{:S(2)}) collective-permute-start(bf16[256,1024]{1,0:T(8,128)(2,1)S(1)} %collective-permute-done.1.refs_1_), channel_id=1, source_target_pairs={{0,6},{1,7},{2,0},{3,1},{4,2},{5,3},{6,4},{7,5},{8,14},{9,15},{10,... | collective-permute-start | bytes 1572872 | tf_op jit(solution)/shard_map/ppermute | solution.py:147
  16.6 1.6 collective-permute-start.8
  18.2 0.8 copy-done.12
  19.5 1.0 collective-permute-start.3
  20.5 2.9 %collective-permute-done.9.refs_10_ = bf16[512,512]{1,0:T(8,128)(2,1)S(1)} collective-permute-done((bf16[512,512]{1,0:T(8,128)(2,1)S(1)}, bf16[512,512]{1,0:T(8,128)(2,1)S(1)}, u32[]{:S(2)}, u32[]{:S(2)}) %collective-permute-start.9) | collective-permute-done | bytes 524320 | tf_op jit(solution)/shard_map/ppermute | solution.py:147
  23.4 1.3 collective-permute-start.6
  24.7 1.5 collective-permute-done.5.refs_5_
  26.2 3.4 %collective-permute-start.7 = (bf16[256,1024]{1,0:T(8,128)(2,1)S(1)}, bf16[256,1024]{1,0:T(8,128)(2,1)}, u32[]{:S(2)}, u32[]{:S(2)}) collective-permute-start(bf16[256,1024]{1,0:T(8,128)(2,1)S(1)} %collective-permute-done.5.refs_5_), channel_id=1, source_target_pairs={{0,6},{1,7},{2,0},{3,1},{4,2},{5,3},{6,4},{7,5},{8,14},{9,15},{10,... | collective-permute-start | bytes 1572872 | tf_op jit(solution)/shard_map/ppermute | solution.py:147
  30.7 3.4 %collective-permute-start.11 = (bf16[256,512]{1,0:T(8,128)(2,1)}, bf16[256,512]{1,0:T(8,128)(2,1)S(1)}, u32[]{:S(2)}, u32[]{:S(2)}) collective-permute-start(bf16[256,512]{1,0:T(8,128)(2,1)} %slice.50), channel_id=1, source_target_pairs={{0,24},{8,0},{16,8},{24,16},{1,25},{9,1},{17,9},{25,17},{2,26},{10... | collective-permute-start | bytes 786440 | tf_op jit(solution)/shard_map/ppermute | solution.py:147
  34.1 0.7 slice.49
  34.9 2.6 %collective-permute-done.4.refs_4_ = bf16[256,1024]{1,0:T(8,128)(2,1)S(1)} collective-permute-done((bf16[256,1024]{1,0:T(8,128)(2,1)S(1)}, bf16[256,1024]{1,0:T(8,128)(2,1)S(1)}, u32[]{:S(2)}, u32[]{:S(2)}) %collective-permute-start.4) | collective-permute-done | bytes 524320 | tf_op jit(solution)/shard_map/ppermute | solution.py:147
  37.5 1.6 collective-permute-start.10
  39.2 2.2 %collective-permute-start.16 = (bf16[512,512]{1,0:T(8,128)(2,1)}, bf16[512,512]{1,0:T(8,128)(2,1)S(1)}, u32[]{:S(2)}, u32[]{:S(2)}) collective-permute-start(bf16[512,512]{1,0:T(8,128)(2,1)} %copy-done.10), channel_id=1, source_target_pairs={{0,24},{8,0},{16,8},{24,16},{1,25},{9,1},{17,9},{25,17},{2,26},{10... | collective-permute-start | bytes 1572872 | tf_op jit(solution)/shard_map/ppermute | solution.py:147
  41.4 4.2 %collective-permute-done.10.refs_11_ = bf16[256,512]{1,0:T(8,128)(2,1)} collective-permute-done((bf16[256,512]{1,0:T(8,128)(2,1)}, bf16[256,512]{1,0:T(8,128)(2,1)}, u32[]{:S(2)}, u32[]{:S(2)}) %collective-permute-start.10) | collective-permute-done | bytes 262176 | tf_op jit(solution)/shard_map/ppermute | solution.py:147
  45.6 3.1 %collective-permute-done.7.refs_7_ = bf16[256,1024]{1,0:T(8,128)(2,1)} collective-permute-done((bf16[256,1024]{1,0:T(8,128)(2,1)S(1)}, bf16[256,1024]{1,0:T(8,128)(2,1)}, u32[]{:S(2)}, u32[]{:S(2)}) %collective-permute-start.7) | collective-permute-done | bytes 524320 | tf_op jit(solution)/shard_map/ppermute | solution.py:147
  48.7 1.0 copy-done.4
  49.8 1.0 copy-done.13
  50.8 9.3 %inner_step.4 = (f32[2,128,1024]{2,1,0:T(8,128)}, f32[2,128,1024]{2,1,0:T(8,128)}) custom-call(s32[4]{0:T(128)S(1)} %pad_add_fusion.where, bf16[256,1024]{1,0:T(8,128)(2,1)S(1)} %bitcast.37, bf16[256,1024]{1,0:T(8,128)(2,1)S(1)} %collective-permute-done.1.refs_1_, bf16[256,1024]{1,0:T(8,128)(2,1)S(1)} %collective-permute-done.2.refs_2_, ...), custom_call_target="tpu_custom_call" | custom-call | flops 2147483648 | bytes 12582912 | tf_op jit(solution)/shard_map/inner_step/pallas_call | solution.py:125
  60.1 3.4 %collective-permute-start.12 = (f32[2,128,1024]{2,1,0:T(8,128)}, f32[2,128,1024]{2,1,0:T(8,128)S(1)}, u32[]{:S(2)}, u32[]{:S(2)}) collective-permute-start(f32[2,128,1024]{2,1,0:T(8,128)} %get-tuple-element.19), channel_id=1, source_target_pairs={{0,32},{32,0},{64,96},{96,64},{1,33},{33,1},{65,97},{97,65},{2,34}... | collective-permute-start | bytes 3145736 | tf_op jit(solution)/shard_map/ppermute | solution.py:156
  63.5 2.9 %collective-permute-start.23 = (bf16[512,512]{1,0:T(8,128)(2,1)S(1)}, bf16[512,512]{1,0:T(8,128)(2,1)S(1)}, u32[]{:S(2)}, u32[]{:S(2)}) collective-permute-start(bf16[512,512]{1,0:T(8,128)(2,1)S(1)} %copy-done.8), channel_id=1, source_target_pairs={{0,24},{8,0},{16,8},{24,16},{1,25},{9,1},{17,9},{25,17},{2,26},{10... | collective-permute-start | bytes 1572872 | tf_op jit(solution)/shard_map/ppermute | solution.py:147
  66.4 2.7 %collective-permute-start.18 = (bf16[256,512]{1,0:T(8,128)(2,1)S(1)}, bf16[256,512]{1,0:T(8,128)(2,1)S(1)}, u32[]{:S(2)}, u32[]{:S(2)}) collective-permute-start(bf16[256,512]{1,0:T(8,128)(2,1)S(1)} %slice.53), channel_id=1, source_target_pairs={{0,24},{8,0},{16,8},{24,16},{1,25},{9,1},{17,9},{25,17},{2,26},{10... | collective-permute-start | bytes 786440 | tf_op jit(solution)/shard_map/ppermute | solution.py:147
  69.3 1.4 fusion.1
  70.7 7.2 %collective-permute-done.23.refs_10_ = bf16[512,512]{1,0:T(8,128)(2,1)S(1)} collective-permute-done((bf16[512,512]{1,0:T(8,128)(2,1)S(1)}, bf16[512,512]{1,0:T(8,128)(2,1)S(1)}, u32[]{:S(2)}, u32[]{:S(2)}) %collective-permute-start.23) | collective-permute-done | bytes 524320 | tf_op jit(solution)/shard_map/ppermute | solution.py:147
  77.9 2.7 %collective-permute-start = (f16[448,1024]{1,0:T(8,128)(2,1)}, f16[448,1024]{1,0:T(8,128)(2,1)}, u32[]{:S(2)}, u32[]{:S(2)}) collective-permute-start(f16[448,1024]{1,0:T(8,128)(2,1)} %fusion.1), channel_id=1, source_target_pairs={{0,64},{32,96},{64,0},{96,32},{1,65},{33,97},{65,1},{97,33},{2,66}... | collective-permute-start | bytes 2752520 | tf_op jit(solution)/shard_map/ppermute | solution.py:156
  81.4 3.2 %collective-permute-start.25 = (bf16[256,512]{1,0:T(8,128)(2,1)}, bf16[256,512]{1,0:T(8,128)(2,1)S(1)}, u32[]{:S(2)}, u32[]{:S(2)}) collective-permute-start(bf16[256,512]{1,0:T(8,128)(2,1)} %slice.56), channel_id=1, source_target_pairs={{0,24},{8,0},{16,8},{24,16},{1,25},{9,1},{17,9},{25,17},{2,26},{10... | collective-permute-start | bytes 786440 | tf_op jit(solution)/shard_map/ppermute | solution.py:147
  85.3 0.8 copy-done.5
  86.5 9.0 %inner_step.5 = (f32[2,128,1024]{2,1,0:T(8,128)}, f32[2,128,1024]{2,1,0:T(8,128)}) custom-call(s32[4]{0:T(128)S(1)} %pad_add_fusion.where, bf16[256,1024]{1,0:T(8,128)(2,1)S(1)} %bitcast.38, bf16[256,1024]{1,0:T(8,128)(2,1)S(1)} %collective-permute-done.1.refs_1_, bf16[256,1024]{1,0:T(8,128)(2,1)S(1)} %collective-permute-done.2.refs_2_, ...), custom_call_target="tpu_custom_call" | custom-call | flops 2147483648 | bytes 12582912 | tf_op jit(solution)/shard_map/inner_step/pallas_call | solution.py:125
  95.5 1.6 collective-permute-start.19
  97.1 1.0 add_convert_fusion.5
  98.1 2.3 %collective-permute-start.13 = (f16[2,128,1024]{2,1,0:T(8,128)(2,1)}, f16[2,128,1024]{2,1,0:T(8,128)(2,1)}, u32[]{:S(2)}, u32[]{:S(2)}) collective-permute-start(f16[2,128,1024]{2,1,0:T(8,128)(2,1)} %add_convert_fusion.5), channel_id=1, source_target_pairs={{0,64},{32,96},{64,0},{96,32},{1,65},{33,97},{65,1},{97,33},{2,66}... | collective-permute-start | bytes 1572872 | tf_op jit(solution)/shard_map/ppermute | solution.py:156
  100.4 1.4 fusion
  101.8 3.1 %maximum_select_fusion = f16[2,448,1024]{2,1,0:T(8,128)(2,1)S(1)} fusion(f16[1,448,1024]{2,1,0:T(8,128)(2,1)} %bitcast.2, f16[1,448,1024]{2,1,0:T(8,128)(2,1)} %fusion, pred[]{:T(512)S(6)} %eq.6), kind=kLoop, calls=%fused_computation | loop fusion | flops 2752512 | bytes 3670017 | tf_op jit(solution)/shard_map/jit(_where)/select_n | solution.py:180
  104.9 9.1 %inner_step.6 = (f32[2,128,1024]{2,1,0:T(8,128)}, f32[2,128,1024]{2,1,0:T(8,128)}) custom-call(s32[4]{0:T(128)S(1)} %pad_add_fusion.where, bf16[256,1024]{1,0:T(8,128)(2,1)S(1)} %bitcast.39, bf16[256,1024]{1,0:T(8,128)(2,1)S(1)} %collective-permute-done.1.refs_1_, bf16[256,1024]{1,0:T(8,128)(2,1)S(1)} %collective-permute-done.2.refs_2_, ...), custom_call_target="tpu_custom_call" | custom-call | flops 2147483648 | bytes 12582912 | tf_op jit(solution)/shard_map/inner_step/pallas_call | solution.py:125
  114.0 0.8 collective-permute-start.26
  115.2 2.5 %bitcast_dynamic-update-slice_fusion.5 = (bf16[2,2,448,1024]{3,2,0,1:T(8,128)(2,1)S(1)}, bf16[2,128,1024]{2,1,0:T(8,128)(2,1)}) fusion(bf16[2,2,448,1024]{3,2,0,1:T(8,128)(2,1)S(1)} %broadcast_in_dim.27, s32[]{:T(128)S(6)} %select_n.44, f16[2,128,1024]{2,1,0:T(8,128)(2,1)} %collective-permute-done.13, f16[2,128,1024]{2,1,0:T(8,128)(2,1)} %add_convert_fusion.5, ...), kind=kLoop, calls=%fused_computation.13 | loop fusion | flops 1835008 | bytes 2621444 | tf_op jit(solution)/shard_map/dynamic_update_slice | solution.py:193
  117.7 3.0 %add_convert_fusion.3 = f16[2,128,1024]{2,1,0:T(8,128)(2,1)} fusion(f32[2,128,1024]{2,1,0:T(8,128)S(1)} %copy-done.23, f32[2,128,1024]{2,1,0:T(8,128)} %collective-permute-done.19), kind=kLoop, calls=%fused_computation.5 | loop fusion | flops 524288 | bytes 2621440 | tf_op jit(solution)/shard_map/convert_element_type | solution.py:187
  120.8 2.7 %collective-permute-start.20 = (f16[2,128,1024]{2,1,0:T(8,128)(2,1)}, f16[2,128,1024]{2,1,0:T(8,128)(2,1)}, u32[]{:S(2)}, u32[]{:S(2)}) collective-permute-start(f16[2,128,1024]{2,1,0:T(8,128)(2,1)} %add_convert_fusion.3), channel_id=1, source_target_pairs={{0,64},{32,96},{64,0},{96,32},{1,65},{33,97},{65,1},{97,33},{2,66}... | collective-permute-start | bytes 1572872 | tf_op jit(solution)/shard_map/ppermute | solution.py:156
  123.5 5.0 %collective-permute-start.30 = (bf16[256,512]{1,0:T(8,128)(2,1)}, bf16[256,512]{1,0:T(8,128)(2,1)S(1)}, u32[]{:S(2)}, u32[]{:S(2)}) collective-permute-start(bf16[256,512]{1,0:T(8,128)(2,1)} %get-tuple-element.26.refs_8_), channel_id=1, source_target_pairs={{0,24},{8,0},{16,8},{24,16},{1,25},{9,1},{17,9},{25,17},{2,26},{10... | collective-permute-start | bytes 786440 | tf_op jit(solution)/shard_map/ppermute | solution.py:147
  128.5 2.0 %bitcast_dynamic-update-slice_fusion.4 = bf16[2,2,448,1024]{3,2,0,1:T(8,128)(2,1)} fusion(bf16[2,2,448,1024]{3,2,0,1:T(8,128)(2,1)} %copy-done.14, s32[]{:T(128)S(6)} %select_n.45, bf16[2,128,1024]{2,1,0:T(8,128)(2,1)} %collective-permute-done.14), kind=kLoop, calls=%fused_computation.12 | loop fusion | bytes 1048580 | tf_op jit(solution)/shard_map/dynamic_update_slice | solution.py:194
  130.5 5.1 %collective-permute-done.20 = f16[2,128,1024]{2,1,0:T(8,128)(2,1)} collective-permute-done((f16[2,128,1024]{2,1,0:T(8,128)(2,1)}, f16[2,128,1024]{2,1,0:T(8,128)(2,1)}, u32[]{:S(2)}, u32[]{:S(2)}) %collective-permute-start.20) | collective-permute-done | bytes 524320 | tf_op jit(solution)/shard_map/ppermute | solution.py:156
  135.6 2.6 %bitcast_dynamic-update-slice_fusion.3 = (bf16[2,2,448,1024]{3,2,0,1:T(8,128)(2,1)}, bf16[2,128,1024]{2,1,0:T(8,128)(2,1)S(1)}) fusion(bf16[2,2,448,1024]{3,2,0,1:T(8,128)(2,1)} %bitcast_dynamic-update-slice_fusion.4, s32[]{:T(128)S(6)} %select_n.44, f16[2,128,1024]{2,1,0:T(8,128)(2,1)} %collective-permute-done.20, ...), kind=kLoop, calls=%fused_computation.11 | loop fusion | flops 1835008 | bytes 2621444 | tf_op jit(solution)/shard_map/dynamic_update_slice | solution.py:193
  138.1 1.3 collective-permute-start.21
  139.5 1.4 add_convert_fusion.1
  140.9 2.8 %collective-permute-start.27 = (f16[2,128,1024]{2,1,0:T(8,128)(2,1)S(1)}, f16[2,128,1024]{2,1,0:T(8,128)(2,1)S(1)}, u32[]{:S(2)}, u32[]{:S(2)}) collective-permute-start(f16[2,128,1024]{2,1,0:T(8,128)(2,1)S(1)} %add_convert_fusion.1), channel_id=1, source_target_pairs={{0,64},{32,96},{64,0},{96,32},{1,65},{33,97},{65,1},{97,33},{2,66}... | collective-permute-start | bytes 1572872 | tf_op jit(solution)/shard_map/ppermute | solution.py:156
  143.8 5.1 %collective-permute-start.32 = (bf16[128,512]{1,0:T(8,128)(2,1)S(1)}, bf16[128,512]{1,0:T(8,128)(2,1)S(1)}, u32[]{:S(2)}, u32[]{:S(2)}) collective-permute-start(bf16[128,512]{1,0:T(8,128)(2,1)S(1)} %slice.59), channel_id=1, source_target_pairs={{0,24},{8,0},{16,8},{24,16},{1,25},{9,1},{17,9},{25,17},{2,26},{10... | collective-permute-start | bytes 393224 | tf_op jit(solution)/shard_map/ppermute | solution.py:147
  148.9 0.9 slice.58
  149.9 1.6 collective-permute-done.32.refs_12_
  151.5 4.1 %collective-permute-done.31.refs_11_ = bf16[128,512]{1,0:T(8,128)(2,1)S(1)} collective-permute-done((bf16[128,512]{1,0:T(8,128)(2,1)S(1)}, bf16[128,512]{1,0:T(8,128)(2,1)S(1)}, u32[]{:S(2)}, u32[]{:S(2)}) %collective-permute-start.31) | collective-permute-done | bytes 131104 | tf_op jit(solution)/shard_map/ppermute | solution.py:147
  155.6 6.4 %inner_step.7 = (f32[2,64,1024]{2,1,0:T(8,128)S(1)}, f32[2,64,1024]{2,1,0:T(8,128)S(1)}) custom-call(s32[4]{0:T(128)S(1)} %pad_add_fusion.where, bf16[256,1024]{1,0:T(8,128)(2,1)S(1)} %bitcast.40, bf16[256,1024]{1,0:T(8,128)(2,1)S(1)} %collective-permute-done.1.refs_1_, bf16[256,1024]{1,0:T(8,128)(2,1)S(1)} %collective-permute-done.2.refs_2_, ...), custom_call_target="tpu_custom_call" | custom-call | flops 1073741824 | bytes 8388608 | tf_op jit(solution)/shard_map/inner_step/pallas_call | solution.py:125
  161.9 1.5 collective-permute-start.33
  163.5 1.4 bitcast_dynamic-update-slice_fusion.1
  165.2 1.7 collective-permute-done.28
  166.9 7.1 %collective-permute-done.34 = f16[2,64,1024]{2,1,0:T(8,128)(2,1)S(1)} collective-permute-done((f16[2,64,1024]{2,1,0:T(8,128)(2,1)S(1)}, f16[2,64,1024]{2,1,0:T(8,128)(2,1)S(1)}, u32[]{:S(2)}, u32[]{:S(2)}) %collective-permute-start.34) | collective-permute-done | bytes 262176 | tf_op jit(solution)/shard_map/ppermute | solution.py:156
  174.1 1.1 bitcast_dynamic-update-slice_fusion.7
  175.2 1.4 collective-permute-start.35
  177.0 0.8 collective-permute-done.35
  177.8 1.8 %copy-done.19 = bf16[2,2,448,1024]{3,2,1,0:T(8,128)(2,1)} copy-done((bf16[2,2,448,1024]{3,2,1,0:T(8,128)(2,1)}, bf16[2,2,448,1024]{3,2,1,0:T(8,128)(2,1)S(1)}, u32[]{:S(2)}) %copy-start.19) | copy-done | bytes 3670040
  (91 shorter events, 5.1 us)
Async XLA Ops:
  0.0 13.4 %collective-permute-start.1 = (bf16[256,1024]{1,0:T(8,128)(2,1)}, bf16[256,1024]{1,0:T(8,128)(2,1)S(1)}, u32[]{:S(2)}, u32[]{:S(2)}) collective-permute-start(bf16[256,1024]{1,0:T(8,128)(2,1)} %bitcast.34), channel_id=1, source_target_pairs={{0,1},{1,0},{2,3},{3,2},{4,5},{5,4},{6,7},{7,6},{8,9},{9,8},{10,11... | collective-permute-start | bytes 1572872 | tf_op jit(solution)/shard_map/ppermute | solution.py:156
  2.0 17.4 %collective-permute-start.2 = (bf16[256,1024]{1,0:T(8,128)(2,1)}, bf16[256,1024]{1,0:T(8,128)(2,1)S(1)}, u32[]{:S(2)}, u32[]{:S(2)}) collective-permute-start(bf16[256,1024]{1,0:T(8,128)(2,1)} %bitcast.35), channel_id=1, source_target_pairs={{0,2},{1,3},{2,4},{3,5},{4,6},{5,7},{6,0},{7,1},{8,10},{9,11},{10,... | collective-permute-start | bytes 1572872 | tf_op jit(solution)/shard_map/ppermute | solution.py:147
  3.3 1.5 copy-start.1
  4.8 1.5 copy-start.2
  6.3 12.7 %copy-start = (bf16[1,256,1024]{2,1,0:T(8,128)(2,1)S(1)}, bf16[1,256,1024]{2,1,0:T(8,128)(2,1)}, u32[]{:S(2)}) copy-start(bf16[1,256,1024]{2,1,0:T(8,128)(2,1)} %param.10) | copy-start | bytes 1572868
  8.9 0.8 copy-start.10
  9.7 29.5 %copy-start.7 = (bf16[512,512]{1,0:T(8,128)(2,1)}, bf16[512,512]{1,0:T(8,128)(2,1)S(1)}, u32[]{:S(2)}) copy-start(bf16[512,512]{1,0:T(8,128)(2,1)S(1)} %get-tuple-element.23.refs_8_) | copy-start | bytes 1572868
  9.7 13.7 %collective-permute-start.9 = (bf16[512,512]{1,0:T(8,128)(2,1)S(1)}, bf16[512,512]{1,0:T(8,128)(2,1)S(1)}, u32[]{:S(2)}, u32[]{:S(2)}) collective-permute-start(bf16[512,512]{1,0:T(8,128)(2,1)S(1)} %get-tuple-element.17.refs_8_), channel_id=1, source_target_pairs={{0,24},{8,0},{16,8},{24,16},{1,25},{9,1},{17,9},{25,17},{2,26},{10... | collective-permute-start | bytes 1572872 | tf_op jit(solution)/shard_map/ppermute | solution.py:147
  13.4 12.8 %collective-permute-start.5 = (bf16[256,1024]{1,0:T(8,128)(2,1)S(1)}, bf16[256,1024]{1,0:T(8,128)(2,1)S(1)}, u32[]{:S(2)}, u32[]{:S(2)}) collective-permute-start(bf16[256,1024]{1,0:T(8,128)(2,1)S(1)} %collective-permute-done.1.refs_1_), channel_id=1, source_target_pairs={{0,6},{1,7},{2,0},{3,1},{4,2},{5,3},{6,4},{7,5},{8,14},{9,15},{10,... | collective-permute-start | bytes 1572872 | tf_op jit(solution)/shard_map/ppermute | solution.py:147
  16.6 14.2 %collective-permute-start.8 = (bf16[512,512]{1,0:T(8,128)(2,1)S(1)}, bf16[512,512]{1,0:T(8,128)(2,1)S(1)}, u32[]{:S(2)}, u32[]{:S(2)}) collective-permute-start(bf16[512,512]{1,0:T(8,128)(2,1)S(1)} %get-tuple-element.17.refs_8_), channel_id=1, source_target_pairs={{0,8},{8,16},{16,24},{24,0},{1,9},{9,17},{17,25},{25,1},{2,10},{10... | collective-permute-start | bytes 1572872 | tf_op jit(solution)/shard_map/ppermute | solution.py:147
  18.2 0.8 copy-start.12
  19.0 18.5 %collective-permute-start.4 = (bf16[256,1024]{1,0:T(8,128)(2,1)S(1)}, bf16[256,1024]{1,0:T(8,128)(2,1)S(1)}, u32[]{:S(2)}, u32[]{:S(2)}) collective-permute-start(bf16[256,1024]{1,0:T(8,128)(2,1)S(1)} %bitcast.36), channel_id=1, source_target_pairs={{0,6},{1,7},{2,0},{3,1},{4,2},{5,3},{6,4},{7,5},{8,14},{9,15},{10,... | collective-permute-start | bytes 1572872 | tf_op jit(solution)/shard_map/ppermute | solution.py:147
  19.5 26.1 %collective-permute-start.3 = (bf16[256,1024]{1,0:T(8,128)(2,1)S(1)}, bf16[256,1024]{1,0:T(8,128)(2,1)S(1)}, u32[]{:S(2)}, u32[]{:S(2)}) collective-permute-start(bf16[256,1024]{1,0:T(8,128)(2,1)S(1)} %collective-permute-done.1.refs_1_), channel_id=1, source_target_pairs={{0,2},{1,3},{2,4},{3,5},{4,6},{5,7},{6,0},{7,1},{8,10},{9,11},{10,... | collective-permute-start | bytes 1572872 | tf_op jit(solution)/shard_map/ppermute | solution.py:147
  23.4 15.7 %copy-start.20 = (bf16[512,512]{1,0:T(8,128)(2,1)}, bf16[512,512]{1,0:T(8,128)(2,1)S(1)}, u32[]{:S(2)}) copy-start(bf16[512,512]{1,0:T(8,128)(2,1)S(1)} %collective-permute-done.9.refs_10_) | copy-start | bytes 1572868
  23.4 22.2 %collective-permute-start.6 = (bf16[256,1024]{1,0:T(8,128)(2,1)S(1)}, bf16[256,1024]{1,0:T(8,128)(2,1)}, u32[]{:S(2)}, u32[]{:S(2)}) collective-permute-start(bf16[256,1024]{1,0:T(8,128)(2,1)S(1)} %collective-permute-done.2.refs_2_), channel_id=1, source_target_pairs={{0,2},{1,3},{2,4},{3,5},{4,6},{5,7},{6,0},{7,1},{8,10},{9,11},{10,... | collective-permute-start | bytes 1572872 | tf_op jit(solution)/shard_map/ppermute | solution.py:147
  26.2 22.5 %collective-permute-start.7 = (bf16[256,1024]{1,0:T(8,128)(2,1)S(1)}, bf16[256,1024]{1,0:T(8,128)(2,1)}, u32[]{:S(2)}, u32[]{:S(2)}) collective-permute-start(bf16[256,1024]{1,0:T(8,128)(2,1)S(1)} %collective-permute-done.5.refs_5_), channel_id=1, source_target_pairs={{0,6},{1,7},{2,0},{3,1},{4,2},{5,3},{6,4},{7,5},{8,14},{9,15},{10,... | collective-permute-start | bytes 1572872 | tf_op jit(solution)/shard_map/ppermute | solution.py:147
  30.7 6.7 %copy-start.3 = (bf16[512,512]{1,0:T(8,128)(2,1)}, bf16[512,512]{1,0:T(8,128)(2,1)S(1)}, u32[]{:S(2)}) copy-start(bf16[512,512]{1,0:T(8,128)(2,1)S(1)} %collective-permute-done.8.refs_9_) | copy-start | bytes 1572868
  30.7 8.5 %collective-permute-start.11 = (bf16[256,512]{1,0:T(8,128)(2,1)}, bf16[256,512]{1,0:T(8,128)(2,1)S(1)}, u32[]{:S(2)}, u32[]{:S(2)}) collective-permute-start(bf16[256,512]{1,0:T(8,128)(2,1)} %slice.50), channel_id=1, source_target_pairs={{0,24},{8,0},{16,8},{24,16},{1,25},{9,1},{17,9},{25,17},{2,26},{10... | collective-permute-start | bytes 786440 | tf_op jit(solution)/shard_map/ppermute | solution.py:147
  37.5 8.1 %collective-permute-start.10 = (bf16[256,512]{1,0:T(8,128)(2,1)}, bf16[256,512]{1,0:T(8,128)(2,1)}, u32[]{:S(2)}, u32[]{:S(2)}) collective-permute-start(bf16[256,512]{1,0:T(8,128)(2,1)} %slice.49), channel_id=1, source_target_pairs={{0,8},{8,16},{16,24},{24,0},{1,9},{9,17},{17,25},{25,1},{2,10},{10... | collective-permute-start | bytes 786440 | tf_op jit(solution)/shard_map/ppermute | solution.py:147
  39.2 27.2 %collective-permute-start.16 = (bf16[512,512]{1,0:T(8,128)(2,1)}, bf16[512,512]{1,0:T(8,128)(2,1)S(1)}, u32[]{:S(2)}, u32[]{:S(2)}) collective-permute-start(bf16[512,512]{1,0:T(8,128)(2,1)} %copy-done.10), channel_id=1, source_target_pairs={{0,24},{8,0},{16,8},{24,16},{1,25},{9,1},{17,9},{25,17},{2,26},{10... | collective-permute-start | bytes 1572872 | tf_op jit(solution)/shard_map/ppermute | solution.py:147
  45.6 23.6 %collective-permute-start.15 = (bf16[512,512]{1,0:T(8,128)(2,1)}, bf16[512,512]{1,0:T(8,128)(2,1)S(1)}, u32[]{:S(2)}, u32[]{:S(2)}) collective-permute-start(bf16[512,512]{1,0:T(8,128)(2,1)} %copy-done.10), channel_id=1, source_target_pairs={{0,8},{8,16},{16,24},{24,0},{1,9},{9,17},{17,25},{25,1},{2,10},{10... | collective-permute-start | bytes 1572872 | tf_op jit(solution)/shard_map/ppermute | solution.py:147
  48.7 1.0 copy-start.4
  49.8 1.0 copy-start.13
  50.8 12.7 %copy-start.8 = (bf16[512,512]{1,0:T(8,128)(2,1)S(1)}, bf16[512,512]{1,0:T(8,128)(2,1)}, u32[]{:S(2)}) copy-start(bf16[512,512]{1,0:T(8,128)(2,1)} %copy-done.7) | copy-start | bytes 1572868
  50.8 18.5 %copy-start.16 = (f32[1,1,448,1024]{3,2,1,0:T(8,128)S(1)}, f32[1,1,448,1024]{3,2,1,0:T(8,128)}, u32[]{:S(2)}) copy-start(f32[1,1,448,1024]{3,2,1,0:T(8,128)} %param.15) | copy-start | bytes 5505028
  50.8 18.5 %copy-start.17 = (f32[1,1,448,1024]{3,2,1,0:T(8,128)S(1)}, f32[1,1,448,1024]{3,2,1,0:T(8,128)}, u32[]{:S(2)}) copy-start(f32[1,1,448,1024]{3,2,1,0:T(8,128)} %param.14) | copy-start | bytes 5505028
  60.1 37.0 %collective-permute-start.12 = (f32[2,128,1024]{2,1,0:T(8,128)}, f32[2,128,1024]{2,1,0:T(8,128)S(1)}, u32[]{:S(2)}, u32[]{:S(2)}) collective-permute-start(f32[2,128,1024]{2,1,0:T(8,128)} %get-tuple-element.19), channel_id=1, source_target_pairs={{0,32},{32,0},{64,96},{96,64},{1,33},{33,1},{65,97},{97,65},{2,34}... | collective-permute-start | bytes 3145736 | tf_op jit(solution)/shard_map/ppermute | solution.py:156
  63.5 14.4 %collective-permute-start.23 = (bf16[512,512]{1,0:T(8,128)(2,1)S(1)}, bf16[512,512]{1,0:T(8,128)(2,1)S(1)}, u32[]{:S(2)}, u32[]{:S(2)}) collective-permute-start(bf16[512,512]{1,0:T(8,128)(2,1)S(1)} %copy-done.8), channel_id=1, source_target_pairs={{0,24},{8,0},{16,8},{24,16},{1,25},{9,1},{17,9},{25,17},{2,26},{10... | collective-permute-start | bytes 1572872 | tf_op jit(solution)/shard_map/ppermute | solution.py:147
  66.4 15.0 %collective-permute-start.22 = (bf16[512,512]{1,0:T(8,128)(2,1)S(1)}, bf16[512,512]{1,0:T(8,128)(2,1)S(1)}, u32[]{:S(2)}, u32[]{:S(2)}) collective-permute-start(bf16[512,512]{1,0:T(8,128)(2,1)S(1)} %copy-done.8), channel_id=1, source_target_pairs={{0,8},{8,16},{16,24},{24,0},{1,9},{9,17},{17,25},{25,1},{2,10},{10... | collective-permute-start | bytes 1572872 | tf_op jit(solution)/shard_map/ppermute | solution.py:147
  66.4 4.3 %copy-start.22 = (bf16[512,512]{1,0:T(8,128)(2,1)}, bf16[512,512]{1,0:T(8,128)(2,1)S(1)}, u32[]{:S(2)}) copy-start(bf16[512,512]{1,0:T(8,128)(2,1)S(1)} %collective-permute-done.16.refs_10_) | copy-start | bytes 1572868
  66.4 19.6 %collective-permute-start.18 = (bf16[256,512]{1,0:T(8,128)(2,1)S(1)}, bf16[256,512]{1,0:T(8,128)(2,1)S(1)}, u32[]{:S(2)}, u32[]{:S(2)}) collective-permute-start(bf16[256,512]{1,0:T(8,128)(2,1)S(1)} %slice.53), channel_id=1, source_target_pairs={{0,24},{8,0},{16,8},{24,16},{1,25},{9,1},{17,9},{25,17},{2,26},{10... | collective-permute-start | bytes 786440 | tf_op jit(solution)/shard_map/ppermute | solution.py:147
  69.2 17.3 %copy-start.11 = (bf16[512,512]{1,0:T(8,128)(2,1)S(1)}, bf16[512,512]{1,0:T(8,128)(2,1)}, u32[]{:S(2)}) copy-start(bf16[512,512]{1,0:T(8,128)(2,1)} %copy-done.10) | copy-start | bytes 1572868
  69.2 17.3 %collective-permute-start.17 = (bf16[256,512]{1,0:T(8,128)(2,1)S(1)}, bf16[256,512]{1,0:T(8,128)(2,1)S(1)}, u32[]{:S(2)}, u32[]{:S(2)}) collective-permute-start(bf16[256,512]{1,0:T(8,128)(2,1)S(1)} %slice.52), channel_id=1, source_target_pairs={{0,8},{8,16},{16,24},{24,0},{1,9},{9,17},{17,25},{25,1},{2,10},{10... | collective-permute-start | bytes 786440 | tf_op jit(solution)/shard_map/ppermute | solution.py:147
  77.9 17.6 %copy-start.21 = (bf16[512,512]{1,0:T(8,128)(2,1)}, bf16[512,512]{1,0:T(8,128)(2,1)S(1)}, u32[]{:S(2)}) copy-start(bf16[512,512]{1,0:T(8,128)(2,1)S(1)} %collective-permute-done.23.refs_10_) | copy-start | bytes 1572868
  77.9 23.9 %collective-permute-start = (f16[448,1024]{1,0:T(8,128)(2,1)}, f16[448,1024]{1,0:T(8,128)(2,1)}, u32[]{:S(2)}, u32[]{:S(2)}) collective-permute-start(f16[448,1024]{1,0:T(8,128)(2,1)} %fusion.1), channel_id=1, source_target_pairs={{0,64},{32,96},{64,0},{96,32},{1,65},{33,97},{65,1},{97,33},{2,66}... | collective-permute-start | bytes 2752520 | tf_op jit(solution)/shard_map/ppermute | solution.py:156
  81.4 23.5 %collective-permute-start.25 = (bf16[256,512]{1,0:T(8,128)(2,1)}, bf16[256,512]{1,0:T(8,128)(2,1)S(1)}, u32[]{:S(2)}, u32[]{:S(2)}) collective-permute-start(bf16[256,512]{1,0:T(8,128)(2,1)} %slice.56), channel_id=1, source_target_pairs={{0,24},{8,0},{16,8},{24,16},{1,25},{9,1},{17,9},{25,17},{2,26},{10... | collective-permute-start | bytes 786440 | tf_op jit(solution)/shard_map/ppermute | solution.py:147
  85.3 0.8 copy-start.5
  86.1 11.0 %copy-start.25 = (f32[2,128,1024]{2,1,0:T(8,128)S(1)}, f32[2,128,1024]{2,1,0:T(8,128)}, u32[]{:S(2)}) copy-start(f32[2,128,1024]{2,1,0:T(8,128)} %get-tuple-element.18) | copy-start | bytes 3145732
  86.1 18.8 %collective-permute-start.24 = (bf16[256,512]{1,0:T(8,128)(2,1)}, bf16[256,512]{1,0:T(8,128)(2,1)}, u32[]{:S(2)}, u32[]{:S(2)}) collective-permute-start(bf16[256,512]{1,0:T(8,128)(2,1)} %slice.55), channel_id=1, source_target_pairs={{0,8},{8,16},{16,24},{24,0},{1,9},{9,17},{17,25},{25,1},{2,10},{10... | collective-permute-start | bytes 786440 | tf_op jit(solution)/shard_map/ppermute | solution.py:147
  95.5 22.2 %collective-permute-start.19 = (f32[2,128,1024]{2,1,0:T(8,128)}, f32[2,128,1024]{2,1,0:T(8,128)}, u32[]{:S(2)}, u32[]{:S(2)}) collective-permute-start(f32[2,128,1024]{2,1,0:T(8,128)} %get-tuple-element.22), channel_id=1, source_target_pairs={{0,32},{32,0},{64,96},{96,64},{1,33},{33,1},{65,97},{97,65},{2,34}... | collective-permute-start | bytes 3145736 | tf_op jit(solution)/shard_map/ppermute | solution.py:156
  98.1 16.7 %collective-permute-start.13 = (f16[2,128,1024]{2,1,0:T(8,128)(2,1)}, f16[2,128,1024]{2,1,0:T(8,128)(2,1)}, u32[]{:S(2)}, u32[]{:S(2)}) collective-permute-start(f16[2,128,1024]{2,1,0:T(8,128)(2,1)} %add_convert_fusion.5), channel_id=1, source_target_pairs={{0,64},{32,96},{64,0},{96,32},{1,65},{33,97},{65,1},{97,33},{2,66}... | collective-permute-start | bytes 1572872 | tf_op jit(solution)/shard_map/ppermute | solution.py:156
  101.8 3.1 %copy-start.6 = (bf16[512,512]{1,0:T(8,128)(2,1)S(1)}, bf16[512,512]{1,0:T(8,128)(2,1)}, u32[]{:S(2)}) copy-start(bf16[512,512]{1,0:T(8,128)(2,1)} %copy-done.5) | copy-start | bytes 1572868
  101.8 3.1 %copy-start.9 = (bf16[512,512]{1,0:T(8,128)(2,1)S(1)}, bf16[512,512]{1,0:T(8,128)(2,1)}, u32[]{:S(2)}) copy-start(bf16[512,512]{1,0:T(8,128)(2,1)} %copy-done.7) | copy-start | bytes 1572868
  104.8 10.4 %copy-start.18 = (f16[2,448,1024]{2,1,0:T(8,128)(2,1)}, f16[2,448,1024]{2,1,0:T(8,128)(2,1)S(1)}, u32[]{:S(2)}) copy-start(f16[2,448,1024]{2,1,0:T(8,128)(2,1)S(1)} %maximum_select_fusion) | copy-start | bytes 5505028
  114.0 25.5 %collective-permute-start.26 = (f32[2,128,1024]{2,1,0:T(8,128)}, f32[2,128,1024]{2,1,0:T(8,128)}, u32[]{:S(2)}, u32[]{:S(2)}) collective-permute-start(f32[2,128,1024]{2,1,0:T(8,128)} %get-tuple-element.25), channel_id=1, source_target_pairs={{0,32},{32,0},{64,96},{96,64},{1,33},{33,1},{65,97},{97,65},{2,34}... | collective-permute-start | bytes 3145736 | tf_op jit(solution)/shard_map/ppermute | solution.py:156
  115.2 2.5 %copy-start.23 = (f32[2,128,1024]{2,1,0:T(8,128)S(1)}, f32[2,128,1024]{2,1,0:T(8,128)}, u32[]{:S(2)}) copy-start(f32[2,128,1024]{2,1,0:T(8,128)} %get-tuple-element.21) | copy-start | bytes 3145732
  117.7 5.8 %copy-start.14 = (bf16[2,2,448,1024]{3,2,0,1:T(8,128)(2,1)}, bf16[2,2,448,1024]{3,2,0,1:T(8,128)(2,1)S(1)}, u32[]{:S(2)}) copy-start(bf16[2,2,448,1024]{3,2,0,1:T(8,128)(2,1)S(1)} %get-tuple-element.35) | copy-start | bytes 11010052
  117.7 10.8 %collective-permute-start.14 = (bf16[2,128,1024]{2,1,0:T(8,128)(2,1)}, bf16[2,128,1024]{2,1,0:T(8,128)(2,1)}, u32[]{:S(2)}, u32[]{:S(2)}) collective-permute-start(bf16[2,128,1024]{2,1,0:T(8,128)(2,1)} %get-tuple-element.36), channel_id=1, source_target_pairs={{0,32},{32,0},{64,96},{96,64},{1,33},{33,1},{65,97},{97,65},{2,34}... | collective-permute-start | bytes 1572872 | tf_op jit(solution)/shard_map/ppermute | solution.py:156
  120.8 14.8 %collective-permute-start.20 = (f16[2,128,1024]{2,1,0:T(8,128)(2,1)}, f16[2,128,1024]{2,1,0:T(8,128)(2,1)}, u32[]{:S(2)}, u32[]{:S(2)}) collective-permute-start(f16[2,128,1024]{2,1,0:T(8,128)(2,1)} %add_convert_fusion.3), channel_id=1, source_target_pairs={{0,64},{32,96},{64,0},{96,32},{1,65},{33,97},{65,1},{97,33},{2,66}... | collective-permute-start | bytes 1572872 | tf_op jit(solution)/shard_map/ppermute | solution.py:156
  123.5 20.3 %collective-permute-start.30 = (bf16[256,512]{1,0:T(8,128)(2,1)}, bf16[256,512]{1,0:T(8,128)(2,1)S(1)}, u32[]{:S(2)}, u32[]{:S(2)}) collective-permute-start(bf16[256,512]{1,0:T(8,128)(2,1)} %get-tuple-element.26.refs_8_), channel_id=1, source_target_pairs={{0,24},{8,0},{16,8},{24,16},{1,25},{9,1},{17,9},{25,17},{2,26},{10... | collective-permute-start | bytes 786440 | tf_op jit(solution)/shard_map/ppermute | solution.py:147
  128.5 20.3 %collective-permute-start.29 = (bf16[256,512]{1,0:T(8,128)(2,1)}, bf16[256,512]{1,0:T(8,128)(2,1)}, u32[]{:S(2)}, u32[]{:S(2)}) collective-permute-start(bf16[256,512]{1,0:T(8,128)(2,1)} %get-tuple-element.26.refs_8_), channel_id=1, source_target_pairs={{0,8},{8,16},{16,24},{24,0},{1,9},{9,17},{17,25},{25,1},{2,10},{10... | collective-permute-start | bytes 786440 | tf_op jit(solution)/shard_map/ppermute | solution.py:147
  128.5 11.0 %copy-start.24 = (f32[2,128,1024]{2,1,0:T(8,128)S(1)}, f32[2,128,1024]{2,1,0:T(8,128)}, u32[]{:S(2)}) copy-start(f32[2,128,1024]{2,1,0:T(8,128)} %get-tuple-element.24) | copy-start | bytes 3145732
  138.1 25.3 %collective-permute-start.21 = (bf16[2,128,1024]{2,1,0:T(8,128)(2,1)S(1)}, bf16[2,128,1024]{2,1,0:T(8,128)(2,1)S(1)}, u32[]{:S(2)}, u32[]{:S(2)}) collective-permute-start(bf16[2,128,1024]{2,1,0:T(8,128)(2,1)S(1)} %get-tuple-element.34), channel_id=1, source_target_pairs={{0,32},{32,0},{64,96},{96,64},{1,33},{33,1},{65,97},{97,65},{2,34}... | collective-permute-start | bytes 1572872 | tf_op jit(solution)/shard_map/ppermute | solution.py:156
  140.9 22.5 %collective-permute-start.27 = (f16[2,128,1024]{2,1,0:T(8,128)(2,1)S(1)}, f16[2,128,1024]{2,1,0:T(8,128)(2,1)S(1)}, u32[]{:S(2)}, u32[]{:S(2)}) collective-permute-start(f16[2,128,1024]{2,1,0:T(8,128)(2,1)S(1)} %add_convert_fusion.1), channel_id=1, source_target_pairs={{0,64},{32,96},{64,0},{96,32},{1,65},{33,97},{65,1},{97,33},{2,66}... | collective-permute-start | bytes 1572872 | tf_op jit(solution)/shard_map/ppermute | solution.py:156
  143.8 7.7 %collective-permute-start.32 = (bf16[128,512]{1,0:T(8,128)(2,1)S(1)}, bf16[128,512]{1,0:T(8,128)(2,1)S(1)}, u32[]{:S(2)}, u32[]{:S(2)}) collective-permute-start(bf16[128,512]{1,0:T(8,128)(2,1)S(1)} %slice.59), channel_id=1, source_target_pairs={{0,24},{8,0},{16,8},{24,16},{1,25},{9,1},{17,9},{25,17},{2,26},{10... | collective-permute-start | bytes 393224 | tf_op jit(solution)/shard_map/ppermute | solution.py:147
  149.8 13.6 %copy-start.15 = (bf16[2,2,448,1024]{3,2,0,1:T(8,128)(2,1)S(1)}, bf16[2,2,448,1024]{3,2,0,1:T(8,128)(2,1)}, u32[]{:S(2)}) copy-start(bf16[2,2,448,1024]{3,2,0,1:T(8,128)(2,1)} %get-tuple-element.33) | copy-start | bytes 11010052
  149.8 5.8 %collective-permute-start.31 = (bf16[128,512]{1,0:T(8,128)(2,1)S(1)}, bf16[128,512]{1,0:T(8,128)(2,1)S(1)}, u32[]{:S(2)}, u32[]{:S(2)}) collective-permute-start(bf16[128,512]{1,0:T(8,128)(2,1)S(1)} %slice.58), channel_id=1, source_target_pairs={{0,8},{8,16},{16,24},{24,0},{1,9},{9,17},{17,25},{25,1},{2,10},{10... | collective-permute-start | bytes 393224 | tf_op jit(solution)/shard_map/ppermute | solution.py:147
  161.9 3.1 %collective-permute-start.33 = (f32[2,64,1024]{2,1,0:T(8,128)S(1)}, f32[2,64,1024]{2,1,0:T(8,128)S(1)}, u32[]{:S(2)}, u32[]{:S(2)}) collective-permute-start(f32[2,64,1024]{2,1,0:T(8,128)S(1)} %get-tuple-element.28), channel_id=1, source_target_pairs={{0,32},{32,0},{64,96},{96,64},{1,33},{33,1},{65,97},{97,65},{2,34}... | collective-permute-start | bytes 1572872 | tf_op jit(solution)/shard_map/ppermute | solution.py:156
  164.9 2.0 %collective-permute-start.28 = (bf16[2,128,1024]{2,1,0:T(8,128)(2,1)S(1)}, bf16[2,128,1024]{2,1,0:T(8,128)(2,1)S(1)}, u32[]{:S(2)}, u32[]{:S(2)}) collective-permute-start(bf16[2,128,1024]{2,1,0:T(8,128)(2,1)S(1)} %get-tuple-element.32), channel_id=1, source_target_pairs={{0,32},{32,0},{64,96},{96,64},{1,33},{33,1},{65,97},{97,65},{2,34}... | collective-permute-start | bytes 1572872 | tf_op jit(solution)/shard_map/ppermute | solution.py:156
  165.1 9.0 %collective-permute-start.34 = (f16[2,64,1024]{2,1,0:T(8,128)(2,1)S(1)}, f16[2,64,1024]{2,1,0:T(8,128)(2,1)S(1)}, u32[]{:S(2)}, u32[]{:S(2)}) collective-permute-start(f16[2,64,1024]{2,1,0:T(8,128)(2,1)S(1)} %add_convert_fusion.7), channel_id=1, source_target_pairs={{0,64},{32,96},{64,0},{96,32},{1,65},{33,97},{65,1},{97,33},{2,66}... | collective-permute-start | bytes 786440 | tf_op jit(solution)/shard_map/ppermute | solution.py:156
  175.2 2.6 %collective-permute-start.35 = (bf16[2,64,1024]{2,1,0:T(8,128)(2,1)S(1)}, bf16[2,64,1024]{2,1,0:T(8,128)(2,1)S(1)}, u32[]{:S(2)}, u32[]{:S(2)}) collective-permute-start(bf16[2,64,1024]{2,1,0:T(8,128)(2,1)S(1)} %get-tuple-element.30), channel_id=1, source_target_pairs={{0,32},{32,0},{64,96},{96,64},{1,33},{33,1},{65,97},{97,65},{2,34}... | collective-permute-start | bytes 786440 | tf_op jit(solution)/shard_map/ppermute | solution.py:156
  177.8 1.8 %copy-start.19 = (bf16[2,2,448,1024]{3,2,1,0:T(8,128)(2,1)}, bf16[2,2,448,1024]{3,2,1,0:T(8,128)(2,1)S(1)}, u32[]{:S(2)}) copy-start(bf16[2,2,448,1024]{3,2,1,0:T(8,128)(2,1)S(1)} %bitcast_dynamic-update-slice_fusion.6) | copy-start | bytes 11010052

commit v2 on v0

v2 whole, which is shorter than its diff:
```python
import functools

import jax
import jax.numpy as jnp
from jax import lax
from jax.experimental import pallas as pl
from jax.experimental.pallas import tpu as pltpu
from jax.sharding import PartitionSpec as P

decay_first = 0.9
decay_second = 0.95
inner_rate = 0.25
weight_decay = 0.1
epsilon = 1e-08
outer_rate = 0.7
nesterov = 0.9
gain = outer_rate * (1.0 + nesterov)

OWNERS, OWNED, TOKENS, WIDTH = 4, 448, 512, 1024
SIZES = (128, 128, 128, 64)
MIB = 1024 * 1024
COST_ACT, COST_PASS, COST_ASM, COST_INNER, COST_HOLD = (0, 0, 0, 0), {2: 0, 3: 8}, 30, 8, 16
VMEM, HBM = pltpu.VMEM, pltpu.HBM


def first_rows(k):
    begin = sum(SIZES[:k])
    return begin, (begin + 64 if k < len(SIZES) - 1 else 0)


def place_in_mesh():
    t, r = lax.axis_index("tensor"), lax.axis_index("region")
    return lax.axis_index("fsdp"), t // 2, lax.rem(t, 2), lax.rem(r, 2), r // 2


def put(x, space):
    return pltpu.with_memory_space_constraint(x, space)


def call(kernel, out, args, spaces, scratch, limit, name, after=(), aliases={}, cost=0):
    spaces = list(spaces) + [VMEM] * len(after)
    args = [put(a, s) for a, s in zip(list(args) + list(after), spaces)]
    skip = len(after)
    count = len(args) - skip

    def body(*refs):
        kernel(*refs[:count], *refs[count + skip :])

    leaves = out if isinstance(out, list) else [out]
    specs = [pl.BlockSpec(memory_space=o.memory_space) for o in leaves]
    return pl.pallas_call(
        body,
        in_specs=[pl.BlockSpec(memory_space=s) for s in spaces],
        out_specs=specs if isinstance(out, list) else specs[0],
        out_shape=out,
        scratch_shapes=scratch,
        input_output_aliases=aliases,
        compiler_params=pltpu.CompilerParams(vmem_limit_bytes=limit),
        cost_estimate=pl.CostEstimate(flops=1000 + int(cost * 1e9), bytes_accessed=1000, transcendentals=0),
        name=name,
    )(*args)


def activate(gate, up, k, passed=None, after=()):
    low, high = first_rows(k)
    if SIZES[k] == 128:
        lanes = [o * OWNED + (low, high)[o % 2] for o in range(OWNERS)]
    else:
        lanes = [h * 2 * OWNED + low for h in range(2)]
    count = len(lanes)
    rows = 128 * count
    half = OWNERS * SIZES[k - 2] // 2 if passed else 0

    def kernel(gate_ref, up_ref, *refs):
        outs, (gates, ups, sems) = refs[-5 if passed else -4 : -3], refs[-3:]
        copies = []
        for g, lane in enumerate(lanes):
            for s, (src, dst) in enumerate(((gate_ref, gates), (up_ref, ups))):
                copies.append(pltpu.make_async_copy(src.at[:, lane : lane + 128], dst.at[g], sems.at[g, s]))
        for copy in copies:
            copy.start()
        if passed:
            before, after = refs[:2]
            outs[0][rows:, :] = before[:half, :]
            outs[1][rows:, :] = after[half : 2 * half, :]
        for g in range(count):
            copies[2 * g].wait()
            copies[2 * g + 1].wait()
            gate = gates[g].astype(jnp.float32)
            hidden = (gate / (1.0 + jnp.exp(-gate)) * ups[g].astype(jnp.float32)).astype(jnp.bfloat16)
            turned = hidden.T
            for out in outs:
                out[128 * g : 128 * (g + 1), :] = turned

    block = VMEM((count, TOKENS, 128), jnp.bfloat16)
    out = VMEM((rows + half, TOKENS), jnp.bfloat16)
    return call(
        kernel,
        [out, out] if passed else out,
        [gate, up, *(passed or ())],
        [HBM, HBM] + [VMEM] * (2 if passed else 0),
        [block, block, pltpu.SemaphoreType.DMA((count, 2))],
        12 * MIB,
        f"activate{k}",
        after,
        cost=COST_ACT[k],
    )


def pass_on(passed, k):
    half = OWNERS * SIZES[k] // 2

    def kernel(before, after, up, down):
        up[...] = before[:half, :]
        down[...] = after[half : 2 * half, :]

    out = VMEM((half, TOKENS), jnp.bfloat16)
    return call(kernel, [out, out], passed, [VMEM] * 2, [], 4 * MIB, f"pass_on{k}", cost=COST_PASS[k])


def assemble(pieces):
    hops = (0, 0, 3, 3, 1, 1, 2, 2)

    def kernel(*refs):
        _, y, x_lo, _, _ = place_in_mesh()
        out_ref = refs[8]
        for i in range(8):
            part = x_lo if i % 2 == 0 else 1 - x_lo
            row = pl.multiple_of(lax.rem(y + hops[i], 4) * 512 + part * 256, 256)
            out_ref[pl.ds(row, 256), :] = refs[i][...]

    return call(
        kernel,
        VMEM((2048, WIDTH), jnp.bfloat16),
        pieces,
        [VMEM] * 8,
        [],
        8 * MIB,
        "assemble",
        cost=COST_ASM,
    )


def inner_step(grads, hidden, state, k, after=(), width=512):
    rows = SIZES[k]
    begins = first_rows(k)
    tiles = WIDTH // width
    scale = gain / 4
    step = scale * inner_rate

    def kernel(grads_ref, own, before, after, far_a, far_b, w, m, v, anchor, momentum, keep, send, *scratch):
        ws, ms, vs, anchors, momenta, sems = scratch
        z, _, _, core, half = place_in_mesh()
        mine = pl.multiple_of(begins[0] + core * (begins[1] - begins[0]), 16)
        copies = []
        for t in range(tiles):
            cols = pl.ds(t * width, width)
            group = []
            for s, (src, dst) in enumerate(((w, ws), (m, ms), (v, vs))):
                for o in range(OWNERS):
                    at = pl.ds(o * OWNED + begins[o % 2], rows)
                    group.append(pltpu.make_async_copy(src.at[at, cols], dst.at[t, o], sems.at[t, 4 * s + o]))
            for s, (src, dst) in enumerate(((anchor, anchors), (momentum, momenta))):
                group.append(pltpu.make_async_copy(src.at[pl.ds(mine, rows), cols], dst.at[t], sems.at[t, 12 + s]))
            copies.append(group)
        for group in copies:
            for copy in group:
                copy.start()

        count = OWNERS * rows

        def dot(a, hop, t, start=0, size=count):
            row = pl.multiple_of(lax.rem(z + hop, 4) * 512, 512)
            b = grads_ref[pl.ds(row, 512), t * width : (t + 1) * width]
            return jnp.dot(a[start : start + size, :], b, preferred_element_type=jnp.float32)

        for t in range(tiles):
            cols = slice(t * width, (t + 1) * width)
            total = dot(own, 0, t) + dot(before, 3, t) + dot(after, 1, t)
            fars = [dot(far, 2, t, far.shape[0] - count // 2, count // 2) for far in (far_a, far_b)]
            total = total + jnp.concatenate(fars, axis=0)
            total = total.reshape(OWNERS, rows, width)
            for copy in copies[t]:
                copy.wait()
            first_new = (step * decay_first) * ms[t].astype(jnp.float32) + (
                step * (1.0 - decay_first) / 2048
            ) * total
            second_new = decay_second * vs[t] + ((1.0 - decay_second) / 2048**2) * (total * total)
            root = second_new * lax.rsqrt(second_new)
            master = ws[t].astype(jnp.float32)
            inner = (scale * (1.0 - inner_rate * weight_decay)) * master - first_new / (root + epsilon)
            rest = (1.0 - gain) * anchors[t] - (outer_rate * nesterov * nesterov) * momenta[t]
            for o in range(OWNERS):

                @pl.when(core == o % 2)
                def _(o=o):
                    keep[o // 2, :, cols] = inner[o]

                @pl.when(core != o % 2)
                def _(o=o):
                    send[o // 2, :, cols] = inner[o]

            keep[half, :, cols] = keep[half, :, cols] + rest

    shape = VMEM((2, rows, WIDTH), jnp.float32)
    state_block = lambda dtype: VMEM((tiles, OWNERS, rows, width), dtype)
    owner_block = VMEM((tiles, rows, width), jnp.float32)
    return call(
        kernel,
        [shape, shape],
        [grads, *hidden, *state],
        [VMEM] * 6 + [HBM] * 5,
        [state_block(jnp.bfloat16), state_block(jnp.bfloat16), state_block(jnp.float32), owner_block, owner_block]
        + [pltpu.SemaphoreType.DMA((tiles, 14))],
        20 * MIB,
        f"inner{k}",
        after,
        cost=COST_INNER,
    )


def hold(arrays, k):
    def kernel(*refs):
        refs[-1][...] = jnp.zeros((8, 128), jnp.float32)

    return call(kernel, VMEM((8, 128), jnp.float32), arrays, [VMEM] * len(arrays), [], 4 * MIB, f"hold{k}", cost=COST_HOLD)


def place(mine, theirs, out, k):
    rows = SIZES[k]
    begins = first_rows(k)

    def kernel(mine_ref, theirs_ref, *refs):
        out_ref, sems = refs[-2:]
        core = place_in_mesh()[3]
        copies = []
        for i, src in enumerate((mine_ref, theirs_ref)):
            c = core if i == 0 else 1 - core
            row = pl.multiple_of(begins[0] + c * (begins[1] - begins[0]), 16)
            for h in range(2):
                copies.append(
                    pltpu.make_async_copy(src.at[h], out_ref.at[2 * h + c, pl.ds(row, rows), :], sems.at[i, h])
                )
        for copy in copies:
            copy.start()
        for copy in copies:
            copy.wait()

    before = [] if out is None else [out]
    return call(
        kernel,
        HBM((OWNERS, OWNED, WIDTH), jnp.bfloat16),
        [mine, theirs] + before,
        [VMEM, VMEM] + [HBM] * len(before),
        [pltpu.SemaphoreType.DMA((2, 2))],
        4 * MIB,
        f"place{k}",
        aliases={2: 0} if before else {},
    )


def shift(x, axis, n, step):
    return lax.ppermute(x, axis, [(i, (i + step) % n) for i in range(n)])


def local(gate_pre, up_pre, out_grad, weights, first_moment, second_moment, anchor, momentum):
    along_z = functools.partial(shift, axis="fsdp", n=4)
    along_y = lambda x, step: shift(x, "tensor", 8, 2 * step)
    swap = lambda x, axis, n, bit: lax.ppermute(x, axis, [(i, i ^ bit) for i in range(n)])
    other_core = lambda x: swap(x, "region", 4, 1)
    other_chip = lambda x: swap(x, "region", 4, 2)

    mine = out_grad[0]
    with jax.named_scope("pair"):
        pair = swap(mine, "tensor", 8, 1)
    with jax.named_scope("mine"):
        mine_up, mine_down = along_y(mine, 1), along_y(mine, -1)
    with jax.named_scope("paired"):
        pair_up, pair_down = along_y(pair, 1), along_y(pair, -1)
    with jax.named_scope("far"):
        mine_far, pair_far = along_y(mine_up, 1), along_y(pair_down, -1)
    grads = assemble([mine, pair, mine_up, pair_up, mine_down, pair_down, mine_far, pair_far])

    chunks = len(SIZES)
    owns, ring = [], []
    for k in range(chunks + 2):
        if k < 2:
            up = down = activate(gate_pre[0], up_pre[0], k)
        elif k < chunks:
            after = [owns[1], pair] if k == 2 else [mine_up, mine_down]
            up, down = activate(gate_pre[0], up_pre[0], k, ring[k - 2], after)
        else:
            up, down = pass_on(ring[k - 2], k - 2)
        owns.append(up)
        with jax.named_scope(f"ring{k}"):
            ring.append((along_z(up, step=1), along_z(down, step=-1)))
    gathered = [(owns[k], *ring[k], *ring[k + 2]) for k in range(chunks)]

    state = (weights[0], first_moment[0], second_moment[0], anchor[0, 0], momentum[0, 0])
    out, sums, results = None, [], []
    for k, hidden in enumerate(gathered):
        if k == 0:
            after = [owns[3], owns[4]]
        elif k == 1:
            after = [owns[5], sums[0]]
        else:
            after = [hold([*ring[k + 2], results[k - 2]], k), sums[k - 1]]
        keep, send = inner_step(grads, hidden, state, k, after)
        with jax.named_scope(f"cores{k}"):
            arrived = other_core(send)
        with jax.named_scope(f"sum{k}"):
            both = (keep + arrived).astype(jnp.float16)
            sums.append(both[0, :8, :128].astype(jnp.float32))
        with jax.named_scope(f"chips{k}"):
            both_there = other_chip(both)
        with jax.named_scope(f"fresh{k}"):
            results.append((both.astype(jnp.float32) + both_there.astype(jnp.float32)).astype(jnp.bfloat16))
    for k, fresh in enumerate(results):
        with jax.named_scope(f"share{k}"):
            shared = other_core(fresh)
        out = place(fresh, shared, out, k)
    return out.reshape(OWNERS * OWNED, WIDTH)


def solution(mesh):
    placed = (
        P("region", "fsdp", "tensor"),
        P("region", "fsdp", "tensor"),
        P("region", "tensor", "fsdp"),
        P("region", "tensor", "fsdp"),
        P("region", "tensor", "fsdp"),
        P("region", "tensor", "fsdp"),
        P("tensor", "region", None, "fsdp"),
        P("tensor", "region", None, "fsdp"),
    )
    return jax.shard_map(
        local, mesh=mesh, in_specs=placed, out_specs=P("tensor", "fsdp"), check_vma=False
    )
```

time: 324 us -> 135 us (0.42)
  waiting for transfers between devices: 277 us -> 49.1 us
  starting transfers between devices: 0.12 us -> 49.5 us
  Pallas kernels: 0 us -> 33.8 us
  matrix products: 21.4 us -> 0 us
  between operations: 13.1 us -> 0.46 us
  other arithmetic: 8.06 us -> 1.43 us
  local copies, waits for them, and re-layouts: 4.25 us -> 0.01 us
    all_gather x3 -> x0, waiting for transfers between devices: 203 us -> none  [the longest x1 91 us: local(): incoming = lax.all_gather(out_grad[0], 'tensor', axis=0, tiled=True)]
    reduce_scatter x1 -> x0, waiting for transfers between devices: 73.1 us -> none  [local(): owned = lax.psum_scatter(inner, 'region', scatter_dimension=0, tiled=True)]
    ppermute x0 -> x31, starting transfers between devices: none -> 49.5 us  [the longest x18 27.3 us: shift(): return lax.ppermute(x, axis, [(i, (i + step) % n) for i in range(n)])]
    ppermute x0 -> x31, waiting for transfers between devices: none -> 49.1 us  [the longest x13 27.5 us: local(): lax.ppermute(x, axis, [(i, i ^ bit) for i in range(n)])]
    pallas_call x0 -> x17, Pallas kernels: none -> 33.8 us  [call(): pl.pallas_call(body, in_specs=[pl.BlockSpec(memory_space=s) for s in spac...]
    dot_general x1 -> x0, matrix products: 21.4 us -> none  [local(): lax.dot_general(lax.all_gather(hidden, 'fsdp', axis=0, tiled=True), incom...]
    convert_element_type x2 -> x11, other arithmetic: 8.06 us -> 1.43 us  [the longest x4 0.74 us: local(): both = (keep + arrived).astype(jnp.float16)]
    unnamed x3 -> x2, local copies, waits for them, and re-layouts: 4.25 us -> 0.01 us
  transfers between devices with their start and end apart: 4 -> 31, of which waited for: 4 -> 10; matrix products, arithmetic and copies ran while one was open for 1% -> 1% of each run, Pallas kernels for 0% -> 22%
where the time goes in v2:
time: 135 us; the launch traced here: 134 us
  starting transfers between devices  49.5 us (37%)
  waiting for transfers between devices  49.1 us (36%)
  Pallas kernels  33.8 us (25%)
  other arithmetic  1.43 us (1%)
    pallas_call x17, Pallas kernels, call(): pl.pallas_call(body, in_specs=[pl.BlockSpec(memory_space=s) for s in spac...  33.8 us
    ppermute x13, waiting for transfers between devices, local(): lax.ppermute(x, axis, [(i, i ^ bit) for i in range(n)])  27.5 us
    ppermute x18, starting transfers between devices, shift(): return lax.ppermute(x, axis, [(i, (i + step) % n) for i in range(n)])  27.3 us
    ppermute x13, starting transfers between devices, local(): lax.ppermute(x, axis, [(i, i ^ bit) for i in range(n)])  22.2 us
    ppermute x18, waiting for transfers between devices, shift(): return lax.ppermute(x, axis, [(i, (i + step) % n) for i in range(n)])  21.6 us
  transfers between devices with their start and end apart: 31, of which 10 were waited for; matrix products, arithmetic and copies ran while one was open for 1% of the time, Pallas kernels for 22%

profile of v2, /device:TPU:1, one launch (start us, length us, event | category | flops | bytes accessed | tf_op | source)
XLA Modules:
  0.0 134.3 jit_solution(14636283164928786307)
XLA Ops:
  0.0 2.0 %collective-permute-start = (bf16[256,1024]{1,0:T(8,128)(2,1)}, bf16[256,1024]{1,0:T(8,128)(2,1)S(1)}, u32[]{:S(2)}, u32[]{:S(2)}) collective-permute-start(bf16[256,1024]{1,0:T(8,128)(2,1)} %bitcast.24), channel_id=1, source_target_pairs={{0,1},{1,0},{2,3},{3,2},{4,5},{5,4},{6,7},{7,6},{8,9},{9,8},{10,11... | collective-permute-start | bytes 1572872 | tf_op jit(solution)/shard_map/pair/ppermute | solution.py:269
  2.0 1.6 %activate0.1.refs_1_ = bf16[512,512]{1,0:T(8,128)(2,1)S(1)} custom-call(bf16[512,1792]{1,0:T(8,128)(2,1)} %bitcast.28, bf16[512,1792]{1,0:T(8,128)(2,1)} %bitcast.32), custom_call_target="tpu_custom_call" | custom-call | flops 1000 | bytes 1000 | tf_op jit(solution)/shard_map/activate0/pallas_call | solution.py:51
  3.7 1.7 %collective-permute-start.13 = (bf16[512,512]{1,0:T(8,128)(2,1)S(1)}, bf16[512,512]{1,0:T(8,128)(2,1)S(1)}, u32[]{:S(2)}, u32[]{:S(2)}) collective-permute-start(bf16[512,512]{1,0:T(8,128)(2,1)S(1)} %activate0.1.refs_1_), channel_id=1, source_target_pairs={{0,8},{8,16},{16,24},{24,0},{1,9},{9,17},{17,25},{25,1},{2,10},{10... | collective-permute-start | bytes 1572872 | tf_op jit(solution)/shard_map/ring0/ppermute | solution.py:263
  5.4 2.2 %collective-permute-start.14 = (bf16[512,512]{1,0:T(8,128)(2,1)S(1)}, bf16[512,512]{1,0:T(8,128)(2,1)S(1)}, u32[]{:S(2)}, u32[]{:S(2)}) collective-permute-start(bf16[512,512]{1,0:T(8,128)(2,1)S(1)} %activate0.1.refs_1_), channel_id=1, source_target_pairs={{0,24},{8,0},{16,8},{24,16},{1,25},{9,1},{17,9},{25,17},{2,26},{10... | collective-permute-start | bytes 1572872 | tf_op jit(solution)/shard_map/ring0/ppermute | solution.py:263
  7.6 1.3 collective-permute-start.1
  8.9 1.4 %collective-permute-start.3 = (bf16[256,1024]{1,0:T(8,128)(2,1)S(1)}, bf16[256,1024]{1,0:T(8,128)(2,1)S(1)}, u32[]{:S(2)}, u32[]{:S(2)}) collective-permute-start(bf16[256,1024]{1,0:T(8,128)(2,1)S(1)} %bitcast.26), channel_id=1, source_target_pairs={{0,6},{1,7},{2,0},{3,1},{4,2},{5,3},{6,4},{7,5},{8,14},{9,15},{10,... | collective-permute-start | bytes 1572872 | tf_op jit(solution)/shard_map/mine/ppermute | solution.py:263
  10.3 1.6 %activate1.1.refs_4_.refs_1_ = bf16[512,512]{1,0:T(8,128)(2,1)S(1)} custom-call(bf16[512,1792]{1,0:T(8,128)(2,1)} %bitcast.29, bf16[512,1792]{1,0:T(8,128)(2,1)} %bitcast.33), custom_call_target="tpu_custom_call" | custom-call | flops 1000 | bytes 1000 | tf_op jit(solution)/shard_map/activate1/pallas_call | solution.py:51
  12.0 1.5 %collective-permute-done.refs_1_.refs_5_ = bf16[256,1024]{1,0:T(8,128)(2,1)S(1)} collective-permute-done((bf16[256,1024]{1,0:T(8,128)(2,1)}, bf16[256,1024]{1,0:T(8,128)(2,1)S(1)}, u32[]{:S(2)}, u32[]{:S(2)}) %collective-permute-start) | collective-permute-done | bytes 524320 | tf_op jit(solution)/shard_map/pair/ppermute | solution.py:269
  13.5 1.9 %collective-permute-start.7 = (bf16[512,512]{1,0:T(8,128)(2,1)S(1)}, bf16[512,512]{1,0:T(8,128)(2,1)S(1)}, u32[]{:S(2)}, u32[]{:S(2)}) collective-permute-start(bf16[512,512]{1,0:T(8,128)(2,1)S(1)} %activate1.1.refs_4_.refs_1_), channel_id=1, source_target_pairs={{0,8},{8,16},{16,24},{24,0},{1,9},{9,17},{17,25},{25,1},{2,10},{10... | collective-permute-start | bytes 1572872 | tf_op jit(solution)/shard_map/ring1/ppermute | solution.py:263
  15.5 3.4 %collective-permute-done.13.refs_2_ = bf16[512,512]{1,0:T(8,128)(2,1)S(1)} collective-permute-done((bf16[512,512]{1,0:T(8,128)(2,1)S(1)}, bf16[512,512]{1,0:T(8,128)(2,1)S(1)}, u32[]{:S(2)}, u32[]{:S(2)}) %collective-permute-start.13) | collective-permute-done | bytes 524320 | tf_op jit(solution)/shard_map/ring0/ppermute | solution.py:263
  18.9 1.1 collective-permute-start.8
  20.0 2.7 %collective-permute-start.4 = (bf16[256,1024]{1,0:T(8,128)(2,1)S(1)}, bf16[256,1024]{1,0:T(8,128)(2,1)S(1)}, u32[]{:S(2)}, u32[]{:S(2)}) collective-permute-start(bf16[256,1024]{1,0:T(8,128)(2,1)S(1)} %collective-permute-done.refs_1_.refs_5_), channel_id=1, source_target_pairs={{0,6},{1,7},{2,0},{3,1},{4,2},{5,3},{6,4},{7,5},{8,14},{9,15},{10,... | collective-permute-start | bytes 1572872 | tf_op jit(solution)/shard_map/paired/ppermute | solution.py:263
  22.7 1.6 %activate2.1 = (bf16[768,512]{1,0:T(8,128)(2,1)S(1)}, bf16[768,512]{1,0:T(8,128)(2,1)S(1)}) custom-call(bf16[512,1792]{1,0:T(8,128)(2,1)} %bitcast.30, bf16[512,1792]{1,0:T(8,128)(2,1)} %bitcast.34, bf16[512,512]{1,0:T(8,128)(2,1)S(1)} %collective-permute-done.13.refs_2_, bf16[512,512]{1,0:T(8,128)(2,1)S(1)} %collective-permute-done.14.refs_3_, ...), custom_call_target="tpu_custom_call" | custom-call | flops 1000 | bytes 1000 | tf_op jit(solution)/shard_map/activate2/pallas_call | solution.py:51
  24.4 0.0 collective-permute-done.1.refs_2_.refs_4_
  24.4 0.4 collective-permute-start.15
  24.8 0.0 collective-permute-done.3.refs_4_.refs_5_
  24.8 2.4 %collective-permute-start.16 = (bf16[768,512]{1,0:T(8,128)(2,1)S(1)}, bf16[768,512]{1,0:T(8,128)(2,1)S(1)}, u32[]{:S(2)}, u32[]{:S(2)}) collective-permute-start(bf16[768,512]{1,0:T(8,128)(2,1)S(1)} %get-tuple-element.26), channel_id=1, source_target_pairs={{0,24},{8,0},{16,8},{24,16},{1,25},{9,1},{17,9},{25,17},{2,26},{10... | collective-permute-start | bytes 2359304 | tf_op jit(solution)/shard_map/ring2/ppermute | solution.py:263
  27.1 2.9 %collective-permute-done.7.refs_2_ = bf16[512,512]{1,0:T(8,128)(2,1)S(1)} collective-permute-done((bf16[512,512]{1,0:T(8,128)(2,1)S(1)}, bf16[512,512]{1,0:T(8,128)(2,1)S(1)}, u32[]{:S(2)}, u32[]{:S(2)}) %collective-permute-start.7) | collective-permute-done | bytes 524320 | tf_op jit(solution)/shard_map/ring1/ppermute | solution.py:263
  30.1 1.3 collective-permute-start.2
  31.4 1.3 collective-permute-start.5
  32.7 0.0 collective-permute-done.4.refs_5_
  32.7 1.4 %collective-permute-start.6 = (bf16[256,1024]{1,0:T(8,128)(2,1)S(1)}, bf16[256,1024]{1,0:T(8,128)(2,1)S(1)}, u32[]{:S(2)}, u32[]{:S(2)}) collective-permute-start(bf16[256,1024]{1,0:T(8,128)(2,1)S(1)} %collective-permute-done.4.refs_5_), channel_id=1, source_target_pairs={{0,6},{1,7},{2,0},{3,1},{4,2},{5,3},{6,4},{7,5},{8,14},{9,15},{10,... | collective-permute-start | bytes 1572872 | tf_op jit(solution)/shard_map/far/ppermute | solution.py:263
  34.1 1.3 activate3.1
  35.4 11.5 %collective-permute-done.15.refs_0_.refs_4_.refs_2_ = bf16[768,512]{1,0:T(8,128)(2,1)S(1)} collective-permute-done((bf16[768,512]{1,0:T(8,128)(2,1)S(1)}, bf16[768,512]{1,0:T(8,128)(2,1)S(1)}, u32[]{:S(2)}, u32[]{:S(2)}) %collective-permute-start.15) | collective-permute-done | bytes 786464 | tf_op jit(solution)/shard_map/ring2/ppermute | solution.py:263
  46.9 2.7 %collective-permute-start.10 = (bf16[512,512]{1,0:T(8,128)(2,1)S(1)}, bf16[512,512]{1,0:T(8,128)(2,1)S(1)}, u32[]{:S(2)}, u32[]{:S(2)}) collective-permute-start(bf16[512,512]{1,0:T(8,128)(2,1)S(1)} %get-tuple-element.22), channel_id=1, source_target_pairs={{0,24},{8,0},{16,8},{24,16},{1,25},{9,1},{17,9},{25,17},{2,26},{10... | collective-permute-start | bytes 1572872 | tf_op jit(solution)/shard_map/ring3/ppermute | solution.py:263
  49.7 0.0 collective-permute-done.2.refs_3_
  49.7 3.7 %collective-permute-done.5.refs_6_ = bf16[256,1024]{1,0:T(8,128)(2,1)S(1)} collective-permute-done((bf16[256,1024]{1,0:T(8,128)(2,1)S(1)}, bf16[256,1024]{1,0:T(8,128)(2,1)S(1)}, u32[]{:S(2)}, u32[]{:S(2)}) %collective-permute-start.5) | collective-permute-done | bytes 524320 | tf_op jit(solution)/shard_map/far/ppermute | solution.py:263
  53.4 0.3 assemble.1.refs_0_
  53.7 6.7 %inner0.1 = (f32[2,128,1024]{2,1,0:T(8,128)S(1)}, f32[2,128,1024]{2,1,0:T(8,128)S(1)}) custom-call(bf16[2048,1024]{1,0:T(8,128)(2,1)S(1)} %assemble.1.refs_0_, bf16[512,512]{1,0:T(8,128)(2,1)S(1)} %activate0.1.refs_1_, bf16[512,512]{1,0:T(8,128)(2,1)S(1)} %collective-permute-done.13.refs_2_, bf16[512,512]{1,0:T(8,128)(2,1)S(1)} %collective-permute-done.14.refs_3_, ...), custom_call_target="tpu_custom_call" | custom-call | flops 8000001024 | bytes 1000 | tf_op jit(solution)/shard_map/inner0/pallas_call | solution.py:51
  60.4 3.6 %collective-permute-start.17 = (f32[2,128,1024]{2,1,0:T(8,128)S(1)}, f32[2,128,1024]{2,1,0:T(8,128)S(1)}, u32[]{:S(2)}, u32[]{:S(2)}) collective-permute-start(f32[2,128,1024]{2,1,0:T(8,128)S(1)} %get-tuple-element.29), channel_id=1, source_target_pairs={{0,32},{32,0},{64,96},{96,64},{1,33},{33,1},{65,97},{97,65},{2,34}... | collective-permute-start | bytes 3145736 | tf_op jit(solution)/shard_map/cores0/ppermute | solution.py:269
  64.1 0.1 collective-permute-start.11
  64.1 2.7 %collective-permute-start.12 = (bf16[128,512]{1,0:T(8,128)(2,1)S(1)}, bf16[128,512]{1,0:T(8,128)(2,1)S(1)}, u32[]{:S(2)}, u32[]{:S(2)}) collective-permute-start(bf16[128,512]{1,0:T(8,128)(2,1)S(1)} %get-tuple-element.24), channel_id=1, source_target_pairs={{0,24},{8,0},{16,8},{24,16},{1,25},{9,1},{17,9},{25,17},{2,26},{10... | collective-permute-start | bytes 393224 | tf_op jit(solution)/shard_map/ring5/ppermute | solution.py:263
  66.8 2.7 %collective-permute-start.21 = (bf16[256,512]{1,0:T(8,128)(2,1)S(1)}, bf16[256,512]{1,0:T(8,128)(2,1)S(1)}, u32[]{:S(2)}, u32[]{:S(2)}) collective-permute-start(bf16[256,512]{1,0:T(8,128)(2,1)S(1)} %get-tuple-element.32), channel_id=1, source_target_pairs={{0,24},{8,0},{16,8},{24,16},{1,25},{9,1},{17,9},{25,17},{2,26},{10... | collective-permute-start | bytes 786440 | tf_op jit(solution)/shard_map/ring4/ppermute | solution.py:263
  69.5 0.2 add_convert_fusion.5
  69.7 2.8 %collective-permute-start.22 = (f16[2,128,1024]{2,1,0:T(8,128)(2,1)S(1)}, f16[2,128,1024]{2,1,0:T(8,128)(2,1)S(1)}, u32[]{:S(2)}, u32[]{:S(2)}) collective-permute-start(f16[2,128,1024]{2,1,0:T(8,128)(2,1)S(1)} %add_convert_fusion.5), channel_id=1, source_target_pairs={{0,64},{32,96},{64,0},{96,32},{1,65},{33,97},{65,1},{97,33},{2,66}... | collective-permute-start | bytes 1572872 | tf_op jit(solution)/shard_map/chips0/ppermute | solution.py:269
  72.5 6.4 %inner1.1 = (f32[2,128,1024]{2,1,0:T(8,128)S(1)}, f32[2,128,1024]{2,1,0:T(8,128)S(1)}) custom-call(bf16[2048,1024]{1,0:T(8,128)(2,1)S(1)} %assemble.1.refs_0_, bf16[512,512]{1,0:T(8,128)(2,1)S(1)} %activate1.1.refs_4_.refs_1_, bf16[512,512]{1,0:T(8,128)(2,1)S(1)} %collective-permute-done.7.refs_2_, bf16[512,512]{1,0:T(8,128)(2,1)S(1)} %collective-permute-done.8.refs_3_, ...), custom_call_target="tpu_custom_call" | custom-call | flops 8000001024 | bytes 1000 | tf_op jit(solution)/shard_map/inner1/pallas_call | solution.py:51
  78.9 4.7 %collective-permute-done.22 = f16[2,128,1024]{2,1,0:T(8,128)(2,1)S(1)} collective-permute-done((f16[2,128,1024]{2,1,0:T(8,128)(2,1)S(1)}, f16[2,128,1024]{2,1,0:T(8,128)(2,1)S(1)}, u32[]{:S(2)}, u32[]{:S(2)}) %collective-permute-start.22) | collective-permute-done | bytes 524320 | tf_op jit(solution)/shard_map/chips0/ppermute | solution.py:269
  83.6 2.1 %collective-permute-start.18 = (f32[2,128,1024]{2,1,0:T(8,128)S(1)}, f32[2,128,1024]{2,1,0:T(8,128)S(1)}, u32[]{:S(2)}, u32[]{:S(2)}) collective-permute-start(f32[2,128,1024]{2,1,0:T(8,128)S(1)} %get-tuple-element.31), channel_id=1, source_target_pairs={{0,32},{32,0},{64,96},{96,64},{1,33},{33,1},{65,97},{97,65},{2,34}... | collective-permute-start | bytes 3145736 | tf_op jit(solution)/shard_map/cores1/ppermute | solution.py:269
  85.6 0.2 add_convert_fusion.2.refs_2_.refs_0_
  85.9 2.0 %collective-permute-done.18 = f32[2,128,1024]{2,1,0:T(8,128)S(1)} collective-permute-done((f32[2,128,1024]{2,1,0:T(8,128)S(1)}, f32[2,128,1024]{2,1,0:T(8,128)S(1)}, u32[]{:S(2)}, u32[]{:S(2)}) %collective-permute-start.18) | collective-permute-done | bytes 1048608 | tf_op jit(solution)/shard_map/cores1/ppermute | solution.py:269
  87.9 0.2 add_convert_fusion.4
  88.2 2.8 %collective-permute-start.19 = (f16[2,128,1024]{2,1,0:T(8,128)(2,1)S(1)}, f16[2,128,1024]{2,1,0:T(8,128)(2,1)S(1)}, u32[]{:S(2)}, u32[]{:S(2)}) collective-permute-start(f16[2,128,1024]{2,1,0:T(8,128)(2,1)S(1)} %add_convert_fusion.4), channel_id=1, source_target_pairs={{0,64},{32,96},{64,0},{96,32},{1,65},{33,97},{65,1},{97,33},{2,66}... | collective-permute-start | bytes 1572872 | tf_op jit(solution)/shard_map/chips1/ppermute | solution.py:269
  90.9 6.4 %inner2.1 = (f32[2,128,1024]{2,1,0:T(8,128)S(1)}, f32[2,128,1024]{2,1,0:T(8,128)S(1)}) custom-call(bf16[2048,1024]{1,0:T(8,128)(2,1)S(1)} %assemble.1.refs_0_, bf16[768,512]{1,0:T(8,128)(2,1)S(1)} %get-tuple-element.25.refs_1_, bf16[768,512]{1,0:T(8,128)(2,1)S(1)} %collective-permute-done.15.refs_0_.refs_4_.refs_2_, ...), custom_call_target="tpu_custom_call" | custom-call | flops 8000001024 | bytes 1000 | tf_op jit(solution)/shard_map/inner2/pallas_call | solution.py:51
  97.3 1.0 collective-permute-start.23
  98.3 4.6 %collective-permute-done.19 = f16[2,128,1024]{2,1,0:T(8,128)(2,1)S(1)} collective-permute-done((f16[2,128,1024]{2,1,0:T(8,128)(2,1)S(1)}, f16[2,128,1024]{2,1,0:T(8,128)(2,1)S(1)}, u32[]{:S(2)}, u32[]{:S(2)}) %collective-permute-start.19) | collective-permute-done | bytes 524320 | tf_op jit(solution)/shard_map/chips1/ppermute | solution.py:269
  102.9 0.2 add_convert_fusion.3.refs_2_.refs_0_
  103.1 0.2 add_convert_fusion.1
  103.4 3.9 %inner3.1 = (f32[2,64,1024]{2,1,0:T(8,128)S(1)}, f32[2,64,1024]{2,1,0:T(8,128)S(1)}) custom-call(bf16[2048,1024]{1,0:T(8,128)(2,1)S(1)} %assemble.1.refs_0_, bf16[512,512]{1,0:T(8,128)(2,1)S(1)} %get-tuple-element.21.refs_11_.refs_1_, bf16[512,512]{1,0:T(8,128)(2,1)S(1)} %collective-permute-done.9.refs_0_.refs_4_.refs_2_, ...), custom_call_target="tpu_custom_call" | custom-call | flops 8000001024 | bytes 1000 | tf_op jit(solution)/shard_map/inner3/pallas_call | solution.py:51
  107.3 1.3 collective-permute-start.24
  108.5 2.7 %collective-permute-start.27 = (f16[2,128,1024]{2,1,0:T(8,128)(2,1)S(1)}, f16[2,128,1024]{2,1,0:T(8,128)(2,1)S(1)}, u32[]{:S(2)}, u32[]{:S(2)}) collective-permute-start(f16[2,128,1024]{2,1,0:T(8,128)(2,1)S(1)} %add_convert_fusion.1), channel_id=1, source_target_pairs={{0,64},{32,96},{64,0},{96,32},{1,65},{33,97},{65,1},{97,33},{2,66}... | collective-permute-start | bytes 1572872 | tf_op jit(solution)/shard_map/chips2/ppermute | solution.py:269
  111.2 0.4 collective-permute-start.30
  111.6 0.2 collective-permute-start.29
  111.7 0.1 add_convert_fusion.7
  111.8 1.1 collective-permute-start.25
  112.9 10.6 %collective-permute-done.27 = f16[2,128,1024]{2,1,0:T(8,128)(2,1)S(1)} collective-permute-done((f16[2,128,1024]{2,1,0:T(8,128)(2,1)S(1)}, f16[2,128,1024]{2,1,0:T(8,128)(2,1)S(1)}, u32[]{:S(2)}, u32[]{:S(2)}) %collective-permute-start.27) | collective-permute-done | bytes 524320 | tf_op jit(solution)/shard_map/chips2/ppermute | solution.py:269
  123.5 0.2 add_convert_fusion.refs_0_
  123.7 1.4 %collective-permute-start.28 = (bf16[2,128,1024]{2,1,0:T(8,128)(2,1)S(1)}, bf16[2,128,1024]{2,1,0:T(8,128)(2,1)S(1)}, u32[]{:S(2)}, u32[]{:S(2)}) collective-permute-start(bf16[2,128,1024]{2,1,0:T(8,128)(2,1)S(1)} %add_convert_fusion.refs_0_), channel_id=1, source_target_pairs={{0,32},{32,0},{64,96},{96,64},{1,33},{33,1},{65,97},{97,65},{2,34}... | collective-permute-start | bytes 1572872 | tf_op jit(solution)/shard_map/share2/ppermute | solution.py:269
  125.2 4.0 %collective-permute-done.25 = f16[2,64,1024]{2,1,0:T(8,128)(2,1)S(1)} collective-permute-done((f16[2,64,1024]{2,1,0:T(8,128)(2,1)S(1)}, f16[2,64,1024]{2,1,0:T(8,128)(2,1)S(1)}, u32[]{:S(2)}, u32[]{:S(2)}) %collective-permute-start.25) | collective-permute-done | bytes 262176 | tf_op jit(solution)/shard_map/chips3/ppermute | solution.py:269
  129.1 0.1 add_convert_fusion.6.refs_0_
  129.2 1.0 collective-permute-start.26
  130.2 1.0 place0.1.refs_2_
  131.2 1.0 place1.1.refs_2_
  132.2 1.0 place2.1.refs_2_
  133.2 0.8 place3.1
  (28 shorter events, 0.1 us)
Async XLA Ops:
  0.0 7.6 %copy-start = (bf16[1,256,1024]{2,1,0:T(8,128)(2,1)S(1)}, bf16[1,256,1024]{2,1,0:T(8,128)(2,1)}, u32[]{:S(2)}) copy-start(bf16[1,256,1024]{2,1,0:T(8,128)(2,1)} %param.10) | copy-start | bytes 1572868
  0.0 13.5 %collective-permute-start = (bf16[256,1024]{1,0:T(8,128)(2,1)}, bf16[256,1024]{1,0:T(8,128)(2,1)S(1)}, u32[]{:S(2)}, u32[]{:S(2)}) collective-permute-start(bf16[256,1024]{1,0:T(8,128)(2,1)} %bitcast.24), channel_id=1, source_target_pairs={{0,1},{1,0},{2,3},{3,2},{4,5},{5,4},{6,7},{7,6},{8,9},{9,8},{10,11... | collective-permute-start | bytes 1572872 | tf_op jit(solution)/shard_map/pair/ppermute | solution.py:269
  3.7 15.2 %collective-permute-start.13 = (bf16[512,512]{1,0:T(8,128)(2,1)S(1)}, bf16[512,512]{1,0:T(8,128)(2,1)S(1)}, u32[]{:S(2)}, u32[]{:S(2)}) collective-permute-start(bf16[512,512]{1,0:T(8,128)(2,1)S(1)} %activate0.1.refs_1_), channel_id=1, source_target_pairs={{0,8},{8,16},{16,24},{24,0},{1,9},{9,17},{17,25},{25,1},{2,10},{10... | collective-permute-start | bytes 1572872 | tf_op jit(solution)/shard_map/ring0/ppermute | solution.py:263
  5.4 14.6 %collective-permute-start.14 = (bf16[512,512]{1,0:T(8,128)(2,1)S(1)}, bf16[512,512]{1,0:T(8,128)(2,1)S(1)}, u32[]{:S(2)}, u32[]{:S(2)}) collective-permute-start(bf16[512,512]{1,0:T(8,128)(2,1)S(1)} %activate0.1.refs_1_), channel_id=1, source_target_pairs={{0,24},{8,0},{16,8},{24,16},{1,25},{9,1},{17,9},{25,17},{2,26},{10... | collective-permute-start | bytes 1572872 | tf_op jit(solution)/shard_map/ring0/ppermute | solution.py:263
  7.6 16.8 %collective-permute-start.1 = (bf16[256,1024]{1,0:T(8,128)(2,1)S(1)}, bf16[256,1024]{1,0:T(8,128)(2,1)S(1)}, u32[]{:S(2)}, u32[]{:S(2)}) collective-permute-start(bf16[256,1024]{1,0:T(8,128)(2,1)S(1)} %bitcast.25), channel_id=1, source_target_pairs={{0,2},{1,3},{2,4},{3,5},{4,6},{5,7},{6,0},{7,1},{8,10},{9,11},{10,... | collective-permute-start | bytes 1572872 | tf_op jit(solution)/shard_map/mine/ppermute | solution.py:263
  8.9 15.9 %collective-permute-start.3 = (bf16[256,1024]{1,0:T(8,128)(2,1)S(1)}, bf16[256,1024]{1,0:T(8,128)(2,1)S(1)}, u32[]{:S(2)}, u32[]{:S(2)}) collective-permute-start(bf16[256,1024]{1,0:T(8,128)(2,1)S(1)} %bitcast.26), channel_id=1, source_target_pairs={{0,6},{1,7},{2,0},{3,1},{4,2},{5,3},{6,4},{7,5},{8,14},{9,15},{10,... | collective-permute-start | bytes 1572872 | tf_op jit(solution)/shard_map/mine/ppermute | solution.py:263
  13.5 16.5 %collective-permute-start.7 = (bf16[512,512]{1,0:T(8,128)(2,1)S(1)}, bf16[512,512]{1,0:T(8,128)(2,1)S(1)}, u32[]{:S(2)}, u32[]{:S(2)}) collective-permute-start(bf16[512,512]{1,0:T(8,128)(2,1)S(1)} %activate1.1.refs_4_.refs_1_), channel_id=1, source_target_pairs={{0,8},{8,16},{16,24},{24,0},{1,9},{9,17},{17,25},{25,1},{2,10},{10... | collective-permute-start | bytes 1572872 | tf_op jit(solution)/shard_map/ring1/ppermute | solution.py:263
  18.9 12.5 %collective-permute-start.8 = (bf16[512,512]{1,0:T(8,128)(2,1)S(1)}, bf16[512,512]{1,0:T(8,128)(2,1)S(1)}, u32[]{:S(2)}, u32[]{:S(2)}) collective-permute-start(bf16[512,512]{1,0:T(8,128)(2,1)S(1)} %activate1.1.refs_4_.refs_1_), channel_id=1, source_target_pairs={{0,24},{8,0},{16,8},{24,16},{1,25},{9,1},{17,9},{25,17},{2,26},{10... | collective-permute-start | bytes 1572872 | tf_op jit(solution)/shard_map/ring1/ppermute | solution.py:263
  20.0 12.7 %collective-permute-start.4 = (bf16[256,1024]{1,0:T(8,128)(2,1)S(1)}, bf16[256,1024]{1,0:T(8,128)(2,1)S(1)}, u32[]{:S(2)}, u32[]{:S(2)}) collective-permute-start(bf16[256,1024]{1,0:T(8,128)(2,1)S(1)} %collective-permute-done.refs_1_.refs_5_), channel_id=1, source_target_pairs={{0,6},{1,7},{2,0},{3,1},{4,2},{5,3},{6,4},{7,5},{8,14},{9,15},{10,... | collective-permute-start | bytes 1572872 | tf_op jit(solution)/shard_map/paired/ppermute | solution.py:263
  24.4 22.5 %collective-permute-start.15 = (bf16[768,512]{1,0:T(8,128)(2,1)S(1)}, bf16[768,512]{1,0:T(8,128)(2,1)S(1)}, u32[]{:S(2)}, u32[]{:S(2)}) collective-permute-start(bf16[768,512]{1,0:T(8,128)(2,1)S(1)} %get-tuple-element.25.refs_1_), channel_id=1, source_target_pairs={{0,8},{8,16},{16,24},{24,0},{1,9},{9,17},{17,25},{25,1},{2,10},{10... | collective-permute-start | bytes 2359304 | tf_op jit(solution)/shard_map/ring2/ppermute | solution.py:263
  24.8 22.2 %collective-permute-start.16 = (bf16[768,512]{1,0:T(8,128)(2,1)S(1)}, bf16[768,512]{1,0:T(8,128)(2,1)S(1)}, u32[]{:S(2)}, u32[]{:S(2)}) collective-permute-start(bf16[768,512]{1,0:T(8,128)(2,1)S(1)} %get-tuple-element.26), channel_id=1, source_target_pairs={{0,24},{8,0},{16,8},{24,16},{1,25},{9,1},{17,9},{25,17},{2,26},{10... | collective-permute-start | bytes 2359304 | tf_op jit(solution)/shard_map/ring2/ppermute | solution.py:263
  30.1 19.6 %collective-permute-start.2 = (bf16[256,1024]{1,0:T(8,128)(2,1)S(1)}, bf16[256,1024]{1,0:T(8,128)(2,1)S(1)}, u32[]{:S(2)}, u32[]{:S(2)}) collective-permute-start(bf16[256,1024]{1,0:T(8,128)(2,1)S(1)} %collective-permute-done.refs_1_.refs_5_), channel_id=1, source_target_pairs={{0,2},{1,3},{2,4},{3,5},{4,6},{5,7},{6,0},{7,1},{8,10},{9,11},{10,... | collective-permute-start | bytes 1572872 | tf_op jit(solution)/shard_map/paired/ppermute | solution.py:263
  31.4 22.0 %collective-permute-start.5 = (bf16[256,1024]{1,0:T(8,128)(2,1)S(1)}, bf16[256,1024]{1,0:T(8,128)(2,1)S(1)}, u32[]{:S(2)}, u32[]{:S(2)}) collective-permute-start(bf16[256,1024]{1,0:T(8,128)(2,1)S(1)} %collective-permute-done.1.refs_2_.refs_4_), channel_id=1, source_target_pairs={{0,2},{1,3},{2,4},{3,5},{4,6},{5,7},{6,0},{7,1},{8,10},{9,11},{10,... | collective-permute-start | bytes 1572872 | tf_op jit(solution)/shard_map/far/ppermute | solution.py:263
  32.7 20.7 %collective-permute-start.6 = (bf16[256,1024]{1,0:T(8,128)(2,1)S(1)}, bf16[256,1024]{1,0:T(8,128)(2,1)S(1)}, u32[]{:S(2)}, u32[]{:S(2)}) collective-permute-start(bf16[256,1024]{1,0:T(8,128)(2,1)S(1)} %collective-permute-done.4.refs_5_), channel_id=1, source_target_pairs={{0,6},{1,7},{2,0},{3,1},{4,2},{5,3},{6,4},{7,5},{8,14},{9,15},{10,... | collective-permute-start | bytes 1572872 | tf_op jit(solution)/shard_map/far/ppermute | solution.py:263
  46.9 17.1 %collective-permute-start.9 = (bf16[512,512]{1,0:T(8,128)(2,1)S(1)}, bf16[512,512]{1,0:T(8,128)(2,1)S(1)}, u32[]{:S(2)}, u32[]{:S(2)}) collective-permute-start(bf16[512,512]{1,0:T(8,128)(2,1)S(1)} %get-tuple-element.21.refs_11_.refs_1_), channel_id=1, source_target_pairs={{0,8},{8,16},{16,24},{24,0},{1,9},{9,17},{17,25},{25,1},{2,10},{10... | collective-permute-start | bytes 1572872 | tf_op jit(solution)/shard_map/ring3/ppermute | solution.py:263
  46.9 17.1 %collective-permute-start.10 = (bf16[512,512]{1,0:T(8,128)(2,1)S(1)}, bf16[512,512]{1,0:T(8,128)(2,1)S(1)}, u32[]{:S(2)}, u32[]{:S(2)}) collective-permute-start(bf16[512,512]{1,0:T(8,128)(2,1)S(1)} %get-tuple-element.22), channel_id=1, source_target_pairs={{0,24},{8,0},{16,8},{24,16},{1,25},{9,1},{17,9},{25,17},{2,26},{10... | collective-permute-start | bytes 1572872 | tf_op jit(solution)/shard_map/ring3/ppermute | solution.py:263
  60.4 9.1 %collective-permute-start.17 = (f32[2,128,1024]{2,1,0:T(8,128)S(1)}, f32[2,128,1024]{2,1,0:T(8,128)S(1)}, u32[]{:S(2)}, u32[]{:S(2)}) collective-permute-start(f32[2,128,1024]{2,1,0:T(8,128)S(1)} %get-tuple-element.29), channel_id=1, source_target_pairs={{0,32},{32,0},{64,96},{96,64},{1,33},{33,1},{65,97},{97,65},{2,34}... | collective-permute-start | bytes 3145736 | tf_op jit(solution)/shard_map/cores0/ppermute | solution.py:269
  64.1 39.0 %collective-permute-start.11 = (bf16[128,512]{1,0:T(8,128)(2,1)S(1)}, bf16[128,512]{1,0:T(8,128)(2,1)S(1)}, u32[]{:S(2)}, u32[]{:S(2)}) collective-permute-start(bf16[128,512]{1,0:T(8,128)(2,1)S(1)} %get-tuple-element.23.refs_11_), channel_id=1, source_target_pairs={{0,8},{8,16},{16,24},{24,0},{1,9},{9,17},{17,25},{25,1},{2,10},{10... | collective-permute-start | bytes 393224 | tf_op jit(solution)/shard_map/ring5/ppermute | solution.py:263
  64.1 39.0 %collective-permute-start.12 = (bf16[128,512]{1,0:T(8,128)(2,1)S(1)}, bf16[128,512]{1,0:T(8,128)(2,1)S(1)}, u32[]{:S(2)}, u32[]{:S(2)}) collective-permute-start(bf16[128,512]{1,0:T(8,128)(2,1)S(1)} %get-tuple-element.24), channel_id=1, source_target_pairs={{0,24},{8,0},{16,8},{24,16},{1,25},{9,1},{17,9},{25,17},{2,26},{10... | collective-permute-start | bytes 393224 | tf_op jit(solution)/shard_map/ring5/ppermute | solution.py:263
  66.8 19.0 %collective-permute-start.20 = (bf16[256,512]{1,0:T(8,128)(2,1)S(1)}, bf16[256,512]{1,0:T(8,128)(2,1)S(1)}, u32[]{:S(2)}, u32[]{:S(2)}) collective-permute-start(bf16[256,512]{1,0:T(8,128)(2,1)S(1)} %get-tuple-element.27.refs_12_), channel_id=1, source_target_pairs={{0,8},{8,16},{16,24},{24,0},{1,9},{9,17},{17,25},{25,1},{2,10},{10... | collective-permute-start | bytes 786440 | tf_op jit(solution)/shard_map/ring4/ppermute | solution.py:263
  66.8 19.1 %collective-permute-start.21 = (bf16[256,512]{1,0:T(8,128)(2,1)S(1)}, bf16[256,512]{1,0:T(8,128)(2,1)S(1)}, u32[]{:S(2)}, u32[]{:S(2)}) collective-permute-start(bf16[256,512]{1,0:T(8,128)(2,1)S(1)} %get-tuple-element.32), channel_id=1, source_target_pairs={{0,24},{8,0},{16,8},{24,16},{1,25},{9,1},{17,9},{25,17},{2,26},{10... | collective-permute-start | bytes 786440 | tf_op jit(solution)/shard_map/ring4/ppermute | solution.py:263
  69.7 13.8 %collective-permute-start.22 = (f16[2,128,1024]{2,1,0:T(8,128)(2,1)S(1)}, f16[2,128,1024]{2,1,0:T(8,128)(2,1)S(1)}, u32[]{:S(2)}, u32[]{:S(2)}) collective-permute-start(f16[2,128,1024]{2,1,0:T(8,128)(2,1)S(1)} %add_convert_fusion.5), channel_id=1, source_target_pairs={{0,64},{32,96},{64,0},{96,32},{1,65},{33,97},{65,1},{97,33},{2,66}... | collective-permute-start | bytes 1572872 | tf_op jit(solution)/shard_map/chips0/ppermute | solution.py:269
  83.6 4.4 %collective-permute-start.18 = (f32[2,128,1024]{2,1,0:T(8,128)S(1)}, f32[2,128,1024]{2,1,0:T(8,128)S(1)}, u32[]{:S(2)}, u32[]{:S(2)}) collective-permute-start(f32[2,128,1024]{2,1,0:T(8,128)S(1)} %get-tuple-element.31), channel_id=1, source_target_pairs={{0,32},{32,0},{64,96},{96,64},{1,33},{33,1},{65,97},{97,65},{2,34}... | collective-permute-start | bytes 3145736 | tf_op jit(solution)/shard_map/cores1/ppermute | solution.py:269
  88.2 14.7 %collective-permute-start.19 = (f16[2,128,1024]{2,1,0:T(8,128)(2,1)S(1)}, f16[2,128,1024]{2,1,0:T(8,128)(2,1)S(1)}, u32[]{:S(2)}, u32[]{:S(2)}) collective-permute-start(f16[2,128,1024]{2,1,0:T(8,128)(2,1)S(1)} %add_convert_fusion.4), channel_id=1, source_target_pairs={{0,64},{32,96},{64,0},{96,32},{1,65},{33,97},{65,1},{97,33},{2,66}... | collective-permute-start | bytes 1572872 | tf_op jit(solution)/shard_map/chips1/ppermute | solution.py:269
  97.3 5.8 %collective-permute-start.23 = (f32[2,128,1024]{2,1,0:T(8,128)S(1)}, f32[2,128,1024]{2,1,0:T(8,128)S(1)}, u32[]{:S(2)}, u32[]{:S(2)}) collective-permute-start(f32[2,128,1024]{2,1,0:T(8,128)S(1)} %get-tuple-element.34), channel_id=1, source_target_pairs={{0,32},{32,0},{64,96},{96,64},{1,33},{33,1},{65,97},{97,65},{2,34}... | collective-permute-start | bytes 3145736 | tf_op jit(solution)/shard_map/cores2/ppermute | solution.py:269
  107.3 4.5 %collective-permute-start.24 = (f32[2,64,1024]{2,1,0:T(8,128)S(1)}, f32[2,64,1024]{2,1,0:T(8,128)S(1)}, u32[]{:S(2)}, u32[]{:S(2)}) collective-permute-start(f32[2,64,1024]{2,1,0:T(8,128)S(1)} %get-tuple-element.36), channel_id=1, source_target_pairs={{0,32},{32,0},{64,96},{96,64},{1,33},{33,1},{65,97},{97,65},{2,34}... | collective-permute-start | bytes 1572872 | tf_op jit(solution)/shard_map/cores3/ppermute | solution.py:269
  108.5 15.0 %collective-permute-start.27 = (f16[2,128,1024]{2,1,0:T(8,128)(2,1)S(1)}, f16[2,128,1024]{2,1,0:T(8,128)(2,1)S(1)}, u32[]{:S(2)}, u32[]{:S(2)}) collective-permute-start(f16[2,128,1024]{2,1,0:T(8,128)(2,1)S(1)} %add_convert_fusion.1), channel_id=1, source_target_pairs={{0,64},{32,96},{64,0},{96,32},{1,65},{33,97},{65,1},{97,33},{2,66}... | collective-permute-start | bytes 1572872 | tf_op jit(solution)/shard_map/chips2/ppermute | solution.py:269
  111.2 18.9 %collective-permute-start.30 = (bf16[2,128,1024]{2,1,0:T(8,128)(2,1)S(1)}, bf16[2,128,1024]{2,1,0:T(8,128)(2,1)S(1)}, u32[]{:S(2)}, u32[]{:S(2)}) collective-permute-start(bf16[2,128,1024]{2,1,0:T(8,128)(2,1)S(1)} %add_convert_fusion.2.refs_2_.refs_0_), channel_id=1, source_target_pairs={{0,32},{32,0},{64,96},{96,64},{1,33},{33,1},{65,97},{97,65},{2,34}... | collective-permute-start | bytes 1572872 | tf_op jit(solution)/shard_map/share0/ppermute | solution.py:269
  111.6 19.6 %collective-permute-start.29 = (bf16[2,128,1024]{2,1,0:T(8,128)(2,1)S(1)}, bf16[2,128,1024]{2,1,0:T(8,128)(2,1)S(1)}, u32[]{:S(2)}, u32[]{:S(2)}) collective-permute-start(bf16[2,128,1024]{2,1,0:T(8,128)(2,1)S(1)} %add_convert_fusion.3.refs_2_.refs_0_), channel_id=1, source_target_pairs={{0,32},{32,0},{64,96},{96,64},{1,33},{33,1},{65,97},{97,65},{2,34}... | collective-permute-start | bytes 1572872 | tf_op jit(solution)/shard_map/share1/ppermute | solution.py:269
  111.8 17.3 %collective-permute-start.25 = (f16[2,64,1024]{2,1,0:T(8,128)(2,1)S(1)}, f16[2,64,1024]{2,1,0:T(8,128)(2,1)S(1)}, u32[]{:S(2)}, u32[]{:S(2)}) collective-permute-start(f16[2,64,1024]{2,1,0:T(8,128)(2,1)S(1)} %add_convert_fusion.7), channel_id=1, source_target_pairs={{0,64},{32,96},{64,0},{96,32},{1,65},{33,97},{65,1},{97,33},{2,66}... | collective-permute-start | bytes 786440 | tf_op jit(solution)/shard_map/chips3/ppermute | solution.py:269
  123.7 8.5 %collective-permute-start.28 = (bf16[2,128,1024]{2,1,0:T(8,128)(2,1)S(1)}, bf16[2,128,1024]{2,1,0:T(8,128)(2,1)S(1)}, u32[]{:S(2)}, u32[]{:S(2)}) collective-permute-start(bf16[2,128,1024]{2,1,0:T(8,128)(2,1)S(1)} %add_convert_fusion.refs_0_), channel_id=1, source_target_pairs={{0,32},{32,0},{64,96},{96,64},{1,33},{33,1},{65,97},{97,65},{2,34}... | collective-permute-start | bytes 1572872 | tf_op jit(solution)/shard_map/share2/ppermute | solution.py:269
  129.2 4.0 %collective-permute-start.26 = (bf16[2,64,1024]{2,1,0:T(8,128)(2,1)S(1)}, bf16[2,64,1024]{2,1,0:T(8,128)(2,1)S(1)}, u32[]{:S(2)}, u32[]{:S(2)}) collective-permute-start(bf16[2,64,1024]{2,1,0:T(8,128)(2,1)S(1)} %add_convert_fusion.6.refs_0_), channel_id=1, source_target_pairs={{0,32},{32,0},{64,96},{96,64},{1,33},{33,1},{65,97},{97,65},{2,34}... | collective-permute-start | bytes 786440 | tf_op jit(solution)/shard_map/share3/ppermute | solution.py:269

commit v3 on v2

v3 whole, which is shorter than its diff:
```python
import functools

import jax
import jax.numpy as jnp
from jax import lax
from jax.experimental import pallas as pl
from jax.experimental.pallas import tpu as pltpu
from jax.sharding import PartitionSpec as P

decay_first = 0.9
decay_second = 0.95
inner_rate = 0.25
weight_decay = 0.1
epsilon = 1e-08
outer_rate = 0.7
nesterov = 0.9
gain = outer_rate * (1.0 + nesterov)

OWNERS, OWNED, TOKENS, WIDTH = 4, 448, 512, 1024
SIZES = (176, 160, 112)
LOADED = (0, 1, 2)
MIB = 1024 * 1024
COST = dict(activate0=0, activate1=0, activate2=0, pass_on0=0, pass_on1=4, pass_on2=8, split=0, load0=8, load1=8, load2=4, assemble=0, inner0=0, inner1=0, inner2=0, hold1=0, gap0=0, gap1=0, gap2=8, gap3=0, place0=0, place1=0, place2=0)
VMEM, HBM = pltpu.VMEM, pltpu.HBM


def first_row(k):
    return sum(SIZES[:k])


def place_in_mesh():
    t, r = lax.axis_index("tensor"), lax.axis_index("region")
    return lax.axis_index("fsdp"), t // 2, lax.rem(t, 2), lax.rem(r, 2), r // 2


def put(x, space):
    return pltpu.with_memory_space_constraint(x, space)


def call(kernel, out, args, spaces, scratch, limit, name, after=(), aliases={}):
    spaces = list(spaces) + [VMEM] * len(after)
    args = [put(a, s) for a, s in zip(list(args) + list(after), spaces)]
    skip = len(after)
    count = len(args) - skip

    def body(*refs):
        kernel(*refs[:count], *refs[count + skip :])

    leaves = out if isinstance(out, list) else [out]
    specs = [pl.BlockSpec(memory_space=o.memory_space) for o in leaves]
    return pl.pallas_call(
        body,
        in_specs=[pl.BlockSpec(memory_space=s) for s in spaces],
        out_specs=specs if isinstance(out, list) else specs[0],
        out_shape=out,
        scratch_shapes=scratch,
        input_output_aliases=aliases,
        compiler_params=pltpu.CompilerParams(vmem_limit_bytes=limit),
        cost_estimate=pl.CostEstimate(flops=1000 + int(COST[name] * 1e9), bytes_accessed=1000, transcendentals=0),
        name=name,
    )(*args)


def activate(gate, up, chunks, after=()):
    size = sum(SIZES[k] for k in chunks)
    starts = [o * OWNED + first_row(chunks[0]) for o in range(OWNERS)]
    spans = [(start // 128 * 128, -(-(start + size) // 128) * 128) for start in starts]
    width = max(high - low for low, high in spans)

    def kernel(gate_ref, up_ref, *refs):
        outs, (gates, ups, sems) = refs[:-3], refs[-3:]
        copies = []
        for g, (low, high) in enumerate(spans):
            for s, (src, dst) in enumerate(((gate_ref, gates), (up_ref, ups))):
                copies.append(
                    pltpu.make_async_copy(src.at[:, low:high], dst.at[g, :, : high - low], sems.at[g, s])
                )
        for copy in copies:
            copy.start()
        for g, (low, high) in enumerate(spans):
            copies[2 * g].wait()
            copies[2 * g + 1].wait()
            gate = gates[g, :, : high - low].astype(jnp.float32)
            up = ups[g, :, : high - low].astype(jnp.float32)
            turned = (gate / (1.0 + jnp.exp(-gate)) * up).astype(jnp.bfloat16).T
            skip = starts[g] - low
            for k, out in zip(chunks, outs):
                out[g * SIZES[k] : (g + 1) * SIZES[k], :] = turned[skip : skip + SIZES[k], :]
                skip += SIZES[k]

    block = VMEM((OWNERS, TOKENS, width), jnp.bfloat16)
    return call(
        kernel,
        [VMEM((OWNERS * SIZES[k], TOKENS), jnp.bfloat16) for k in chunks],
        [gate, up],
        [HBM, HBM],
        [block, block, pltpu.SemaphoreType.DMA((OWNERS, 2))],
        16 * MIB,
        f"activate{chunks[0]}",
        after,
    )


def halves(first, second, name, after=()):
    half = first.shape[0] // 2

    def kernel(first_ref, second_ref, low, high):
        low[...] = first_ref[:half, :]
        high[...] = second_ref[half:, :]

    out = VMEM((half, first.shape[1]), jnp.bfloat16)
    return call(kernel, [out, out], [first, second], [VMEM] * 2, [], 4 * MIB, name, after)


def assemble(pieces, after=()):
    def kernel(*refs):
        _, y, x_lo, _, _ = place_in_mesh()
        out_ref = refs[-1]
        for ref, (_, hop, other, part) in zip(refs, pieces):
            rows = ref.shape[0]
            token = lax.rem(y + hop, 4) * 512 + (1 - x_lo if other else x_lo) * 256 + part * 128
            out_ref[pl.ds(pl.multiple_of(token, 128), rows), :] = ref[...]

    return call(
        kernel,
        VMEM((2048, WIDTH), jnp.bfloat16),
        [p[0] for p in pieces],
        [VMEM] * len(pieces),
        [],
        8 * MIB,
        "assemble",
        after,
    )


def state_blocks(k):
    rows = SIZES[k]
    block = lambda dtype: VMEM((OWNERS, rows, WIDTH), dtype)
    owned = VMEM((rows, WIDTH), jnp.float32)
    return [block(jnp.bfloat16), block(jnp.bfloat16), block(jnp.float32), owned, owned]


def state_copies(k, sources, targets, sems, cols, t):
    begin = first_row(k)
    rows = SIZES[k]
    copies = []
    for s in range(3):
        for o in range(OWNERS):
            at = pl.ds(o * OWNED + begin, rows)
            copies.append((sources[s].at[at, cols], targets[s].at[o, :, cols], sems.at[t, 4 * s + o]))
    for s in (3, 4):
        copies.append((sources[s].at[pl.ds(begin, rows), cols], targets[s].at[:, cols], sems.at[t, 9 + s]))
    return [pltpu.make_async_copy(*copy) for copy in copies]


def load(state, k, after=()):
    def kernel(*refs):
        copies = state_copies(k, refs[:5], refs[5:10], refs[10], slice(0, WIDTH), 0)
        for copy in copies:
            copy.start()
        for copy in copies:
            copy.wait()

    return call(
        kernel, state_blocks(k), state, [HBM] * 5, [pltpu.SemaphoreType.DMA((1, 14))], 4 * MIB, f"load{k}", after
    )


def inner_step(grads, hidden, state, loaded, k, after=(), width=512):
    rows = SIZES[k]
    tiles = WIDTH // width
    scale = gain / 4
    step = scale * inner_rate
    count = OWNERS * rows

    def kernel(grads_ref, own, before, after, far_a, far_b, *refs):
        z, _, _, core, half = place_in_mesh()
        keep, send = refs[5:7]
        copies = []
        if loaded:
            here = refs[:5]
        else:
            here, sems = refs[7:12], refs[12]
            for t in range(tiles):
                copies.append(state_copies(k, refs[:5], here, sems, pl.ds(t * width, width), t))
        ws, ms, vs, anchors, momenta = here
        for group in copies:
            for copy in group:
                copy.start()

        def dot(a, hop, cols, start=0, size=count):
            row = pl.multiple_of(lax.rem(z + hop, 4) * 512, 512)
            return jnp.dot(a[start : start + size, :], grads_ref[pl.ds(row, 512), cols], preferred_element_type=jnp.float32)

        for t in range(tiles):
            cols = slice(t * width, (t + 1) * width)
            total = dot(own, 0, cols) + dot(before, 3, cols) + dot(after, 1, cols)
            total = total + jnp.concatenate([dot(far, 2, cols, 0, count // 2) for far in (far_a, far_b)], axis=0)
            total = total.reshape(OWNERS, rows, width)
            for copy in copies[t] if copies else ():
                copy.wait()
            first_new = (step * decay_first) * ms[:, :, cols].astype(jnp.float32) + (
                step * (1.0 - decay_first) / 2048
            ) * total
            second_new = decay_second * vs[:, :, cols] + ((1.0 - decay_second) / 2048**2) * (total * total)
            root = second_new * lax.rsqrt(second_new)
            master = ws[:, :, cols].astype(jnp.float32)
            inner = (scale * (1.0 - inner_rate * weight_decay)) * master - first_new / (root + epsilon)
            rest = (1.0 - gain) * anchors[:, cols] - (outer_rate * nesterov * nesterov) * momenta[:, cols]
            for o in range(OWNERS):

                @pl.when(core == o % 2)
                def _(o=o):
                    keep[o // 2, :, cols] = inner[o]

                @pl.when(core != o % 2)
                def _(o=o):
                    send[o // 2, :, cols] = inner[o]

            keep[half, :, cols] = keep[half, :, cols] + rest

    shape = VMEM((2, rows, WIDTH), jnp.float32)
    return call(
        kernel,
        [shape, shape],
        [grads, *hidden, *state],
        [VMEM] * 6 + [VMEM if loaded else HBM] * 5,
        [] if loaded else [*state_blocks(k), pltpu.SemaphoreType.DMA((tiles, 14))],
        20 * MIB,
        f"inner{k}",
        after,
    )


def hold(arrays, k):
    def kernel(*refs):
        refs[-1][...] = jnp.zeros((8, 128), jnp.float32)

    return call(kernel, VMEM((8, 128), jnp.float32), arrays, [VMEM] * len(arrays), [], 4 * MIB, f"hold{k}")


def gap(array, name, after=()):
    out = VMEM(array.shape, array.dtype)
    return call(lambda a, b: None, out, [array], [VMEM], [], 4 * MIB, name, after, {0: 0})


def place(mine, theirs, out, k, after=()):
    rows = SIZES[k]
    begin = first_row(k)

    def kernel(mine_ref, theirs_ref, *refs):
        out_ref, said, sems = refs[-3:]
        core = place_in_mesh()[3]
        copies = []
        for i, src in enumerate((mine_ref, theirs_ref)):
            c = core if i == 0 else 1 - core
            for h in range(2):
                copies.append(
                    pltpu.make_async_copy(src.at[h], out_ref.at[2 * h + c, pl.ds(begin, rows), :], sems.at[i, h])
                )
        for copy in copies:
            copy.start()
        said[...] = jnp.zeros((8, 128), jnp.float32)
        for copy in copies:
            copy.wait()

    before = [] if out is None else [out]
    return call(
        kernel,
        [HBM((OWNERS, OWNED, WIDTH), jnp.bfloat16), VMEM((8, 128), jnp.float32)],
        [mine, theirs] + before,
        [VMEM, VMEM] + [HBM] * len(before),
        [pltpu.SemaphoreType.DMA((2, 2))],
        4 * MIB,
        f"place{k}",
        after,
        {2: 0} if before else {},
    )


def shift(x, axis, n, step):
    return lax.ppermute(x, axis, [(i, (i + step) % n) for i in range(n)])


def local(gate_pre, up_pre, out_grad, weights, first_moment, second_moment, anchor, momentum):
    along_z = functools.partial(shift, axis="fsdp", n=4)
    along_y = lambda x, step: shift(x, "tensor", 8, 2 * step)
    swap = lambda x, axis, n, bit: lax.ppermute(x, axis, [(i, i ^ bit) for i in range(n)])
    other_core = lambda x: swap(x, "region", 4, 1)
    other_chip = lambda x: swap(x, "region", 4, 2)

    state = (weights[0], first_moment[0], second_moment[0], anchor[0, 0], momentum[0, 0])
    gate, up = gate_pre[0], up_pre[0]

    def both_ways(up, down, name):
        with jax.named_scope(name):
            return along_z(up, step=1), along_z(down, step=-1)

    mine = out_grad[0]
    with jax.named_scope("pair"):
        pair = swap(mine, "tensor", 8, 1)
    with jax.named_scope("mine"):
        mine_up, mine_down = along_y(mine, 1), along_y(mine, -1)
    own = activate(gate, up, (0,))
    ring = {0: both_ways(own[0], own[0], "ring0")}
    with jax.named_scope("down"):
        pair_down = along_y(pair, -1)
    with jax.named_scope("cross"):
        cross_up = swap(mine_up, "tensor", 8, 1)
    with jax.named_scope("far"):
        mine_far = along_y(mine_up, 1)
    step = own[:1]
    loaded0 = load(state, 0, step)
    step = [loaded0[3]]
    on = halves(*ring[0], "pass_on0", [*step, pair, mine_up, mine_down])
    passed = {0: both_ways(*on, "on0")}
    last = halves(cross_up, pair_down, "split", [on[0], mine_far])
    with jax.named_scope("last"):
        last_up, last_down = along_y(last[0], 1), along_y(last[1], -1)
    own += activate(gate, up, (1,), last[:1])
    ring[1] = both_ways(own[1], own[1], "ring1")
    grads = assemble(
        [
            (mine, 0, False, 0),
            (pair, 0, True, 0),
            (mine_up, 3, False, 0),
            (cross_up, 3, True, 0),
            (mine_down, 1, False, 0),
            (pair_down, 1, True, 0),
            (mine_far, 2, False, 0),
            (last_up, 2, True, 0),
            (last_down, 2, True, 1),
        ],
    )

    out, sums, results, later, placed = None, [], [], [], []

    def finish(k, out, after=()):
        with jax.named_scope(f"share{k}"):
            shared = other_core(results[k])
        out, said = place(results[k], shared, out, k, after)
        placed.append(said)
        return out

    for k in range(len(SIZES)):
        after = []
        if k == 0:
            mine_state = loaded0
        else:
            previous = [sums[k - 1]]
            if k == 1:
                own += activate(gate, up, (2,), previous)
                ring[2] = both_ways(own[2], own[2], "ring2")
                previous = own[2:]
            mine_state = load(state, k, previous)
            if k == 1:
                after = [hold([*passed[k], mine_state[3]], k)]
        hidden = (own[k], *ring[k], *passed[k])
        keep, other = inner_step(grads, hidden, mine_state, True, k, after)
        if k + 1 < len(SIZES):
            on = halves(*ring[k + 1], f"pass_on{k + 1}", [keep, *results[:k]])
            passed[k + 1] = both_ways(*on, f"on{k + 1}")
            waited = [on[0]]
        else:
            out = finish(0, out)
            waited = placed
        with jax.named_scope(f"cores{k}"):
            arrived = other_core(other.astype(jnp.float16)).astype(jnp.float32)
        with jax.named_scope(f"sum{k}"):
            later.append(gap(keep, f"gap{k}", waited))
            both = (later[k] + arrived).astype(jnp.float16)
            sums.append(both[0, :8, :128].astype(jnp.float32))
        with jax.named_scope(f"chips{k}"):
            both_there = other_chip(both)
        with jax.named_scope(f"fresh{k}"):
            results.append((both.astype(jnp.float32) + both_there.astype(jnp.float32)).astype(jnp.bfloat16))
    out = finish(1, out)
    results[2] = gap(results[2], "gap3", placed[1:])
    out = finish(2, out)
    return out.reshape(OWNERS * OWNED, WIDTH)


def solution(mesh):
    placed = (
        P("region", "fsdp", "tensor"),
        P("region", "fsdp", "tensor"),
        P("region", "tensor", "fsdp"),
        P("region", "tensor", "fsdp"),
        P("region", "tensor", "fsdp"),
        P("region", "tensor", "fsdp"),
        P("tensor", "region", None, "fsdp"),
        P("tensor", "region", None, "fsdp"),
    )
    return jax.shard_map(
        local, mesh=mesh, in_specs=placed, out_specs=P("tensor", "fsdp"), check_vma=False
    )
```

time: 135 us -> 113 us (0.84)
  waiting for transfers between devices: 49.1 us -> 29.9 us
  Pallas kernels: 33.8 us -> 31 us
    ppermute x13 -> x11, waiting for transfers between devices: 27.5 us -> 14.8 us  [local(): lax.ppermute(x, axis, [(i, i ^ bit) for i in range(n)])]
    ppermute x18, waiting for transfers between devices: 21.6 us -> 15.1 us  [shift(): return lax.ppermute(x, axis, [(i, (i + step) % n) for i in range(n)])]
    pallas_call x17 -> x22, Pallas kernels: 33.8 us -> 31 us  [call(): pl.pallas_call(body, in_specs=[pl.BlockSpec(memory_space=s) for s in spac...]
    ppermute x13 -> x11, starting transfers between devices: 22.2 us -> 22.2 us  [local(): lax.ppermute(x, axis, [(i, i ^ bit) for i in range(n)])]
  transfers between devices with their start and end apart: 31 -> 29, of which waited for: 10 -> 11; matrix products, arithmetic and copies ran while one was open for 1% -> 1% of each run, Pallas kernels for 22% -> 25%
where the time goes in v3:
time: 113 us
  starting transfers between devices  50 us (44%)
  Pallas kernels  31 us (27%)
  waiting for transfers between devices  29.9 us (26%)
  other arithmetic  1.66 us (1%)
    pallas_call x22, Pallas kernels, call(): pl.pallas_call(body, in_specs=[pl.BlockSpec(memory_space=s) for s in spac...  31 us
    ppermute x18, starting transfers between devices, shift(): return lax.ppermute(x, axis, [(i, (i + step) % n) for i in range(n)])  27.8 us
    ppermute x11, starting transfers between devices, local(): lax.ppermute(x, axis, [(i, i ^ bit) for i in range(n)])  22.2 us
    ppermute x18, waiting for transfers between devices, shift(): return lax.ppermute(x, axis, [(i, (i + step) % n) for i in range(n)])  15.1 us
    ppermute x11, waiting for transfers between devices, local(): lax.ppermute(x, axis, [(i, i ^ bit) for i in range(n)])  14.8 us
  transfers between devices with their start and end apart: 29, of which 11 were waited for; matrix products, arithmetic and copies ran while one was open for 1% of the time, Pallas kernels for 25%

profile of v3, /device:TPU:1, one launch (start us, length us, event | category | flops | bytes accessed | tf_op | source)
XLA Modules:
  0.0 113.0 jit_solution(5382612136583682044)
XLA Ops:
  0.0 2.1 %collective-permute-start.1 = (bf16[256,1024]{1,0:T(8,128)(2,1)}, bf16[256,1024]{1,0:T(8,128)(2,1)S(1)}, u32[]{:S(2)}, u32[]{:S(2)}) collective-permute-start(bf16[256,1024]{1,0:T(8,128)(2,1)} %bitcast.19), channel_id=1, source_target_pairs={{0,2},{1,3},{2,4},{3,5},{4,6},{5,7},{6,0},{7,1},{8,10},{9,11},{10,... | collective-permute-start | bytes 1572872 | tf_op jit(solution)/shard_map/mine/ppermute | solution.py:282
  2.1 1.2 %collective-permute-start = (bf16[256,1024]{1,0:T(8,128)(2,1)}, bf16[256,1024]{1,0:T(8,128)(2,1)S(1)}, u32[]{:S(2)}, u32[]{:S(2)}) collective-permute-start(bf16[256,1024]{1,0:T(8,128)(2,1)} %bitcast.20), channel_id=1, source_target_pairs={{0,1},{1,0},{2,3},{3,2},{4,5},{5,4},{6,7},{7,6},{8,9},{9,8},{10,11... | collective-permute-start | bytes 1572872 | tf_op jit(solution)/shard_map/pair/ppermute | solution.py:288
  3.3 1.4 %collective-permute-start.3 = (bf16[256,1024]{1,0:T(8,128)(2,1)}, bf16[256,1024]{1,0:T(8,128)(2,1)S(1)}, u32[]{:S(2)}, u32[]{:S(2)}) collective-permute-start(bf16[256,1024]{1,0:T(8,128)(2,1)} %bitcast.21), channel_id=1, source_target_pairs={{0,6},{1,7},{2,0},{3,1},{4,2},{5,3},{6,4},{7,5},{8,14},{9,15},{10,... | collective-permute-start | bytes 1572872 | tf_op jit(solution)/shard_map/mine/ppermute | solution.py:282
  4.8 2.0 %activate0.1.refs_5_.refs_1_ = bf16[704,512]{1,0:T(8,128)(2,1)S(1)} custom-call(bf16[512,1792]{1,0:T(8,128)(2,1)} %bitcast.23, bf16[512,1792]{1,0:T(8,128)(2,1)} %bitcast.26), custom_call_target="tpu_custom_call" | custom-call | flops 1000 | bytes 1000 | tf_op jit(solution)/shard_map/activate0/pallas_call | solution.py:51
  6.8 1.7 %collective-permute-start.6 = (bf16[704,512]{1,0:T(8,128)(2,1)S(1)}, bf16[704,512]{1,0:T(8,128)(2,1)S(1)}, u32[]{:S(2)}, u32[]{:S(2)}) collective-permute-start(bf16[704,512]{1,0:T(8,128)(2,1)S(1)} %activate0.1.refs_5_.refs_1_), channel_id=1, source_target_pairs={{0,8},{8,16},{16,24},{24,0},{1,9},{9,17},{17,25},{25,1},{2,10},{10... | collective-permute-start | bytes 2162696 | tf_op jit(solution)/shard_map/ring0/ppermute | solution.py:282
  8.5 2.2 %collective-permute-start.7 = (bf16[704,512]{1,0:T(8,128)(2,1)S(1)}, bf16[704,512]{1,0:T(8,128)(2,1)S(1)}, u32[]{:S(2)}, u32[]{:S(2)}) collective-permute-start(bf16[704,512]{1,0:T(8,128)(2,1)S(1)} %activate0.1.refs_5_.refs_1_), channel_id=1, source_target_pairs={{0,24},{8,0},{16,8},{24,16},{1,25},{9,1},{17,9},{25,17},{2,26},{10... | collective-permute-start | bytes 2162696 | tf_op jit(solution)/shard_map/ring0/ppermute | solution.py:282
  10.7 4.6 %collective-permute-done.1.refs_4_.refs_2_ = bf16[256,1024]{1,0:T(8,128)(2,1)S(1)} collective-permute-done((bf16[256,1024]{1,0:T(8,128)(2,1)}, bf16[256,1024]{1,0:T(8,128)(2,1)S(1)}, u32[]{:S(2)}, u32[]{:S(2)}) %collective-permute-start.1) | collective-permute-done | bytes 524320 | tf_op jit(solution)/shard_map/mine/ppermute | solution.py:282
  15.3 1.1 collective-permute-start.2
  16.4 0.0 collective-permute-done.refs_3_.refs_1_
  16.4 0.0 collective-permute-start.5
  16.4 2.7 %collective-permute-start.4 = (bf16[256,1024]{1,0:T(8,128)(2,1)S(1)}, bf16[256,1024]{1,0:T(8,128)(2,1)S(1)}, u32[]{:S(2)}, u32[]{:S(2)}) collective-permute-start(bf16[256,1024]{1,0:T(8,128)(2,1)S(1)} %collective-permute-done.refs_3_.refs_1_), channel_id=1, source_target_pairs={{0,6},{1,7},{2,0},{3,1},{4,2},{5,3},{6,4},{7,5},{8,14},{9,15},{10,... | collective-permute-start | bytes 1572872 | tf_op jit(solution)/shard_map/down/ppermute | solution.py:282
  19.1 3.2 %load0.1 = (bf16[4,176,1024]{2,1,0:T(8,128)(2,1)S(1)}, bf16[4,176,1024]{2,1,0:T(8,128)(2,1)S(1)}, f32[4,176,1024]{2,1,0:T(8,128)S(1)}, f32[176,1024]{1,0:T(8,128)S(1)}, f32[176,1024]{1,0:T(8,128)S(1)}) custom-call(bf16[1792,1024]{1,0:T(8,128)(2,1)} %bitcast.32, bf16[1792,1024]{1,0:T(8,128)(2,1)} %bitcast.35, f32[1792,1024]{1,0:T(8,128)} %bitcast.29, ...), custom_call_target="tpu_custom_call" | custom-call | flops 8000001024 | bytes 1000 | tf_op jit(solution)/shard_map/load0/pallas_call | solution.py:51
  22.2 3.4 %collective-permute-done.6.refs_0_.refs_2_ = bf16[704,512]{1,0:T(8,128)(2,1)S(1)} collective-permute-done((bf16[704,512]{1,0:T(8,128)(2,1)S(1)}, bf16[704,512]{1,0:T(8,128)(2,1)S(1)}, u32[]{:S(2)}, u32[]{:S(2)}) %collective-permute-start.6) | collective-permute-done | bytes 720928 | tf_op jit(solution)/shard_map/ring0/ppermute | solution.py:282
  25.6 0.0 collective-permute-done.7.refs_1_.refs_3_
  25.7 1.6 %collective-permute-done.2.refs_0_.refs_3_ = bf16[256,1024]{1,0:T(8,128)(2,1)S(1)} collective-permute-done((bf16[256,1024]{1,0:T(8,128)(2,1)S(1)}, bf16[256,1024]{1,0:T(8,128)(2,1)S(1)}, u32[]{:S(2)}, u32[]{:S(2)}) %collective-permute-start.2) | collective-permute-done | bytes 524320 | tf_op jit(solution)/shard_map/cross/ppermute | solution.py:288
  27.3 2.0 %collective-permute-done.5.refs_3_.refs_6_ = bf16[256,1024]{1,0:T(8,128)(2,1)S(1)} collective-permute-done((bf16[256,1024]{1,0:T(8,128)(2,1)S(1)}, bf16[256,1024]{1,0:T(8,128)(2,1)S(1)}, u32[]{:S(2)}, u32[]{:S(2)}) %collective-permute-start.5) | collective-permute-done | bytes 524320 | tf_op jit(solution)/shard_map/far/ppermute | solution.py:282
  29.3 0.1 collective-permute-start.8
  29.4 1.7 %collective-permute-start.10 = (bf16[352,512]{1,0:T(8,128)(2,1)S(1)}, bf16[352,512]{1,0:T(8,128)(2,1)S(1)}, u32[]{:S(2)}, u32[]{:S(2)}) collective-permute-start(bf16[352,512]{1,0:T(8,128)(2,1)S(1)} %get-tuple-element.40.refs_2_), channel_id=1, source_target_pairs={{0,8},{8,16},{16,24},{24,0},{1,9},{9,17},{17,25},{25,1},{2,10},{10... | collective-permute-start | bytes 1081352 | tf_op jit(solution)/shard_map/on0/ppermute | solution.py:282
  31.1 2.2 %collective-permute-start.11 = (bf16[352,512]{1,0:T(8,128)(2,1)S(1)}, bf16[352,512]{1,0:T(8,128)(2,1)S(1)}, u32[]{:S(2)}, u32[]{:S(2)}) collective-permute-start(bf16[352,512]{1,0:T(8,128)(2,1)S(1)} %get-tuple-element.43), channel_id=1, source_target_pairs={{0,24},{8,0},{16,8},{24,16},{1,25},{9,1},{17,9},{25,17},{2,26},{10... | collective-permute-start | bytes 1081352 | tf_op jit(solution)/shard_map/on0/ppermute | solution.py:282
  33.3 2.2 %activate1.1.refs_1_ = bf16[640,512]{1,0:T(8,128)(2,1)S(1)} custom-call(bf16[512,1792]{1,0:T(8,128)(2,1)} %bitcast.24, bf16[512,1792]{1,0:T(8,128)(2,1)} %bitcast.27, bf16[128,1024]{1,0:T(8,128)(2,1)S(1)} %get-tuple-element.41.refs_2_), custom_call_target="tpu_custom_call" | custom-call | flops 1000 | bytes 1000 | tf_op jit(solution)/shard_map/activate1/pallas_call | solution.py:51
  35.5 0.1 collective-permute-start.12
  35.6 2.7 %collective-permute-start.13 = (bf16[640,512]{1,0:T(8,128)(2,1)S(1)}, bf16[640,512]{1,0:T(8,128)(2,1)S(1)}, u32[]{:S(2)}, u32[]{:S(2)}) collective-permute-start(bf16[640,512]{1,0:T(8,128)(2,1)S(1)} %activate1.1.refs_1_), channel_id=1, source_target_pairs={{0,24},{8,0},{16,8},{24,16},{1,25},{9,1},{17,9},{25,17},{2,26},{10... | collective-permute-start | bytes 1966088 | tf_op jit(solution)/shard_map/ring1/ppermute | solution.py:282
  38.3 2.5 %collective-permute-start.9 = (bf16[128,1024]{1,0:T(8,128)(2,1)S(1)}, bf16[128,1024]{1,0:T(8,128)(2,1)S(1)}, u32[]{:S(2)}, u32[]{:S(2)}) collective-permute-start(bf16[128,1024]{1,0:T(8,128)(2,1)S(1)} %get-tuple-element.42), channel_id=1, source_target_pairs={{0,6},{1,7},{2,0},{3,1},{4,2},{5,3},{6,4},{7,5},{8,14},{9,15},{10,... | collective-permute-start | bytes 786440 | tf_op jit(solution)/shard_map/last/ppermute | solution.py:282
  40.8 3.3 %collective-permute-done.9.refs_8_ = bf16[128,1024]{1,0:T(8,128)(2,1)S(1)} collective-permute-done((bf16[128,1024]{1,0:T(8,128)(2,1)S(1)}, bf16[128,1024]{1,0:T(8,128)(2,1)S(1)}, u32[]{:S(2)}, u32[]{:S(2)}) %collective-permute-start.9) | collective-permute-done | bytes 262176 | tf_op jit(solution)/shard_map/last/ppermute | solution.py:282
  44.1 0.3 assemble.1.refs_0_
  44.4 4.7 %inner0.1 = (f32[2,176,1024]{2,1,0:T(8,128)S(1)}, f32[2,176,1024]{2,1,0:T(8,128)S(1)}) custom-call(bf16[2048,1024]{1,0:T(8,128)(2,1)S(1)} %assemble.1.refs_0_, bf16[704,512]{1,0:T(8,128)(2,1)S(1)} %activate0.1.refs_5_.refs_1_, bf16[704,512]{1,0:T(8,128)(2,1)S(1)} %collective-permute-done.6.refs_0_.refs_2_, ...), custom_call_target="tpu_custom_call" | custom-call | flops 1000 | bytes 1000 | tf_op jit(solution)/shard_map/inner0/pallas_call | solution.py:51
  49.1 0.1 convert_element_type.64
  49.2 4.7 %collective-permute-start.14 = (f16[2,176,1024]{2,1,0:T(8,128)(2,1)S(1)}, f16[2,176,1024]{2,1,0:T(8,128)(2,1)S(1)}, u32[]{:S(2)}, u32[]{:S(2)}) collective-permute-start(f16[2,176,1024]{2,1,0:T(8,128)(2,1)S(1)} %convert_element_type.64), channel_id=1, source_target_pairs={{0,32},{32,0},{64,96},{96,64},{1,33},{33,1},{65,97},{97,65},{2,34}... | collective-permute-start | bytes 2162696 | tf_op jit(solution)/shard_map/cores0/ppermute | solution.py:288
  54.0 0.3 collective-permute-start.17
  54.3 2.7 %collective-permute-start.18 = (bf16[320,512]{1,0:T(8,128)(2,1)S(1)}, bf16[320,512]{1,0:T(8,128)(2,1)S(1)}, u32[]{:S(2)}, u32[]{:S(2)}) collective-permute-start(bf16[320,512]{1,0:T(8,128)(2,1)S(1)} %get-tuple-element.51), channel_id=1, source_target_pairs={{0,24},{8,0},{16,8},{24,16},{1,25},{9,1},{17,9},{25,17},{2,26},{10... | collective-permute-start | bytes 983048 | tf_op jit(solution)/shard_map/on1/ppermute | solution.py:282
  56.9 0.2 add_convert_fusion.1
  57.2 2.5 %collective-permute-start.19 = (f16[2,176,1024]{2,1,0:T(8,128)(2,1)S(1)}, f16[2,176,1024]{2,1,0:T(8,128)(2,1)S(1)}, u32[]{:S(2)}, u32[]{:S(2)}) collective-permute-start(f16[2,176,1024]{2,1,0:T(8,128)(2,1)S(1)} %add_convert_fusion.1), channel_id=1, source_target_pairs={{0,64},{32,96},{64,0},{96,32},{1,65},{33,97},{65,1},{97,33},{2,66}... | collective-permute-start | bytes 2162696 | tf_op jit(solution)/shard_map/chips0/ppermute | solution.py:288
  59.7 1.8 %activate2.1.refs_5_.refs_1_ = bf16[448,512]{1,0:T(8,128)(2,1)S(1)} custom-call(bf16[512,1792]{1,0:T(8,128)(2,1)} %bitcast.25, bf16[512,1792]{1,0:T(8,128)(2,1)} %bitcast.28, f32[8,128]{1,0:T(8,128)S(1)} %fusion.1.refs_2_), custom_call_target="tpu_custom_call" | custom-call | flops 1000 | bytes 1000 | tf_op jit(solution)/shard_map/activate2/pallas_call | solution.py:51
  61.6 0.1 collective-permute-start.15
  61.7 2.7 %collective-permute-start.16 = (bf16[448,512]{1,0:T(8,128)(2,1)S(1)}, bf16[448,512]{1,0:T(8,128)(2,1)S(1)}, u32[]{:S(2)}, u32[]{:S(2)}) collective-permute-start(bf16[448,512]{1,0:T(8,128)(2,1)S(1)} %activate2.1.refs_5_.refs_1_), channel_id=1, source_target_pairs={{0,24},{8,0},{16,8},{24,16},{1,25},{9,1},{17,9},{25,17},{2,26},{10... | collective-permute-start | bytes 1376264 | tf_op jit(solution)/shard_map/ring2/ppermute | solution.py:282
  64.3 3.0 %load1.1 = (bf16[4,160,1024]{2,1,0:T(8,128)(2,1)S(1)}, bf16[4,160,1024]{2,1,0:T(8,128)(2,1)S(1)}, f32[4,160,1024]{2,1,0:T(8,128)S(1)}, f32[160,1024]{1,0:T(8,128)S(1)}, f32[160,1024]{1,0:T(8,128)S(1)}) custom-call(bf16[1792,1024]{1,0:T(8,128)(2,1)} %bitcast.33, bf16[1792,1024]{1,0:T(8,128)(2,1)} %bitcast.36, f32[1792,1024]{1,0:T(8,128)} %bitcast.30, ...), custom_call_target="tpu_custom_call" | custom-call | flops 8000001024 | bytes 1000 | tf_op jit(solution)/shard_map/load1/pallas_call | solution.py:51
  67.4 4.3 %inner1.1 = (f32[2,160,1024]{2,1,0:T(8,128)S(1)}, f32[2,160,1024]{2,1,0:T(8,128)S(1)}) custom-call(bf16[2048,1024]{1,0:T(8,128)(2,1)S(1)} %assemble.1.refs_0_, bf16[640,512]{1,0:T(8,128)(2,1)S(1)} %activate1.1.refs_1_, bf16[640,512]{1,0:T(8,128)(2,1)S(1)} %collective-permute-done.12.refs_0_.refs_2_, ...), custom_call_target="tpu_custom_call" | custom-call | flops 1000 | bytes 1000 | tf_op jit(solution)/shard_map/inner1/pallas_call | solution.py:51
  71.7 0.1 convert_element_type.72
  71.8 4.2 %collective-permute-start.22 = (f16[2,160,1024]{2,1,0:T(8,128)(2,1)S(1)}, f16[2,160,1024]{2,1,0:T(8,128)(2,1)S(1)}, u32[]{:S(2)}, u32[]{:S(2)}) collective-permute-start(f16[2,160,1024]{2,1,0:T(8,128)(2,1)S(1)} %convert_element_type.72), channel_id=1, source_target_pairs={{0,32},{32,0},{64,96},{96,64},{1,33},{33,1},{65,97},{97,65},{2,34}... | collective-permute-start | bytes 1966088 | tf_op jit(solution)/shard_map/cores1/ppermute | solution.py:288
  75.9 0.3 add_convert_fusion.refs_3_.refs_0_
  76.2 1.5 %collective-permute-start.23 = (bf16[2,176,1024]{2,1,0:T(8,128)(2,1)S(1)}, bf16[2,176,1024]{2,1,0:T(8,128)(2,1)S(1)}, u32[]{:S(2)}, u32[]{:S(2)}) collective-permute-start(bf16[2,176,1024]{2,1,0:T(8,128)(2,1)S(1)} %add_convert_fusion.refs_3_.refs_0_), channel_id=1, source_target_pairs={{0,32},{32,0},{64,96},{96,64},{1,33},{33,1},{65,97},{97,65},{2,34}... | collective-permute-start | bytes 2162696 | tf_op jit(solution)/shard_map/share0/ppermute | solution.py:288
  77.8 0.1 collective-permute-start.20
  77.9 0.2 add_convert_fusion.3
  78.1 2.5 %collective-permute-start.26 = (f16[2,160,1024]{2,1,0:T(8,128)(2,1)S(1)}, f16[2,160,1024]{2,1,0:T(8,128)(2,1)S(1)}, u32[]{:S(2)}, u32[]{:S(2)}) collective-permute-start(f16[2,160,1024]{2,1,0:T(8,128)(2,1)S(1)} %add_convert_fusion.3), channel_id=1, source_target_pairs={{0,64},{32,96},{64,0},{96,32},{1,65},{33,97},{65,1},{97,33},{2,66}... | collective-permute-start | bytes 1966088 | tf_op jit(solution)/shard_map/chips1/ppermute | solution.py:288
  80.7 2.7 %collective-permute-start.21 = (bf16[224,512]{1,0:T(8,128)(2,1)S(1)}, bf16[224,512]{1,0:T(8,128)(2,1)S(1)}, u32[]{:S(2)}, u32[]{:S(2)}) collective-permute-start(bf16[224,512]{1,0:T(8,128)(2,1)S(1)} %get-tuple-element.59), channel_id=1, source_target_pairs={{0,24},{8,0},{16,8},{24,16},{1,25},{9,1},{17,9},{25,17},{2,26},{10... | collective-permute-start | bytes 688136 | tf_op jit(solution)/shard_map/on2/ppermute | solution.py:282
  83.3 2.5 %load2.1 = (bf16[4,112,1024]{2,1,0:T(8,128)(2,1)S(1)}, bf16[4,112,1024]{2,1,0:T(8,128)(2,1)S(1)}, f32[4,112,1024]{2,1,0:T(8,128)S(1)}, f32[112,1024]{1,0:T(8,128)S(1)}, f32[112,1024]{1,0:T(8,128)S(1)}) custom-call(bf16[1792,1024]{1,0:T(8,128)(2,1)} %bitcast.34, bf16[1792,1024]{1,0:T(8,128)(2,1)} %bitcast.37, f32[1792,1024]{1,0:T(8,128)} %bitcast.31, ...), custom_call_target="tpu_custom_call" | custom-call | flops 4000001024 | bytes 1000 | tf_op jit(solution)/shard_map/load2/pallas_call | solution.py:51
  85.9 0.4 collective-permute-done.20.refs_4_
  86.3 1.4 %collective-permute-done.21.refs_5_ = bf16[224,512]{1,0:T(8,128)(2,1)S(1)} collective-permute-done((bf16[224,512]{1,0:T(8,128)(2,1)S(1)}, bf16[224,512]{1,0:T(8,128)(2,1)S(1)}, u32[]{:S(2)}, u32[]{:S(2)}) %collective-permute-start.21) | collective-permute-done | bytes 229408 | tf_op jit(solution)/shard_map/on2/ppermute | solution.py:282
  87.7 3.0 %inner2.1 = (f32[2,112,1024]{2,1,0:T(8,128)S(1)}, f32[2,112,1024]{2,1,0:T(8,128)S(1)}) custom-call(bf16[2048,1024]{1,0:T(8,128)(2,1)S(1)} %assemble.1.refs_0_, bf16[448,512]{1,0:T(8,128)(2,1)S(1)} %activate2.1.refs_5_.refs_1_, bf16[448,512]{1,0:T(8,128)(2,1)S(1)} %collective-permute-done.15.refs_0_.refs_2_, ...), custom_call_target="tpu_custom_call" | custom-call | flops 1000 | bytes 1000 | tf_op jit(solution)/shard_map/inner2/pallas_call | solution.py:51
  90.7 0.1 convert_element_type.77
  90.8 1.5 %collective-permute-start.24 = (f16[2,112,1024]{2,1,0:T(8,128)(2,1)S(1)}, f16[2,112,1024]{2,1,0:T(8,128)(2,1)S(1)}, u32[]{:S(2)}, u32[]{:S(2)}) collective-permute-start(f16[2,112,1024]{2,1,0:T(8,128)(2,1)S(1)} %convert_element_type.77), channel_id=1, source_target_pairs={{0,32},{32,0},{64,96},{96,64},{1,33},{33,1},{65,97},{97,65},{2,34}... | collective-permute-start | bytes 1376264 | tf_op jit(solution)/shard_map/cores2/ppermute | solution.py:288
  92.4 1.1 place0.1
  93.5 0.3 collective-permute-done.24
  93.8 0.1 add_convert_fusion.5
  93.9 0.6 collective-permute-start.25
  94.5 1.4 %collective-permute-done.26 = f16[2,160,1024]{2,1,0:T(8,128)(2,1)S(1)} collective-permute-done((f16[2,160,1024]{2,1,0:T(8,128)(2,1)S(1)}, f16[2,160,1024]{2,1,0:T(8,128)(2,1)S(1)}, u32[]{:S(2)}, u32[]{:S(2)}) %collective-permute-start.26) | collective-permute-done | bytes 655392 | tf_op jit(solution)/shard_map/chips1/ppermute | solution.py:288
  95.9 0.3 add_convert_fusion.2.refs_0_
  96.2 1.0 collective-permute-start.27
  97.2 10.0 %collective-permute-done.25 = f16[2,112,1024]{2,1,0:T(8,128)(2,1)S(1)} collective-permute-done((f16[2,112,1024]{2,1,0:T(8,128)(2,1)S(1)}, f16[2,112,1024]{2,1,0:T(8,128)(2,1)S(1)}, u32[]{:S(2)}, u32[]{:S(2)}) %collective-permute-start.25) | collective-permute-done | bytes 458784 | tf_op jit(solution)/shard_map/chips2/ppermute | solution.py:288
  107.3 0.2 add_convert_fusion.4.refs_0_
  107.4 1.1 place1.1
  108.6 1.3 %collective-permute-start.28 = (bf16[2,112,1024]{2,1,0:T(8,128)(2,1)S(1)}, bf16[2,112,1024]{2,1,0:T(8,128)(2,1)S(1)}, u32[]{:S(2)}, u32[]{:S(2)}) collective-permute-start(bf16[2,112,1024]{2,1,0:T(8,128)(2,1)S(1)} %gap3.1.refs_0_), channel_id=1, source_target_pairs={{0,32},{32,0},{64,96},{96,64},{1,33},{33,1},{65,97},{97,65},{2,34}... | collective-permute-start | bytes 1376264 | tf_op jit(solution)/shard_map/share2/ppermute | solution.py:288
  109.8 1.4 %collective-permute-done.28.refs_1_ = bf16[2,112,1024]{2,1,0:T(8,128)(2,1)S(1)} collective-permute-done((bf16[2,112,1024]{2,1,0:T(8,128)(2,1)S(1)}, bf16[2,112,1024]{2,1,0:T(8,128)(2,1)S(1)}, u32[]{:S(2)}, u32[]{:S(2)}) %collective-permute-start.28) | collective-permute-done | bytes 458784 | tf_op jit(solution)/shard_map/share2/ppermute | solution.py:288
  111.3 1.5 %place2.1 = (bf16[4,448,1024]{2,1,0:T(8,128)(2,1)}, f32[8,128]{1,0:T(8,128)}) custom-call(bf16[2,112,1024]{2,1,0:T(8,128)(2,1)S(1)} %gap3.1.refs_0_, bf16[2,112,1024]{2,1,0:T(8,128)(2,1)S(1)} %collective-permute-done.28.refs_1_, bf16[4,448,1024]{2,1,0:T(8,128)(2,1)} %get-tuple-element.71.refs_2_), custom_call_target="tpu_custom_call", output_to_operand_aliasing={{0}: (2, {})} | custom-call | flops 1000 | bytes 1000 | tf_op jit(solution)/shard_map/place2/pallas_call | solution.py:51
  (29 shorter events, 0.2 us)
Async XLA Ops:
  0.0 15.3 %collective-permute-start.1 = (bf16[256,1024]{1,0:T(8,128)(2,1)}, bf16[256,1024]{1,0:T(8,128)(2,1)S(1)}, u32[]{:S(2)}, u32[]{:S(2)}) collective-permute-start(bf16[256,1024]{1,0:T(8,128)(2,1)} %bitcast.19), channel_id=1, source_target_pairs={{0,2},{1,3},{2,4},{3,5},{4,6},{5,7},{6,0},{7,1},{8,10},{9,11},{10,... | collective-permute-start | bytes 1572872 | tf_op jit(solution)/shard_map/mine/ppermute | solution.py:282
  2.1 14.3 %collective-permute-start = (bf16[256,1024]{1,0:T(8,128)(2,1)}, bf16[256,1024]{1,0:T(8,128)(2,1)S(1)}, u32[]{:S(2)}, u32[]{:S(2)}) collective-permute-start(bf16[256,1024]{1,0:T(8,128)(2,1)} %bitcast.20), channel_id=1, source_target_pairs={{0,1},{1,0},{2,3},{3,2},{4,5},{5,4},{6,7},{7,6},{8,9},{9,8},{10,11... | collective-permute-start | bytes 1572872 | tf_op jit(solution)/shard_map/pair/ppermute | solution.py:288
  3.3 13.1 %collective-permute-start.3 = (bf16[256,1024]{1,0:T(8,128)(2,1)}, bf16[256,1024]{1,0:T(8,128)(2,1)S(1)}, u32[]{:S(2)}, u32[]{:S(2)}) collective-permute-start(bf16[256,1024]{1,0:T(8,128)(2,1)} %bitcast.21), channel_id=1, source_target_pairs={{0,6},{1,7},{2,0},{3,1},{4,2},{5,3},{6,4},{7,5},{8,14},{9,15},{10,... | collective-permute-start | bytes 1572872 | tf_op jit(solution)/shard_map/mine/ppermute | solution.py:282
  6.8 18.8 %collective-permute-start.6 = (bf16[704,512]{1,0:T(8,128)(2,1)S(1)}, bf16[704,512]{1,0:T(8,128)(2,1)S(1)}, u32[]{:S(2)}, u32[]{:S(2)}) collective-permute-start(bf16[704,512]{1,0:T(8,128)(2,1)S(1)} %activate0.1.refs_5_.refs_1_), channel_id=1, source_target_pairs={{0,8},{8,16},{16,24},{24,0},{1,9},{9,17},{17,25},{25,1},{2,10},{10... | collective-permute-start | bytes 2162696 | tf_op jit(solution)/shard_map/ring0/ppermute | solution.py:282
  8.5 17.1 %collective-permute-start.7 = (bf16[704,512]{1,0:T(8,128)(2,1)S(1)}, bf16[704,512]{1,0:T(8,128)(2,1)S(1)}, u32[]{:S(2)}, u32[]{:S(2)}) collective-permute-start(bf16[704,512]{1,0:T(8,128)(2,1)S(1)} %activate0.1.refs_5_.refs_1_), channel_id=1, source_target_pairs={{0,24},{8,0},{16,8},{24,16},{1,25},{9,1},{17,9},{25,17},{2,26},{10... | collective-permute-start | bytes 2162696 | tf_op jit(solution)/shard_map/ring0/ppermute | solution.py:282
  15.3 12.0 %collective-permute-start.2 = (bf16[256,1024]{1,0:T(8,128)(2,1)S(1)}, bf16[256,1024]{1,0:T(8,128)(2,1)S(1)}, u32[]{:S(2)}, u32[]{:S(2)}) collective-permute-start(bf16[256,1024]{1,0:T(8,128)(2,1)S(1)} %collective-permute-done.1.refs_4_.refs_2_), channel_id=1, source_target_pairs={{0,1},{1,0},{2,3},{3,2},{4,5},{5,4},{6,7},{7,6},{8,9},{9,8},{10,11... | collective-permute-start | bytes 1572872 | tf_op jit(solution)/shard_map/cross/ppermute | solution.py:288
  16.4 12.9 %collective-permute-start.5 = (bf16[256,1024]{1,0:T(8,128)(2,1)S(1)}, bf16[256,1024]{1,0:T(8,128)(2,1)S(1)}, u32[]{:S(2)}, u32[]{:S(2)}) collective-permute-start(bf16[256,1024]{1,0:T(8,128)(2,1)S(1)} %collective-permute-done.1.refs_4_.refs_2_), channel_id=1, source_target_pairs={{0,2},{1,3},{2,4},{3,5},{4,6},{5,7},{6,0},{7,1},{8,10},{9,11},{10,... | collective-permute-start | bytes 1572872 | tf_op jit(solution)/shard_map/far/ppermute | solution.py:282
  16.4 12.9 %collective-permute-start.4 = (bf16[256,1024]{1,0:T(8,128)(2,1)S(1)}, bf16[256,1024]{1,0:T(8,128)(2,1)S(1)}, u32[]{:S(2)}, u32[]{:S(2)}) collective-permute-start(bf16[256,1024]{1,0:T(8,128)(2,1)S(1)} %collective-permute-done.refs_3_.refs_1_), channel_id=1, source_target_pairs={{0,6},{1,7},{2,0},{3,1},{4,2},{5,3},{6,4},{7,5},{8,14},{9,15},{10,... | collective-permute-start | bytes 1572872 | tf_op jit(solution)/shard_map/down/ppermute | solution.py:282
  29.3 9.0 %collective-permute-start.8 = (bf16[128,1024]{1,0:T(8,128)(2,1)S(1)}, bf16[128,1024]{1,0:T(8,128)(2,1)S(1)}, u32[]{:S(2)}, u32[]{:S(2)}) collective-permute-start(bf16[128,1024]{1,0:T(8,128)(2,1)S(1)} %get-tuple-element.41.refs_2_), channel_id=1, source_target_pairs={{0,2},{1,3},{2,4},{3,5},{4,6},{5,7},{6,0},{7,1},{8,10},{9,11},{10,... | collective-permute-start | bytes 786440 | tf_op jit(solution)/shard_map/last/ppermute | solution.py:282
  29.4 15.0 %collective-permute-start.10 = (bf16[352,512]{1,0:T(8,128)(2,1)S(1)}, bf16[352,512]{1,0:T(8,128)(2,1)S(1)}, u32[]{:S(2)}, u32[]{:S(2)}) collective-permute-start(bf16[352,512]{1,0:T(8,128)(2,1)S(1)} %get-tuple-element.40.refs_2_), channel_id=1, source_target_pairs={{0,8},{8,16},{16,24},{24,0},{1,9},{9,17},{17,25},{25,1},{2,10},{10... | collective-permute-start | bytes 1081352 | tf_op jit(solution)/shard_map/on0/ppermute | solution.py:282
  31.1 13.0 %copy-start = (bf16[1,256,1024]{2,1,0:T(8,128)(2,1)S(1)}, bf16[1,256,1024]{2,1,0:T(8,128)(2,1)}, u32[]{:S(2)}) copy-start(bf16[1,256,1024]{2,1,0:T(8,128)(2,1)} %param.10) | copy-start | bytes 1572868
  31.1 13.3 %collective-permute-start.11 = (bf16[352,512]{1,0:T(8,128)(2,1)S(1)}, bf16[352,512]{1,0:T(8,128)(2,1)S(1)}, u32[]{:S(2)}, u32[]{:S(2)}) collective-permute-start(bf16[352,512]{1,0:T(8,128)(2,1)S(1)} %get-tuple-element.43), channel_id=1, source_target_pairs={{0,24},{8,0},{16,8},{24,16},{1,25},{9,1},{17,9},{25,17},{2,26},{10... | collective-permute-start | bytes 1081352 | tf_op jit(solution)/shard_map/on0/ppermute | solution.py:282
  35.5 18.4 %collective-permute-start.12 = (bf16[640,512]{1,0:T(8,128)(2,1)S(1)}, bf16[640,512]{1,0:T(8,128)(2,1)S(1)}, u32[]{:S(2)}, u32[]{:S(2)}) collective-permute-start(bf16[640,512]{1,0:T(8,128)(2,1)S(1)} %activate1.1.refs_1_), channel_id=1, source_target_pairs={{0,8},{8,16},{16,24},{24,0},{1,9},{9,17},{17,25},{25,1},{2,10},{10... | collective-permute-start | bytes 1966088 | tf_op jit(solution)/shard_map/ring1/ppermute | solution.py:282
  35.6 18.4 %collective-permute-start.13 = (bf16[640,512]{1,0:T(8,128)(2,1)S(1)}, bf16[640,512]{1,0:T(8,128)(2,1)S(1)}, u32[]{:S(2)}, u32[]{:S(2)}) collective-permute-start(bf16[640,512]{1,0:T(8,128)(2,1)S(1)} %activate1.1.refs_1_), channel_id=1, source_target_pairs={{0,24},{8,0},{16,8},{24,16},{1,25},{9,1},{17,9},{25,17},{2,26},{10... | collective-permute-start | bytes 1966088 | tf_op jit(solution)/shard_map/ring1/ppermute | solution.py:282
  38.3 5.8 %collective-permute-start.9 = (bf16[128,1024]{1,0:T(8,128)(2,1)S(1)}, bf16[128,1024]{1,0:T(8,128)(2,1)S(1)}, u32[]{:S(2)}, u32[]{:S(2)}) collective-permute-start(bf16[128,1024]{1,0:T(8,128)(2,1)S(1)} %get-tuple-element.42), channel_id=1, source_target_pairs={{0,6},{1,7},{2,0},{3,1},{4,2},{5,3},{6,4},{7,5},{8,14},{9,15},{10,... | collective-permute-start | bytes 786440 | tf_op jit(solution)/shard_map/last/ppermute | solution.py:282
  49.2 7.7 %collective-permute-start.14 = (f16[2,176,1024]{2,1,0:T(8,128)(2,1)S(1)}, f16[2,176,1024]{2,1,0:T(8,128)(2,1)S(1)}, u32[]{:S(2)}, u32[]{:S(2)}) collective-permute-start(f16[2,176,1024]{2,1,0:T(8,128)(2,1)S(1)} %convert_element_type.64), channel_id=1, source_target_pairs={{0,32},{32,0},{64,96},{96,64},{1,33},{33,1},{65,97},{97,65},{2,34}... | collective-permute-start | bytes 2162696 | tf_op jit(solution)/shard_map/cores0/ppermute | solution.py:288
  54.0 13.3 %collective-permute-start.17 = (bf16[320,512]{1,0:T(8,128)(2,1)S(1)}, bf16[320,512]{1,0:T(8,128)(2,1)S(1)}, u32[]{:S(2)}, u32[]{:S(2)}) collective-permute-start(bf16[320,512]{1,0:T(8,128)(2,1)S(1)} %get-tuple-element.49.refs_1_), channel_id=1, source_target_pairs={{0,8},{8,16},{16,24},{24,0},{1,9},{9,17},{17,25},{25,1},{2,10},{10... | collective-permute-start | bytes 983048 | tf_op jit(solution)/shard_map/on1/ppermute | solution.py:282
  54.3 13.1 %collective-permute-start.18 = (bf16[320,512]{1,0:T(8,128)(2,1)S(1)}, bf16[320,512]{1,0:T(8,128)(2,1)S(1)}, u32[]{:S(2)}, u32[]{:S(2)}) collective-permute-start(bf16[320,512]{1,0:T(8,128)(2,1)S(1)} %get-tuple-element.51), channel_id=1, source_target_pairs={{0,24},{8,0},{16,8},{24,16},{1,25},{9,1},{17,9},{25,17},{2,26},{10... | collective-permute-start | bytes 983048 | tf_op jit(solution)/shard_map/on1/ppermute | solution.py:282
  57.2 18.7 %collective-permute-start.19 = (f16[2,176,1024]{2,1,0:T(8,128)(2,1)S(1)}, f16[2,176,1024]{2,1,0:T(8,128)(2,1)S(1)}, u32[]{:S(2)}, u32[]{:S(2)}) collective-permute-start(f16[2,176,1024]{2,1,0:T(8,128)(2,1)S(1)} %add_convert_fusion.1), channel_id=1, source_target_pairs={{0,64},{32,96},{64,0},{96,32},{1,65},{33,97},{65,1},{97,33},{2,66}... | collective-permute-start | bytes 2162696 | tf_op jit(solution)/shard_map/chips0/ppermute | solution.py:288
  61.6 16.2 %collective-permute-start.15 = (bf16[448,512]{1,0:T(8,128)(2,1)S(1)}, bf16[448,512]{1,0:T(8,128)(2,1)S(1)}, u32[]{:S(2)}, u32[]{:S(2)}) collective-permute-start(bf16[448,512]{1,0:T(8,128)(2,1)S(1)} %activate2.1.refs_5_.refs_1_), channel_id=1, source_target_pairs={{0,8},{8,16},{16,24},{24,0},{1,9},{9,17},{17,25},{25,1},{2,10},{10... | collective-permute-start | bytes 1376264 | tf_op jit(solution)/shard_map/ring2/ppermute | solution.py:282
  61.7 16.1 %collective-permute-start.16 = (bf16[448,512]{1,0:T(8,128)(2,1)S(1)}, bf16[448,512]{1,0:T(8,128)(2,1)S(1)}, u32[]{:S(2)}, u32[]{:S(2)}) collective-permute-start(bf16[448,512]{1,0:T(8,128)(2,1)S(1)} %activate2.1.refs_5_.refs_1_), channel_id=1, source_target_pairs={{0,24},{8,0},{16,8},{24,16},{1,25},{9,1},{17,9},{25,17},{2,26},{10... | collective-permute-start | bytes 1376264 | tf_op jit(solution)/shard_map/ring2/ppermute | solution.py:282
  71.8 6.1 %collective-permute-start.22 = (f16[2,160,1024]{2,1,0:T(8,128)(2,1)S(1)}, f16[2,160,1024]{2,1,0:T(8,128)(2,1)S(1)}, u32[]{:S(2)}, u32[]{:S(2)}) collective-permute-start(f16[2,160,1024]{2,1,0:T(8,128)(2,1)S(1)} %convert_element_type.72), channel_id=1, source_target_pairs={{0,32},{32,0},{64,96},{96,64},{1,33},{33,1},{65,97},{97,65},{2,34}... | collective-permute-start | bytes 1966088 | tf_op jit(solution)/shard_map/cores1/ppermute | solution.py:288
  76.2 16.1 %collective-permute-start.23 = (bf16[2,176,1024]{2,1,0:T(8,128)(2,1)S(1)}, bf16[2,176,1024]{2,1,0:T(8,128)(2,1)S(1)}, u32[]{:S(2)}, u32[]{:S(2)}) collective-permute-start(bf16[2,176,1024]{2,1,0:T(8,128)(2,1)S(1)} %add_convert_fusion.refs_3_.refs_0_), channel_id=1, source_target_pairs={{0,32},{32,0},{64,96},{96,64},{1,33},{33,1},{65,97},{97,65},{2,34}... | collective-permute-start | bytes 2162696 | tf_op jit(solution)/shard_map/share0/ppermute | solution.py:288
  77.8 8.5 %collective-permute-start.20 = (bf16[224,512]{1,0:T(8,128)(2,1)S(1)}, bf16[224,512]{1,0:T(8,128)(2,1)S(1)}, u32[]{:S(2)}, u32[]{:S(2)}) collective-permute-start(bf16[224,512]{1,0:T(8,128)(2,1)S(1)} %get-tuple-element.58.refs_1_), channel_id=1, source_target_pairs={{0,8},{8,16},{16,24},{24,0},{1,9},{9,17},{17,25},{25,1},{2,10},{10... | collective-permute-start | bytes 688136 | tf_op jit(solution)/shard_map/on2/ppermute | solution.py:282
  78.1 17.8 %collective-permute-start.26 = (f16[2,160,1024]{2,1,0:T(8,128)(2,1)S(1)}, f16[2,160,1024]{2,1,0:T(8,128)(2,1)S(1)}, u32[]{:S(2)}, u32[]{:S(2)}) collective-permute-start(f16[2,160,1024]{2,1,0:T(8,128)(2,1)S(1)} %add_convert_fusion.3), channel_id=1, source_target_pairs={{0,64},{32,96},{64,0},{96,32},{1,65},{33,97},{65,1},{97,33},{2,66}... | collective-permute-start | bytes 1966088 | tf_op jit(solution)/shard_map/chips1/ppermute | solution.py:288
  80.7 7.0 %collective-permute-start.21 = (bf16[224,512]{1,0:T(8,128)(2,1)S(1)}, bf16[224,512]{1,0:T(8,128)(2,1)S(1)}, u32[]{:S(2)}, u32[]{:S(2)}) collective-permute-start(bf16[224,512]{1,0:T(8,128)(2,1)S(1)} %get-tuple-element.59), channel_id=1, source_target_pairs={{0,24},{8,0},{16,8},{24,16},{1,25},{9,1},{17,9},{25,17},{2,26},{10... | collective-permute-start | bytes 688136 | tf_op jit(solution)/shard_map/on2/ppermute | solution.py:282
  90.8 3.0 %collective-permute-start.24 = (f16[2,112,1024]{2,1,0:T(8,128)(2,1)S(1)}, f16[2,112,1024]{2,1,0:T(8,128)(2,1)S(1)}, u32[]{:S(2)}, u32[]{:S(2)}) collective-permute-start(f16[2,112,1024]{2,1,0:T(8,128)(2,1)S(1)} %convert_element_type.77), channel_id=1, source_target_pairs={{0,32},{32,0},{64,96},{96,64},{1,33},{33,1},{65,97},{97,65},{2,34}... | collective-permute-start | bytes 1376264 | tf_op jit(solution)/shard_map/cores2/ppermute | solution.py:288
  93.9 13.3 %collective-permute-start.25 = (f16[2,112,1024]{2,1,0:T(8,128)(2,1)S(1)}, f16[2,112,1024]{2,1,0:T(8,128)(2,1)S(1)}, u32[]{:S(2)}, u32[]{:S(2)}) collective-permute-start(f16[2,112,1024]{2,1,0:T(8,128)(2,1)S(1)} %add_convert_fusion.5), channel_id=1, source_target_pairs={{0,64},{32,96},{64,0},{96,32},{1,65},{33,97},{65,1},{97,33},{2,66}... | collective-permute-start | bytes 1376264 | tf_op jit(solution)/shard_map/chips2/ppermute | solution.py:288
  96.2 11.2 %collective-permute-start.27 = (bf16[2,160,1024]{2,1,0:T(8,128)(2,1)S(1)}, bf16[2,160,1024]{2,1,0:T(8,128)(2,1)S(1)}, u32[]{:S(2)}, u32[]{:S(2)}) collective-permute-start(bf16[2,160,1024]{2,1,0:T(8,128)(2,1)S(1)} %add_convert_fusion.2.refs_0_), channel_id=1, source_target_pairs={{0,32},{32,0},{64,96},{96,64},{1,33},{33,1},{65,97},{97,65},{2,34}... | collective-permute-start | bytes 1966088 | tf_op jit(solution)/shard_map/share1/ppermute | solution.py:288
  108.6 2.7 %collective-permute-start.28 = (bf16[2,112,1024]{2,1,0:T(8,128)(2,1)S(1)}, bf16[2,112,1024]{2,1,0:T(8,128)(2,1)S(1)}, u32[]{:S(2)}, u32[]{:S(2)}) collective-permute-start(bf16[2,112,1024]{2,1,0:T(8,128)(2,1)S(1)} %gap3.1.refs_0_), channel_id=1, source_target_pairs={{0,32},{32,0},{64,96},{96,64},{1,33},{33,1},{65,97},{97,65},{2,34}... | collective-permute-start | bytes 1376264 | tf_op jit(solution)/shard_map/share2/ppermute | solution.py:288

commit v4 on v3

--- a/solution.py
+++ b/solution.py
@@ -20,7 +20,7 @@
 SIZES = (176, 160, 112)
 LOADED = (0, 1, 2)
 MIB = 1024 * 1024
-COST = dict(activate0=0, activate1=0, activate2=0, pass_on0=0, pass_on1=4, pass_on2=8, split=0, load0=8, load1=8, load2=4, assemble=0, inner0=0, inner1=0, inner2=0, hold1=0, gap0=0, gap1=0, gap2=8, gap3=0, place0=0, place1=0, place2=0)
+COST = dict(near1=0, near2=8, activate0=0, activate1=0, gap_ring1=0, gap_ring2=0, tick=4, pass_on0=0, pass_on1=1, pass_on2=8, split=0, load0=8, load1=0, load2=4, assemble=0, inner0=0, inner1=0, inner2=0, hold1=0, gap0=0, gap1=0, gap2=8, gap3=0, place0=0, place1=0, place2=0)
 VMEM, HBM = pltpu.VMEM, pltpu.HBM
 
 
@@ -166,6 +166,23 @@
     )
 
 
+def near_step(grads, hidden, k, after=(), width=512):
+    count = OWNERS * SIZES[k]
+
+    def kernel(grads_ref, own, before, after, total):
+        z = place_in_mesh()[0]
+        for t in range(WIDTH // width):
+            cols = slice(t * width, (t + 1) * width)
+            parts = []
+            for ref, hop in ((own, 0), (before, 3), (after, 1)):
+                row = pl.multiple_of(lax.rem(z + hop, 4) * 512, 512)
+                parts.append(jnp.dot(ref[...], grads_ref[pl.ds(row, 512), cols], preferred_element_type=jnp.float32))
+            total[:, cols] = parts[0] + parts[1] + parts[2]
+
+    out = VMEM((count, WIDTH), jnp.float32)
+    return call(kernel, out, [grads, *hidden], [VMEM] * 4, [], 12 * MIB, f"near{k}", after)
+
+
 def inner_step(grads, hidden, state, loaded, k, after=(), width=512):
     rows = SIZES[k]
     tiles = WIDTH // width
@@ -173,7 +190,11 @@
     step = scale * inner_rate
     count = OWNERS * rows
 
-    def kernel(grads_ref, own, before, after, far_a, far_b, *refs):
+    near = len(hidden) == 3
+
+    def kernel(grads_ref, *refs):
+        hidden_refs, refs = refs[: len(hidden)], refs[len(hidden) :]
+        far_a, far_b = hidden_refs[-2:]
         z, _, _, core, half = place_in_mesh()
         keep, send = refs[5:7]
         copies = []
@@ -194,7 +215,11 @@
 
         for t in range(tiles):
             cols = slice(t * width, (t + 1) * width)
-            total = dot(own, 0, cols) + dot(before, 3, cols) + dot(after, 1, cols)
+            if near:
+                total = hidden_refs[0][:, cols]
+            else:
+                own, before, after = hidden_refs[:3]
+                total = dot(own, 0, cols) + dot(before, 3, cols) + dot(after, 1, cols)
             total = total + jnp.concatenate([dot(far, 2, cols, 0, count // 2) for far in (far_a, far_b)], axis=0)
             total = total.reshape(OWNERS, rows, width)
             for copy in copies[t] if copies else ():
@@ -224,7 +249,7 @@
         kernel,
         [shape, shape],
         [grads, *hidden, *state],
-        [VMEM] * 6 + [VMEM if loaded else HBM] * 5,
+        [VMEM] * (1 + len(hidden)) + [VMEM if loaded else HBM] * 5,
         [] if loaded else [*state_blocks(k), pltpu.SemaphoreType.DMA((tiles, 14))],
         20 * MIB,
         f"inner{k}",
@@ -232,11 +257,11 @@
     )
 
 
-def hold(arrays, k):
+def hold(arrays, name):
     def kernel(*refs):
         refs[-1][...] = jnp.zeros((8, 128), jnp.float32)
 
-    return call(kernel, VMEM((8, 128), jnp.float32), arrays, [VMEM] * len(arrays), [], 4 * MIB, f"hold{k}")
+    return call(kernel, VMEM((8, 128), jnp.float32), arrays, [VMEM] * len(arrays), [], 4 * MIB, name)
 
 
 def gap(array, name, after=()):
@@ -244,20 +269,18 @@
     return call(lambda a, b: None, out, [array], [VMEM], [], 4 * MIB, name, after, {0: 0})
 
 
-def place(mine, theirs, out, k, after=()):
-    rows = SIZES[k]
-    begin = first_row(k)
-
-    def kernel(mine_ref, theirs_ref, *refs):
+def place(pieces, out, name):
+    count = len(pieces)
+
+    def kernel(*refs):
         out_ref, said, sems = refs[-3:]
         core = place_in_mesh()[3]
         copies = []
-        for i, src in enumerate((mine_ref, theirs_ref)):
-            c = core if i == 0 else 1 - core
+        for i, (ref, (_, theirs, k)) in enumerate(zip(refs, pieces)):
+            c = 1 - core if theirs else core
             for h in range(2):
-                copies.append(
-                    pltpu.make_async_copy(src.at[h], out_ref.at[2 * h + c, pl.ds(begin, rows), :], sems.at[i, h])
-                )
+                to = out_ref.at[2 * h + c, pl.ds(first_row(k), SIZES[k]), :]
+                copies.append(pltpu.make_async_copy(ref.at[h], to, sems.at[i, h]))
         for copy in copies:
             copy.start()
         said[...] = jnp.zeros((8, 128), jnp.float32)
@@ -268,13 +291,12 @@
     return call(
         kernel,
         [HBM((OWNERS, OWNED, WIDTH), jnp.bfloat16), VMEM((8, 128), jnp.float32)],
-        [mine, theirs] + before,
-        [VMEM, VMEM] + [HBM] * len(before),
-        [pltpu.SemaphoreType.DMA((2, 2))],
+        [p[0] for p in pieces] + before,
+        [VMEM] * count + [HBM] * len(before),
+        [pltpu.SemaphoreType.DMA((count, 2))],
         4 * MIB,
-        f"place{k}",
-        after,
-        {2: 0} if before else {},
+        name,
+        aliases={count: 0} if before else {},
     )
 
 
@@ -301,7 +323,8 @@
         pair = swap(mine, "tensor", 8, 1)
     with jax.named_scope("mine"):
         mine_up, mine_down = along_y(mine, 1), along_y(mine, -1)
-    own = activate(gate, up, (0,))
+    own = list(activate(gate, up, (0,)))
+    later_own = activate(gate, up, (1, 2), own)
     ring = {0: both_ways(own[0], own[0], "ring0")}
     with jax.named_scope("down"):
         pair_down = along_y(pair, -1)
@@ -309,15 +332,14 @@
         cross_up = swap(mine_up, "tensor", 8, 1)
     with jax.named_scope("far"):
         mine_far = along_y(mine_up, 1)
-    step = own[:1]
-    loaded0 = load(state, 0, step)
-    step = [loaded0[3]]
-    on = halves(*ring[0], "pass_on0", [*step, pair, mine_up, mine_down])
+    loaded = [load(state, 0, later_own[:1])]
+    loaded.append(load(state, 1, loaded[0][3:4]))
+    on = halves(*ring[0], "pass_on0", [loaded[1][3], pair, mine_up, mine_down])
     passed = {0: both_ways(*on, "on0")}
     last = halves(cross_up, pair_down, "split", [on[0], mine_far])
     with jax.named_scope("last"):
         last_up, last_down = along_y(last[0], 1), along_y(last[1], -1)
-    own += activate(gate, up, (1,), last[:1])
+    own.append(gap(later_own[0], "gap_ring1", last[:1]))
     ring[1] = both_ways(own[1], own[1], "ring1")
     grads = assemble(
         [
@@ -333,37 +355,32 @@
         ],
     )
 
-    out, sums, results, later, placed = None, [], [], [], []
-
-    def finish(k, out, after=()):
+    sums, results, later = [], [], []
+
+    def share(k):
         with jax.named_scope(f"share{k}"):
-            shared = other_core(results[k])
-        out, said = place(results[k], shared, out, k, after)
-        placed.append(said)
-        return out
+            return other_core(results[k])
 
     for k in range(len(SIZES)):
         after = []
-        if k == 0:
-            mine_state = loaded0
-        else:
-            previous = [sums[k - 1]]
-            if k == 1:
-                own += activate(gate, up, (2,), previous)
-                ring[2] = both_ways(own[2], own[2], "ring2")
-                previous = own[2:]
-            mine_state = load(state, k, previous)
-            if k == 1:
-                after = [hold([*passed[k], mine_state[3]], k)]
-        hidden = (own[k], *ring[k], *passed[k])
-        keep, other = inner_step(grads, hidden, mine_state, True, k, after)
+        if k == 1:
+            own.append(gap(later_own[1], "gap_ring2", sums))
+            ring[2] = both_ways(own[2], own[2], "ring2")
+            near = near_step(grads, (own[1], *ring[1]), 1, own[2:])
+            after = [hold([*passed[k], hold([near], "tick")], "hold1")]
+        if k == 2:
+            loaded.append(load(state, 2, sums[1:]))
+            near = near_step(grads, (own[2], *ring[2]), 2, loaded[2][3:4])
+        hidden = (near, *passed[k]) if k else (own[k], *ring[k], *passed[k])
+        keep, other = inner_step(grads, hidden, loaded[k], True, k, after)
         if k + 1 < len(SIZES):
             on = halves(*ring[k + 1], f"pass_on{k + 1}", [keep, *results[:k]])
             passed[k + 1] = both_ways(*on, f"on{k + 1}")
             waited = [on[0]]
         else:
-            out = finish(0, out)
-            waited = placed
+            results[0] = gap(results[0], "gap3", loaded[2][3:4])
+            out, said = place([(results[0], False, 0), (share(0), True, 0)], None, "place0")
+            waited = [said]
         with jax.named_scope(f"cores{k}"):
             arrived = other_core(other.astype(jnp.float16)).astype(jnp.float32)
         with jax.named_scope(f"sum{k}"):
@@ -374,9 +391,8 @@
             both_there = other_chip(both)
         with jax.named_scope(f"fresh{k}"):
             results.append((both.astype(jnp.float32) + both_there.astype(jnp.float32)).astype(jnp.bfloat16))
-    out = finish(1, out)
-    results[2] = gap(results[2], "gap3", placed[1:])
-    out = finish(2, out)
+    out, _ = place([(results[1], False, 1), (share(1), True, 1), (results[2], False, 2)], out, "place1")
+    out, _ = place([(share(2), True, 2)], out, "place2")
     return out.reshape(OWNERS * OWNED, WIDTH)
 
 

time: 113 us -> 107 us (0.947)
  waiting for transfers between devices: 29.9 us -> 20.9 us
  starting transfers between devices: 50 us -> 53.5 us
    ppermute x11, starting transfers between devices: 22.2 us -> 27.3 us  [local(): lax.ppermute(x, axis, [(i, i ^ bit) for i in range(n)])]
    ppermute x11, waiting for transfers between devices: 14.8 us -> 9.87 us  [local(): lax.ppermute(x, axis, [(i, i ^ bit) for i in range(n)])]
    ppermute x18, waiting for transfers between devices: 15.1 us -> 11.1 us  [shift(): return lax.ppermute(x, axis, [(i, (i + step) % n) for i in range(n)])]
    ppermute x18, starting transfers between devices: 27.8 us -> 26.1 us  [shift(): return lax.ppermute(x, axis, [(i, (i + step) % n) for i in range(n)])]
    pallas_call x22 -> x26, Pallas kernels: 31 us -> 30.5 us  [call(): pl.pallas_call(body, in_specs=[pl.BlockSpec(memory_space=s) for s in spac...]
  transfers between devices with their start and end apart: 29 -> 29, of which waited for: 11 -> 11; matrix products, arithmetic and copies ran while one was open for 1% -> 1% of each run, Pallas kernels for 25% -> 27%
where the time goes in v4:
time: 107 us
  starting transfers between devices  53.5 us (50%)
  Pallas kernels  30.5 us (29%)
  waiting for transfers between devices  20.9 us (20%)
  other arithmetic  1.66 us (2%)
    pallas_call x26, Pallas kernels, call(): pl.pallas_call(body, in_specs=[pl.BlockSpec(memory_space=s) for s in spac...  30.5 us
    ppermute x11, starting transfers between devices, local(): lax.ppermute(x, axis, [(i, i ^ bit) for i in range(n)])  27.3 us
    ppermute x18, starting transfers between devices, shift(): return lax.ppermute(x, axis, [(i, (i + step) % n) for i in range(n)])  26.1 us
    ppermute x18, waiting for transfers between devices, shift(): return lax.ppermute(x, axis, [(i, (i + step) % n) for i in range(n)])  11.1 us
    ppermute x11, waiting for transfers between devices, local(): lax.ppermute(x, axis, [(i, i ^ bit) for i in range(n)])  9.87 us
  transfers between devices with their start and end apart: 29, of which 11 were waited for; matrix products, arithmetic and copies ran while one was open for 1% of the time, Pallas kernels for 27%

profile of v4, /device:TPU:1, one launch (start us, length us, event | category | flops | bytes accessed | tf_op | source)
XLA Modules:
  0.0 107.0 jit_solution(3046619412077129531)
XLA Ops:
  0.0 2.1 %collective-permute-start.1 = (bf16[256,1024]{1,0:T(8,128)(2,1)}, bf16[256,1024]{1,0:T(8,128)(2,1)S(1)}, u32[]{:S(2)}, u32[]{:S(2)}) collective-permute-start(bf16[256,1024]{1,0:T(8,128)(2,1)} %bitcast.19), channel_id=1, source_target_pairs={{0,2},{1,3},{2,4},{3,5},{4,6},{5,7},{6,0},{7,1},{8,10},{9,11},{10,... | collective-permute-start | bytes 1572872 | tf_op jit(solution)/shard_map/mine/ppermute | solution.py:304
  2.1 1.4 %collective-permute-start.3 = (bf16[256,1024]{1,0:T(8,128)(2,1)}, bf16[256,1024]{1,0:T(8,128)(2,1)S(1)}, u32[]{:S(2)}, u32[]{:S(2)}) collective-permute-start(bf16[256,1024]{1,0:T(8,128)(2,1)} %bitcast.20), channel_id=1, source_target_pairs={{0,6},{1,7},{2,0},{3,1},{4,2},{5,3},{6,4},{7,5},{8,14},{9,15},{10,... | collective-permute-start | bytes 1572872 | tf_op jit(solution)/shard_map/mine/ppermute | solution.py:304
  3.6 1.2 %collective-permute-start = (bf16[256,1024]{1,0:T(8,128)(2,1)}, bf16[256,1024]{1,0:T(8,128)(2,1)S(1)}, u32[]{:S(2)}, u32[]{:S(2)}) collective-permute-start(bf16[256,1024]{1,0:T(8,128)(2,1)} %bitcast.21), channel_id=1, source_target_pairs={{0,1},{1,0},{2,3},{3,2},{4,5},{5,4},{6,7},{7,6},{8,9},{9,8},{10,11... | collective-permute-start | bytes 1572872 | tf_op jit(solution)/shard_map/pair/ppermute | solution.py:310
  4.8 2.0 %activate0.1.refs_2_.refs_1_ = bf16[704,512]{1,0:T(8,128)(2,1)S(1)} custom-call(bf16[512,1792]{1,0:T(8,128)(2,1)} %bitcast.38, bf16[512,1792]{1,0:T(8,128)(2,1)} %bitcast.40), custom_call_target="tpu_custom_call" | custom-call | flops 1000 | bytes 1000 | tf_op jit(solution)/shard_map/activate0/pallas_call | solution.py:51
  6.8 3.8 %collective-permute-start.7 = (bf16[704,512]{1,0:T(8,128)(2,1)S(1)}, bf16[704,512]{1,0:T(8,128)(2,1)S(1)}, u32[]{:S(2)}, u32[]{:S(2)}) collective-permute-start(bf16[704,512]{1,0:T(8,128)(2,1)S(1)} %activate0.1.refs_2_.refs_1_), channel_id=1, source_target_pairs={{0,24},{8,0},{16,8},{24,16},{1,25},{9,1},{17,9},{25,17},{2,26},{10... | collective-permute-start | bytes 2162696 | tf_op jit(solution)/shard_map/ring0/ppermute | solution.py:304
  10.6 0.0 collective-permute-start.6
  10.6 2.4 %activate1.1 = (bf16[640,512]{1,0:T(8,128)(2,1)S(1)}, bf16[448,512]{1,0:T(8,128)(2,1)S(1)}) custom-call(bf16[512,1792]{1,0:T(8,128)(2,1)} %bitcast.39, bf16[512,1792]{1,0:T(8,128)(2,1)} %bitcast.41, bf16[704,512]{1,0:T(8,128)(2,1)S(1)} %activate0.1.refs_2_.refs_1_), custom_call_target="tpu_custom_call" | custom-call | flops 1000 | bytes 1000 | tf_op jit(solution)/shard_map/activate1/pallas_call | solution.py:51
  13.1 2.2 %collective-permute-done.1.refs_4_.refs_2_ = bf16[256,1024]{1,0:T(8,128)(2,1)S(1)} collective-permute-done((bf16[256,1024]{1,0:T(8,128)(2,1)}, bf16[256,1024]{1,0:T(8,128)(2,1)S(1)}, u32[]{:S(2)}, u32[]{:S(2)}) %collective-permute-start.1) | collective-permute-done | bytes 524320 | tf_op jit(solution)/shard_map/mine/ppermute | solution.py:304
  15.3 0.0 collective-permute-start.5
  15.3 0.0 collective-permute-done.3.refs_5_.refs_4_
  15.3 1.1 %collective-permute-start.2 = (bf16[256,1024]{1,0:T(8,128)(2,1)S(1)}, bf16[256,1024]{1,0:T(8,128)(2,1)S(1)}, u32[]{:S(2)}, u32[]{:S(2)}) collective-permute-start(bf16[256,1024]{1,0:T(8,128)(2,1)S(1)} %collective-permute-done.1.refs_4_.refs_2_), channel_id=1, source_target_pairs={{0,1},{1,0},{2,3},{3,2},{4,5},{5,4},{6,7},{7,6},{8,9},{9,8},{10,11... | collective-permute-start | bytes 1572872 | tf_op jit(solution)/shard_map/cross/ppermute | solution.py:310
  16.4 2.7 %collective-permute-start.4 = (bf16[256,1024]{1,0:T(8,128)(2,1)S(1)}, bf16[256,1024]{1,0:T(8,128)(2,1)S(1)}, u32[]{:S(2)}, u32[]{:S(2)}) collective-permute-start(bf16[256,1024]{1,0:T(8,128)(2,1)S(1)} %collective-permute-done.refs_3_.refs_1_), channel_id=1, source_target_pairs={{0,6},{1,7},{2,0},{3,1},{4,2},{5,3},{6,4},{7,5},{8,14},{9,15},{10,... | collective-permute-start | bytes 1572872 | tf_op jit(solution)/shard_map/down/ppermute | solution.py:304
  19.1 3.2 %load0.1 = (bf16[4,176,1024]{2,1,0:T(8,128)(2,1)S(1)}, bf16[4,176,1024]{2,1,0:T(8,128)(2,1)S(1)}, f32[4,176,1024]{2,1,0:T(8,128)S(1)}, f32[176,1024]{1,0:T(8,128)S(1)}, f32[176,1024]{1,0:T(8,128)S(1)}) custom-call(bf16[1792,1024]{1,0:T(8,128)(2,1)} %bitcast.26, bf16[1792,1024]{1,0:T(8,128)(2,1)} %bitcast.29, f32[1792,1024]{1,0:T(8,128)} %bitcast.23, ...), custom_call_target="tpu_custom_call" | custom-call | flops 8000001024 | bytes 1000 | tf_op jit(solution)/shard_map/load0/pallas_call | solution.py:51
  22.2 3.0 %load1.1 = (bf16[4,160,1024]{2,1,0:T(8,128)(2,1)S(1)}, bf16[4,160,1024]{2,1,0:T(8,128)(2,1)S(1)}, f32[4,160,1024]{2,1,0:T(8,128)S(1)}, f32[160,1024]{1,0:T(8,128)S(1)}, f32[160,1024]{1,0:T(8,128)S(1)}) custom-call(bf16[1792,1024]{1,0:T(8,128)(2,1)} %bitcast.27, bf16[1792,1024]{1,0:T(8,128)(2,1)} %bitcast.30, f32[1792,1024]{1,0:T(8,128)} %bitcast.24, ...), custom_call_target="tpu_custom_call" | custom-call | flops 1000 | bytes 1000 | tf_op jit(solution)/shard_map/load1/pallas_call | solution.py:51
  25.2 0.0 collective-permute-done.7.refs_1_.refs_3_
  25.3 2.5 %collective-permute-done.6.refs_0_.refs_2_ = bf16[704,512]{1,0:T(8,128)(2,1)S(1)} collective-permute-done((bf16[704,512]{1,0:T(8,128)(2,1)S(1)}, bf16[704,512]{1,0:T(8,128)(2,1)S(1)}, u32[]{:S(2)}, u32[]{:S(2)}) %collective-permute-start.6) | collective-permute-done | bytes 720928 | tf_op jit(solution)/shard_map/ring0/ppermute | solution.py:304
  27.8 1.4 %collective-permute-start.11 = (bf16[352,512]{1,0:T(8,128)(2,1)S(1)}, bf16[352,512]{1,0:T(8,128)(2,1)S(1)}, u32[]{:S(2)}, u32[]{:S(2)}) collective-permute-start(bf16[352,512]{1,0:T(8,128)(2,1)S(1)} %get-tuple-element.47), channel_id=1, source_target_pairs={{0,24},{8,0},{16,8},{24,16},{1,25},{9,1},{17,9},{25,17},{2,26},{10... | collective-permute-start | bytes 1081352 | tf_op jit(solution)/shard_map/on0/ppermute | solution.py:304
  29.2 0.1 collective-permute-start.10
  29.3 0.0 collective-permute-done.5.refs_3_.refs_6_
  29.4 2.4 %collective-permute-start.9 = (bf16[128,1024]{1,0:T(8,128)(2,1)S(1)}, bf16[128,1024]{1,0:T(8,128)(2,1)S(1)}, u32[]{:S(2)}, u32[]{:S(2)}) collective-permute-start(bf16[128,1024]{1,0:T(8,128)(2,1)S(1)} %get-tuple-element.45), channel_id=1, source_target_pairs={{0,6},{1,7},{2,0},{3,1},{4,2},{5,3},{6,4},{7,5},{8,14},{9,15},{10,... | collective-permute-start | bytes 786440 | tf_op jit(solution)/shard_map/last/ppermute | solution.py:304
  31.8 3.8 %collective-permute-start.13 = (bf16[640,512]{1,0:T(8,128)(2,1)S(1)}, bf16[640,512]{1,0:T(8,128)(2,1)S(1)}, u32[]{:S(2)}, u32[]{:S(2)}) collective-permute-start(bf16[640,512]{1,0:T(8,128)(2,1)S(1)} %gap_ring1.1.refs_1_), channel_id=1, source_target_pairs={{0,24},{8,0},{16,8},{24,16},{1,25},{9,1},{17,9},{25,17},{2,26},{10... | collective-permute-start | bytes 1966088 | tf_op jit(solution)/shard_map/ring1/ppermute | solution.py:304
  35.5 1.2 %collective-permute-start.12 = (bf16[640,512]{1,0:T(8,128)(2,1)S(1)}, bf16[640,512]{1,0:T(8,128)(2,1)S(1)}, u32[]{:S(2)}, u32[]{:S(2)}) collective-permute-start(bf16[640,512]{1,0:T(8,128)(2,1)S(1)} %gap_ring1.1.refs_1_), channel_id=1, source_target_pairs={{0,8},{8,16},{16,24},{24,0},{1,9},{9,17},{17,25},{25,1},{2,10},{10... | collective-permute-start | bytes 1966088 | tf_op jit(solution)/shard_map/ring1/ppermute | solution.py:304
  36.7 1.8 %collective-permute-done.8.refs_7_ = bf16[128,1024]{1,0:T(8,128)(2,1)S(1)} collective-permute-done((bf16[128,1024]{1,0:T(8,128)(2,1)S(1)}, bf16[128,1024]{1,0:T(8,128)(2,1)S(1)}, u32[]{:S(2)}, u32[]{:S(2)}) %collective-permute-start.8) | collective-permute-done | bytes 262176 | tf_op jit(solution)/shard_map/last/ppermute | solution.py:304
  38.5 0.3 assemble.1.refs_0_
  38.8 4.7 %inner0.1 = (f32[2,176,1024]{2,1,0:T(8,128)S(1)}, f32[2,176,1024]{2,1,0:T(8,128)S(1)}) custom-call(bf16[2048,1024]{1,0:T(8,128)(2,1)S(1)} %assemble.1.refs_0_, bf16[704,512]{1,0:T(8,128)(2,1)S(1)} %activate0.1.refs_2_.refs_1_, bf16[704,512]{1,0:T(8,128)(2,1)S(1)} %collective-permute-done.6.refs_0_.refs_2_, ...), custom_call_target="tpu_custom_call" | custom-call | flops 1000 | bytes 1000 | tf_op jit(solution)/shard_map/inner0/pallas_call | solution.py:51
  43.5 0.1 convert_element_type.64
  43.6 4.4 %collective-permute-start.14 = (f16[2,176,1024]{2,1,0:T(8,128)(2,1)S(1)}, f16[2,176,1024]{2,1,0:T(8,128)(2,1)S(1)}, u32[]{:S(2)}, u32[]{:S(2)}) collective-permute-start(f16[2,176,1024]{2,1,0:T(8,128)(2,1)S(1)} %convert_element_type.64), channel_id=1, source_target_pairs={{0,32},{32,0},{64,96},{96,64},{1,33},{33,1},{65,97},{97,65},{2,34}... | collective-permute-start | bytes 2162696 | tf_op jit(solution)/shard_map/cores0/ppermute | solution.py:310
  48.0 1.1 %collective-permute-done.13.refs_1_.refs_3_ = bf16[640,512]{1,0:T(8,128)(2,1)S(1)} collective-permute-done((bf16[640,512]{1,0:T(8,128)(2,1)S(1)}, bf16[640,512]{1,0:T(8,128)(2,1)S(1)}, u32[]{:S(2)}, u32[]{:S(2)}) %collective-permute-start.13) | collective-permute-done | bytes 655392 | tf_op jit(solution)/shard_map/ring1/ppermute | solution.py:304
  49.1 2.4 %collective-permute-done.12.refs_0_.refs_2_ = bf16[640,512]{1,0:T(8,128)(2,1)S(1)} collective-permute-done((bf16[640,512]{1,0:T(8,128)(2,1)S(1)}, bf16[640,512]{1,0:T(8,128)(2,1)S(1)}, u32[]{:S(2)}, u32[]{:S(2)}) %collective-permute-start.12) | collective-permute-done | bytes 655392 | tf_op jit(solution)/shard_map/ring1/ppermute | solution.py:304
  51.6 0.2 add_convert_fusion.1
  51.8 2.5 %collective-permute-start.19 = (f16[2,176,1024]{2,1,0:T(8,128)(2,1)S(1)}, f16[2,176,1024]{2,1,0:T(8,128)(2,1)S(1)}, u32[]{:S(2)}, u32[]{:S(2)}) collective-permute-start(f16[2,176,1024]{2,1,0:T(8,128)(2,1)S(1)} %add_convert_fusion.1), channel_id=1, source_target_pairs={{0,64},{32,96},{64,0},{96,32},{1,65},{33,97},{65,1},{97,33},{2,66}... | collective-permute-start | bytes 2162696 | tf_op jit(solution)/shard_map/chips0/ppermute | solution.py:310
  54.3 2.7 %collective-permute-start.18 = (bf16[320,512]{1,0:T(8,128)(2,1)S(1)}, bf16[320,512]{1,0:T(8,128)(2,1)S(1)}, u32[]{:S(2)}, u32[]{:S(2)}) collective-permute-start(bf16[320,512]{1,0:T(8,128)(2,1)S(1)} %get-tuple-element.55), channel_id=1, source_target_pairs={{0,24},{8,0},{16,8},{24,16},{1,25},{9,1},{17,9},{25,17},{2,26},{10... | collective-permute-start | bytes 983048 | tf_op jit(solution)/shard_map/on1/ppermute | solution.py:304
  57.0 0.8 collective-permute-start.16
  57.8 0.7 collective-permute-start.15
  58.5 2.2 %near1.1.refs_0_.refs_1_ = f32[640,1024]{1,0:T(8,128)S(1)} custom-call(bf16[2048,1024]{1,0:T(8,128)(2,1)S(1)} %assemble.1.refs_0_, bf16[640,512]{1,0:T(8,128)(2,1)S(1)} %gap_ring1.1.refs_1_, bf16[640,512]{1,0:T(8,128)(2,1)S(1)} %collective-permute-done.12.refs_0_.refs_2_, bf16[640,512]{1,0:T(8,128)(2,1)S(1)} %collective-permute-done.13.refs_1_.refs_3_, ...), custom_call_target="tpu_custom_call" | custom-call | flops 1000 | bytes 1000 | tf_op jit(solution)/shard_map/near1/pallas_call | solution.py:51
  60.7 0.3 collective-permute-done.18.refs_1_.refs_3_
  61.0 0.7 collective-permute-done.17.refs_0_.refs_2_
  61.8 2.4 %inner1.1 = (f32[2,160,1024]{2,1,0:T(8,128)S(1)}, f32[2,160,1024]{2,1,0:T(8,128)S(1)}) custom-call(bf16[2048,1024]{1,0:T(8,128)(2,1)S(1)} %assemble.1.refs_0_, f32[640,1024]{1,0:T(8,128)S(1)} %near1.1.refs_0_.refs_1_, bf16[320,512]{1,0:T(8,128)(2,1)S(1)} %collective-permute-done.17.refs_0_.refs_2_, ...), custom_call_target="tpu_custom_call" | custom-call | flops 1000 | bytes 1000 | tf_op jit(solution)/shard_map/inner1/pallas_call | solution.py:51
  64.1 0.1 convert_element_type.72
  64.2 8.5 %collective-permute-start.20 = (f16[2,160,1024]{2,1,0:T(8,128)(2,1)S(1)}, f16[2,160,1024]{2,1,0:T(8,128)(2,1)S(1)}, u32[]{:S(2)}, u32[]{:S(2)}) collective-permute-start(f16[2,160,1024]{2,1,0:T(8,128)(2,1)S(1)} %convert_element_type.72), channel_id=1, source_target_pairs={{0,32},{32,0},{64,96},{96,64},{1,33},{33,1},{65,97},{97,65},{2,34}... | collective-permute-start | bytes 1966088 | tf_op jit(solution)/shard_map/cores1/ppermute | solution.py:310
  72.8 0.3 add_convert_fusion.refs_3_.refs_0_
  73.2 0.1 collective-permute-start.21
  73.3 1.2 %collective-permute-done.20 = f16[2,160,1024]{2,1,0:T(8,128)(2,1)S(1)} collective-permute-done((f16[2,160,1024]{2,1,0:T(8,128)(2,1)S(1)}, f16[2,160,1024]{2,1,0:T(8,128)(2,1)S(1)}, u32[]{:S(2)}, u32[]{:S(2)}) %collective-permute-start.20) | collective-permute-done | bytes 655392 | tf_op jit(solution)/shard_map/cores1/ppermute | solution.py:310
  74.5 0.2 add_convert_fusion.3
  74.8 0.6 collective-permute-start.27
  75.4 3.0 %collective-permute-start.22 = (bf16[224,512]{1,0:T(8,128)(2,1)S(1)}, bf16[224,512]{1,0:T(8,128)(2,1)S(1)}, u32[]{:S(2)}, u32[]{:S(2)}) collective-permute-start(bf16[224,512]{1,0:T(8,128)(2,1)S(1)} %get-tuple-element.64), channel_id=1, source_target_pairs={{0,24},{8,0},{16,8},{24,16},{1,25},{9,1},{17,9},{25,17},{2,26},{10... | collective-permute-start | bytes 688136 | tf_op jit(solution)/shard_map/on2/ppermute | solution.py:304
  78.3 2.5 %load2.1 = (bf16[4,112,1024]{2,1,0:T(8,128)(2,1)S(1)}, bf16[4,112,1024]{2,1,0:T(8,128)(2,1)S(1)}, f32[4,112,1024]{2,1,0:T(8,128)S(1)}, f32[112,1024]{1,0:T(8,128)S(1)}, f32[112,1024]{1,0:T(8,128)S(1)}) custom-call(bf16[1792,1024]{1,0:T(8,128)(2,1)} %bitcast.28, bf16[1792,1024]{1,0:T(8,128)(2,1)} %bitcast.31, f32[1792,1024]{1,0:T(8,128)} %bitcast.25, ...), custom_call_target="tpu_custom_call" | custom-call | flops 4000001024 | bytes 1000 | tf_op jit(solution)/shard_map/load2/pallas_call | solution.py:51
  80.9 1.7 %collective-permute-start.23 = (bf16[2,176,1024]{2,1,0:T(8,128)(2,1)S(1)}, bf16[2,176,1024]{2,1,0:T(8,128)(2,1)S(1)}, u32[]{:S(2)}, u32[]{:S(2)}) collective-permute-start(bf16[2,176,1024]{2,1,0:T(8,128)(2,1)S(1)} %gap3.1.refs_0_), channel_id=1, source_target_pairs={{0,32},{32,0},{64,96},{96,64},{1,33},{33,1},{65,97},{97,65},{2,34}... | collective-permute-start | bytes 2162696 | tf_op jit(solution)/shard_map/share0/ppermute | solution.py:310
  82.6 1.6 %near2.1.refs_1_ = f32[448,1024]{1,0:T(8,128)S(1)} custom-call(bf16[2048,1024]{1,0:T(8,128)(2,1)S(1)} %assemble.1.refs_0_, bf16[448,512]{1,0:T(8,128)(2,1)S(1)} %gap_ring2.1.refs_4_.refs_1_, bf16[448,512]{1,0:T(8,128)(2,1)S(1)} %collective-permute-done.15.refs_0_.refs_2_, bf16[448,512]{1,0:T(8,128)(2,1)S(1)} %collective-permute-done.16.refs_1_.refs_3_, ...), custom_call_target="tpu_custom_call" | custom-call | flops 8000001024 | bytes 1000 | tf_op jit(solution)/shard_map/near2/pallas_call | solution.py:51
  84.2 1.7 %inner2.1 = (f32[2,112,1024]{2,1,0:T(8,128)S(1)}, f32[2,112,1024]{2,1,0:T(8,128)S(1)}) custom-call(bf16[2048,1024]{1,0:T(8,128)(2,1)S(1)} %assemble.1.refs_0_, f32[448,1024]{1,0:T(8,128)S(1)} %near2.1.refs_1_, bf16[224,512]{1,0:T(8,128)(2,1)S(1)} %collective-permute-done.21.refs_2_, bf16[224,512]{1,0:T(8,128)(2,1)S(1)} %collective-permute-done.22.refs_3_, ...), custom_call_target="tpu_custom_call" | custom-call | flops 1000 | bytes 1000 | tf_op jit(solution)/shard_map/inner2/pallas_call | solution.py:51
  85.9 0.1 convert_element_type.77
  86.0 0.1 collective-permute-start.24
  86.1 1.1 %place0.1 = (bf16[4,448,1024]{2,1,0:T(8,128)(2,1)}, f32[8,128]{1,0:T(8,128)S(1)}) custom-call(bf16[2,176,1024]{2,1,0:T(8,128)(2,1)S(1)} %gap3.1.refs_0_, bf16[2,176,1024]{2,1,0:T(8,128)(2,1)S(1)} %collective-permute-done.23.refs_1_), custom_call_target="tpu_custom_call" | custom-call | flops 1000 | bytes 1000 | tf_op jit(solution)/shard_map/place0/pallas_call | solution.py:51
  87.3 0.6 collective-permute-done.24
  87.9 0.1 add_convert_fusion.5
  88.1 2.5 %collective-permute-start.25 = (f16[2,112,1024]{2,1,0:T(8,128)(2,1)S(1)}, f16[2,112,1024]{2,1,0:T(8,128)(2,1)S(1)}, u32[]{:S(2)}, u32[]{:S(2)}) collective-permute-start(f16[2,112,1024]{2,1,0:T(8,128)(2,1)S(1)} %add_convert_fusion.5), channel_id=1, source_target_pairs={{0,64},{32,96},{64,0},{96,32},{1,65},{33,97},{65,1},{97,33},{2,66}... | collective-permute-start | bytes 1376264 | tf_op jit(solution)/shard_map/chips2/ppermute | solution.py:310
  90.6 0.3 collective-permute-done.27
  90.9 0.3 add_convert_fusion.2.refs_0_
  91.2 3.4 %collective-permute-start.28 = (bf16[2,160,1024]{2,1,0:T(8,128)(2,1)S(1)}, bf16[2,160,1024]{2,1,0:T(8,128)(2,1)S(1)}, u32[]{:S(2)}, u32[]{:S(2)}) collective-permute-start(bf16[2,160,1024]{2,1,0:T(8,128)(2,1)S(1)} %add_convert_fusion.2.refs_0_), channel_id=1, source_target_pairs={{0,32},{32,0},{64,96},{96,64},{1,33},{33,1},{65,97},{97,65},{2,34}... | collective-permute-start | bytes 1966088 | tf_op jit(solution)/shard_map/share1/ppermute | solution.py:310
  94.6 7.7 %collective-permute-done.25 = f16[2,112,1024]{2,1,0:T(8,128)(2,1)S(1)} collective-permute-done((f16[2,112,1024]{2,1,0:T(8,128)(2,1)S(1)}, f16[2,112,1024]{2,1,0:T(8,128)(2,1)S(1)}, u32[]{:S(2)}, u32[]{:S(2)}) %collective-permute-start.25) | collective-permute-done | bytes 458784 | tf_op jit(solution)/shard_map/chips2/ppermute | solution.py:310
  102.2 0.2 add_convert_fusion.4.refs_2_
  102.4 1.2 %collective-permute-start.26 = (bf16[2,112,1024]{2,1,0:T(8,128)(2,1)S(1)}, bf16[2,112,1024]{2,1,0:T(8,128)(2,1)S(1)}, u32[]{:S(2)}, u32[]{:S(2)}) collective-permute-start(bf16[2,112,1024]{2,1,0:T(8,128)(2,1)S(1)} %add_convert_fusion.4.refs_2_), channel_id=1, source_target_pairs={{0,32},{32,0},{64,96},{96,64},{1,33},{33,1},{65,97},{97,65},{2,34}... | collective-permute-start | bytes 1376264 | tf_op jit(solution)/shard_map/share2/ppermute | solution.py:310
  103.6 1.8 %place1.1 = (bf16[4,448,1024]{2,1,0:T(8,128)(2,1)}, f32[8,128]{1,0:T(8,128)}) custom-call(bf16[2,160,1024]{2,1,0:T(8,128)(2,1)S(1)} %add_convert_fusion.2.refs_0_, bf16[2,160,1024]{2,1,0:T(8,128)(2,1)S(1)} %collective-permute-done.28.refs_1_, bf16[2,112,1024]{2,1,0:T(8,128)(2,1)S(1)} %add_convert_fusion.4.refs_2_, ...), custom_call_target="tpu_custom_call", output_to_operand_aliasing={{0}: (3, {})} | custom-call | flops 1000 | bytes 1000 | tf_op jit(solution)/shard_map/place1/pallas_call | solution.py:51
  105.5 1.4 %place2.1 = (bf16[4,448,1024]{2,1,0:T(8,128)(2,1)}, f32[8,128]{1,0:T(8,128)}) custom-call(bf16[2,112,1024]{2,1,0:T(8,128)(2,1)S(1)} %collective-permute-done.26.refs_0_, bf16[4,448,1024]{2,1,0:T(8,128)(2,1)} %get-tuple-element.73.refs_1_), custom_call_target="tpu_custom_call", output_to_operand_aliasing={{0}: (1, {})} | custom-call | flops 1000 | bytes 1000 | tf_op jit(solution)/shard_map/place2/pallas_call | solution.py:51
  (33 shorter events, 0.2 us)
Async XLA Ops:
  0.0 15.3 %collective-permute-start.1 = (bf16[256,1024]{1,0:T(8,128)(2,1)}, bf16[256,1024]{1,0:T(8,128)(2,1)S(1)}, u32[]{:S(2)}, u32[]{:S(2)}) collective-permute-start(bf16[256,1024]{1,0:T(8,128)(2,1)} %bitcast.19), channel_id=1, source_target_pairs={{0,2},{1,3},{2,4},{3,5},{4,6},{5,7},{6,0},{7,1},{8,10},{9,11},{10,... | collective-permute-start | bytes 1572872 | tf_op jit(solution)/shard_map/mine/ppermute | solution.py:304
  2.1 13.1 %collective-permute-start.3 = (bf16[256,1024]{1,0:T(8,128)(2,1)}, bf16[256,1024]{1,0:T(8,128)(2,1)S(1)}, u32[]{:S(2)}, u32[]{:S(2)}) collective-permute-start(bf16[256,1024]{1,0:T(8,128)(2,1)} %bitcast.20), channel_id=1, source_target_pairs={{0,6},{1,7},{2,0},{3,1},{4,2},{5,3},{6,4},{7,5},{8,14},{9,15},{10,... | collective-permute-start | bytes 1572872 | tf_op jit(solution)/shard_map/mine/ppermute | solution.py:304
  3.6 12.8 %collective-permute-start = (bf16[256,1024]{1,0:T(8,128)(2,1)}, bf16[256,1024]{1,0:T(8,128)(2,1)S(1)}, u32[]{:S(2)}, u32[]{:S(2)}) collective-permute-start(bf16[256,1024]{1,0:T(8,128)(2,1)} %bitcast.21), channel_id=1, source_target_pairs={{0,1},{1,0},{2,3},{3,2},{4,5},{5,4},{6,7},{7,6},{8,9},{9,8},{10,11... | collective-permute-start | bytes 1572872 | tf_op jit(solution)/shard_map/pair/ppermute | solution.py:310
  6.8 18.5 %collective-permute-start.7 = (bf16[704,512]{1,0:T(8,128)(2,1)S(1)}, bf16[704,512]{1,0:T(8,128)(2,1)S(1)}, u32[]{:S(2)}, u32[]{:S(2)}) collective-permute-start(bf16[704,512]{1,0:T(8,128)(2,1)S(1)} %activate0.1.refs_2_.refs_1_), channel_id=1, source_target_pairs={{0,24},{8,0},{16,8},{24,16},{1,25},{9,1},{17,9},{25,17},{2,26},{10... | collective-permute-start | bytes 2162696 | tf_op jit(solution)/shard_map/ring0/ppermute | solution.py:304
  10.6 17.1 %collective-permute-start.6 = (bf16[704,512]{1,0:T(8,128)(2,1)S(1)}, bf16[704,512]{1,0:T(8,128)(2,1)S(1)}, u32[]{:S(2)}, u32[]{:S(2)}) collective-permute-start(bf16[704,512]{1,0:T(8,128)(2,1)S(1)} %activate0.1.refs_2_.refs_1_), channel_id=1, source_target_pairs={{0,8},{8,16},{16,24},{24,0},{1,9},{9,17},{17,25},{25,1},{2,10},{10... | collective-permute-start | bytes 2162696 | tf_op jit(solution)/shard_map/ring0/ppermute | solution.py:304
  15.3 14.0 %collective-permute-start.5 = (bf16[256,1024]{1,0:T(8,128)(2,1)S(1)}, bf16[256,1024]{1,0:T(8,128)(2,1)S(1)}, u32[]{:S(2)}, u32[]{:S(2)}) collective-permute-start(bf16[256,1024]{1,0:T(8,128)(2,1)S(1)} %collective-permute-done.1.refs_4_.refs_2_), channel_id=1, source_target_pairs={{0,2},{1,3},{2,4},{3,5},{4,6},{5,7},{6,0},{7,1},{8,10},{9,11},{10,... | collective-permute-start | bytes 1572872 | tf_op jit(solution)/shard_map/far/ppermute | solution.py:304
  15.3 14.0 %collective-permute-start.2 = (bf16[256,1024]{1,0:T(8,128)(2,1)S(1)}, bf16[256,1024]{1,0:T(8,128)(2,1)S(1)}, u32[]{:S(2)}, u32[]{:S(2)}) collective-permute-start(bf16[256,1024]{1,0:T(8,128)(2,1)S(1)} %collective-permute-done.1.refs_4_.refs_2_), channel_id=1, source_target_pairs={{0,1},{1,0},{2,3},{3,2},{4,5},{5,4},{6,7},{7,6},{8,9},{9,8},{10,11... | collective-permute-start | bytes 1572872 | tf_op jit(solution)/shard_map/cross/ppermute | solution.py:310
  16.4 12.9 %collective-permute-start.4 = (bf16[256,1024]{1,0:T(8,128)(2,1)S(1)}, bf16[256,1024]{1,0:T(8,128)(2,1)S(1)}, u32[]{:S(2)}, u32[]{:S(2)}) collective-permute-start(bf16[256,1024]{1,0:T(8,128)(2,1)S(1)} %collective-permute-done.refs_3_.refs_1_), channel_id=1, source_target_pairs={{0,6},{1,7},{2,0},{3,1},{4,2},{5,3},{6,4},{7,5},{8,14},{9,15},{10,... | collective-permute-start | bytes 1572872 | tf_op jit(solution)/shard_map/down/ppermute | solution.py:304
  27.8 11.0 %collective-permute-start.11 = (bf16[352,512]{1,0:T(8,128)(2,1)S(1)}, bf16[352,512]{1,0:T(8,128)(2,1)S(1)}, u32[]{:S(2)}, u32[]{:S(2)}) collective-permute-start(bf16[352,512]{1,0:T(8,128)(2,1)S(1)} %get-tuple-element.47), channel_id=1, source_target_pairs={{0,24},{8,0},{16,8},{24,16},{1,25},{9,1},{17,9},{25,17},{2,26},{10... | collective-permute-start | bytes 1081352 | tf_op jit(solution)/shard_map/on0/ppermute | solution.py:304
  29.2 9.3 %copy-start = (bf16[1,256,1024]{2,1,0:T(8,128)(2,1)S(1)}, bf16[1,256,1024]{2,1,0:T(8,128)(2,1)}, u32[]{:S(2)}) copy-start(bf16[1,256,1024]{2,1,0:T(8,128)(2,1)} %param.10) | copy-start | bytes 1572868
  29.2 9.7 %collective-permute-start.10 = (bf16[352,512]{1,0:T(8,128)(2,1)S(1)}, bf16[352,512]{1,0:T(8,128)(2,1)S(1)}, u32[]{:S(2)}, u32[]{:S(2)}) collective-permute-start(bf16[352,512]{1,0:T(8,128)(2,1)S(1)} %get-tuple-element.43.refs_2_), channel_id=1, source_target_pairs={{0,8},{8,16},{16,24},{24,0},{1,9},{9,17},{17,25},{25,1},{2,10},{10... | collective-permute-start | bytes 1081352 | tf_op jit(solution)/shard_map/on0/ppermute | solution.py:304
  29.4 6.2 %collective-permute-start.9 = (bf16[128,1024]{1,0:T(8,128)(2,1)S(1)}, bf16[128,1024]{1,0:T(8,128)(2,1)S(1)}, u32[]{:S(2)}, u32[]{:S(2)}) collective-permute-start(bf16[128,1024]{1,0:T(8,128)(2,1)S(1)} %get-tuple-element.45), channel_id=1, source_target_pairs={{0,6},{1,7},{2,0},{3,1},{4,2},{5,3},{6,4},{7,5},{8,14},{9,15},{10,... | collective-permute-start | bytes 786440 | tf_op jit(solution)/shard_map/last/ppermute | solution.py:304
  31.8 6.7 %collective-permute-start.8 = (bf16[128,1024]{1,0:T(8,128)(2,1)S(1)}, bf16[128,1024]{1,0:T(8,128)(2,1)S(1)}, u32[]{:S(2)}, u32[]{:S(2)}) collective-permute-start(bf16[128,1024]{1,0:T(8,128)(2,1)S(1)} %get-tuple-element.44.refs_1_), channel_id=1, source_target_pairs={{0,2},{1,3},{2,4},{3,5},{4,6},{5,7},{6,0},{7,1},{8,10},{9,11},{10,... | collective-permute-start | bytes 786440 | tf_op jit(solution)/shard_map/last/ppermute | solution.py:304
  31.8 17.3 %collective-permute-start.13 = (bf16[640,512]{1,0:T(8,128)(2,1)S(1)}, bf16[640,512]{1,0:T(8,128)(2,1)S(1)}, u32[]{:S(2)}, u32[]{:S(2)}) collective-permute-start(bf16[640,512]{1,0:T(8,128)(2,1)S(1)} %gap_ring1.1.refs_1_), channel_id=1, source_target_pairs={{0,24},{8,0},{16,8},{24,16},{1,25},{9,1},{17,9},{25,17},{2,26},{10... | collective-permute-start | bytes 1966088 | tf_op jit(solution)/shard_map/ring1/ppermute | solution.py:304
  35.5 16.0 %collective-permute-start.12 = (bf16[640,512]{1,0:T(8,128)(2,1)S(1)}, bf16[640,512]{1,0:T(8,128)(2,1)S(1)}, u32[]{:S(2)}, u32[]{:S(2)}) collective-permute-start(bf16[640,512]{1,0:T(8,128)(2,1)S(1)} %gap_ring1.1.refs_1_), channel_id=1, source_target_pairs={{0,8},{8,16},{16,24},{24,0},{1,9},{9,17},{17,25},{25,1},{2,10},{10... | collective-permute-start | bytes 1966088 | tf_op jit(solution)/shard_map/ring1/ppermute | solution.py:304
  43.6 7.9 %collective-permute-start.14 = (f16[2,176,1024]{2,1,0:T(8,128)(2,1)S(1)}, f16[2,176,1024]{2,1,0:T(8,128)(2,1)S(1)}, u32[]{:S(2)}, u32[]{:S(2)}) collective-permute-start(f16[2,176,1024]{2,1,0:T(8,128)(2,1)S(1)} %convert_element_type.64), channel_id=1, source_target_pairs={{0,32},{32,0},{64,96},{96,64},{1,33},{33,1},{65,97},{97,65},{2,34}... | collective-permute-start | bytes 2162696 | tf_op jit(solution)/shard_map/cores0/ppermute | solution.py:310
  51.8 21.0 %collective-permute-start.19 = (f16[2,176,1024]{2,1,0:T(8,128)(2,1)S(1)}, f16[2,176,1024]{2,1,0:T(8,128)(2,1)S(1)}, u32[]{:S(2)}, u32[]{:S(2)}) collective-permute-start(f16[2,176,1024]{2,1,0:T(8,128)(2,1)S(1)} %add_convert_fusion.1), channel_id=1, source_target_pairs={{0,64},{32,96},{64,0},{96,32},{1,65},{33,97},{65,1},{97,33},{2,66}... | collective-permute-start | bytes 2162696 | tf_op jit(solution)/shard_map/chips0/ppermute | solution.py:310
  54.3 7.4 %collective-permute-start.17 = (bf16[320,512]{1,0:T(8,128)(2,1)S(1)}, bf16[320,512]{1,0:T(8,128)(2,1)S(1)}, u32[]{:S(2)}, u32[]{:S(2)}) collective-permute-start(bf16[320,512]{1,0:T(8,128)(2,1)S(1)} %get-tuple-element.53.refs_1_), channel_id=1, source_target_pairs={{0,8},{8,16},{16,24},{24,0},{1,9},{9,17},{17,25},{25,1},{2,10},{10... | collective-permute-start | bytes 983048 | tf_op jit(solution)/shard_map/on1/ppermute | solution.py:304
  54.3 6.7 %collective-permute-start.18 = (bf16[320,512]{1,0:T(8,128)(2,1)S(1)}, bf16[320,512]{1,0:T(8,128)(2,1)S(1)}, u32[]{:S(2)}, u32[]{:S(2)}) collective-permute-start(bf16[320,512]{1,0:T(8,128)(2,1)S(1)} %get-tuple-element.55), channel_id=1, source_target_pairs={{0,24},{8,0},{16,8},{24,16},{1,25},{9,1},{17,9},{25,17},{2,26},{10... | collective-permute-start | bytes 983048 | tf_op jit(solution)/shard_map/on1/ppermute | solution.py:304
  57.0 16.1 %collective-permute-start.16 = (bf16[448,512]{1,0:T(8,128)(2,1)S(1)}, bf16[448,512]{1,0:T(8,128)(2,1)S(1)}, u32[]{:S(2)}, u32[]{:S(2)}) collective-permute-start(bf16[448,512]{1,0:T(8,128)(2,1)S(1)} %gap_ring2.1.refs_4_.refs_1_), channel_id=1, source_target_pairs={{0,24},{8,0},{16,8},{24,16},{1,25},{9,1},{17,9},{25,17},{2,26},{10... | collective-permute-start | bytes 1376264 | tf_op jit(solution)/shard_map/ring2/ppermute | solution.py:304
  57.8 15.3 %collective-permute-start.15 = (bf16[448,512]{1,0:T(8,128)(2,1)S(1)}, bf16[448,512]{1,0:T(8,128)(2,1)S(1)}, u32[]{:S(2)}, u32[]{:S(2)}) collective-permute-start(bf16[448,512]{1,0:T(8,128)(2,1)S(1)} %gap_ring2.1.refs_4_.refs_1_), channel_id=1, source_target_pairs={{0,8},{8,16},{16,24},{24,0},{1,9},{9,17},{17,25},{25,1},{2,10},{10... | collective-permute-start | bytes 1376264 | tf_op jit(solution)/shard_map/ring2/ppermute | solution.py:304
  64.2 10.3 %collective-permute-start.20 = (f16[2,160,1024]{2,1,0:T(8,128)(2,1)S(1)}, f16[2,160,1024]{2,1,0:T(8,128)(2,1)S(1)}, u32[]{:S(2)}, u32[]{:S(2)}) collective-permute-start(f16[2,160,1024]{2,1,0:T(8,128)(2,1)S(1)} %convert_element_type.72), channel_id=1, source_target_pairs={{0,32},{32,0},{64,96},{96,64},{1,33},{33,1},{65,97},{97,65},{2,34}... | collective-permute-start | bytes 1966088 | tf_op jit(solution)/shard_map/cores1/ppermute | solution.py:310
  73.2 11.0 %collective-permute-start.21 = (bf16[224,512]{1,0:T(8,128)(2,1)S(1)}, bf16[224,512]{1,0:T(8,128)(2,1)S(1)}, u32[]{:S(2)}, u32[]{:S(2)}) collective-permute-start(bf16[224,512]{1,0:T(8,128)(2,1)S(1)} %get-tuple-element.61.refs_1_), channel_id=1, source_target_pairs={{0,8},{8,16},{16,24},{24,0},{1,9},{9,17},{17,25},{25,1},{2,10},{10... | collective-permute-start | bytes 688136 | tf_op jit(solution)/shard_map/on2/ppermute | solution.py:304
  74.8 16.1 %collective-permute-start.27 = (f16[2,160,1024]{2,1,0:T(8,128)(2,1)S(1)}, f16[2,160,1024]{2,1,0:T(8,128)(2,1)S(1)}, u32[]{:S(2)}, u32[]{:S(2)}) collective-permute-start(f16[2,160,1024]{2,1,0:T(8,128)(2,1)S(1)} %add_convert_fusion.3), channel_id=1, source_target_pairs={{0,64},{32,96},{64,0},{96,32},{1,65},{33,97},{65,1},{97,33},{2,66}... | collective-permute-start | bytes 1966088 | tf_op jit(solution)/shard_map/chips1/ppermute | solution.py:310
  75.4 8.8 %collective-permute-start.22 = (bf16[224,512]{1,0:T(8,128)(2,1)S(1)}, bf16[224,512]{1,0:T(8,128)(2,1)S(1)}, u32[]{:S(2)}, u32[]{:S(2)}) collective-permute-start(bf16[224,512]{1,0:T(8,128)(2,1)S(1)} %get-tuple-element.64), channel_id=1, source_target_pairs={{0,24},{8,0},{16,8},{24,16},{1,25},{9,1},{17,9},{25,17},{2,26},{10... | collective-permute-start | bytes 688136 | tf_op jit(solution)/shard_map/on2/ppermute | solution.py:304
  80.9 5.3 %collective-permute-start.23 = (bf16[2,176,1024]{2,1,0:T(8,128)(2,1)S(1)}, bf16[2,176,1024]{2,1,0:T(8,128)(2,1)S(1)}, u32[]{:S(2)}, u32[]{:S(2)}) collective-permute-start(bf16[2,176,1024]{2,1,0:T(8,128)(2,1)S(1)} %gap3.1.refs_0_), channel_id=1, source_target_pairs={{0,32},{32,0},{64,96},{96,64},{1,33},{33,1},{65,97},{97,65},{2,34}... | collective-permute-start | bytes 2162696 | tf_op jit(solution)/shard_map/share0/ppermute | solution.py:310
  86.0 1.9 %collective-permute-start.24 = (f16[2,112,1024]{2,1,0:T(8,128)(2,1)S(1)}, f16[2,112,1024]{2,1,0:T(8,128)(2,1)S(1)}, u32[]{:S(2)}, u32[]{:S(2)}) collective-permute-start(f16[2,112,1024]{2,1,0:T(8,128)(2,1)S(1)} %convert_element_type.77), channel_id=1, source_target_pairs={{0,32},{32,0},{64,96},{96,64},{1,33},{33,1},{65,97},{97,65},{2,34}... | collective-permute-start | bytes 1376264 | tf_op jit(solution)/shard_map/cores2/ppermute | solution.py:310
  88.1 14.2 %collective-permute-start.25 = (f16[2,112,1024]{2,1,0:T(8,128)(2,1)S(1)}, f16[2,112,1024]{2,1,0:T(8,128)(2,1)S(1)}, u32[]{:S(2)}, u32[]{:S(2)}) collective-permute-start(f16[2,112,1024]{2,1,0:T(8,128)(2,1)S(1)} %add_convert_fusion.5), channel_id=1, source_target_pairs={{0,64},{32,96},{64,0},{96,32},{1,65},{33,97},{65,1},{97,33},{2,66}... | collective-permute-start | bytes 1376264 | tf_op jit(solution)/shard_map/chips2/ppermute | solution.py:310
  91.2 12.4 %collective-permute-start.28 = (bf16[2,160,1024]{2,1,0:T(8,128)(2,1)S(1)}, bf16[2,160,1024]{2,1,0:T(8,128)(2,1)S(1)}, u32[]{:S(2)}, u32[]{:S(2)}) collective-permute-start(bf16[2,160,1024]{2,1,0:T(8,128)(2,1)S(1)} %add_convert_fusion.2.refs_0_), channel_id=1, source_target_pairs={{0,32},{32,0},{64,96},{96,64},{1,33},{33,1},{65,97},{97,65},{2,34}... | collective-permute-start | bytes 1966088 | tf_op jit(solution)/shard_map/share1/ppermute | solution.py:310
  102.4 3.0 %collective-permute-start.26 = (bf16[2,112,1024]{2,1,0:T(8,128)(2,1)S(1)}, bf16[2,112,1024]{2,1,0:T(8,128)(2,1)S(1)}, u32[]{:S(2)}, u32[]{:S(2)}) collective-permute-start(bf16[2,112,1024]{2,1,0:T(8,128)(2,1)S(1)} %add_convert_fusion.4.refs_2_), channel_id=1, source_target_pairs={{0,32},{32,0},{64,96},{96,64},{1,33},{33,1},{65,97},{97,65},{2,34}... | collective-permute-start | bytes 1376264 | tf_op jit(solution)/shard_map/share2/ppermute | solution.py:310

commit v5 on v4

--- a/solution.py
+++ b/solution.py
@@ -67,25 +67,33 @@
     spans = [(start // 128 * 128, -(-(start + size) // 128) * 128) for start in starts]
     width = max(high - low for low, high in spans)
 
+    part = TOKENS // 2
+
     def kernel(gate_ref, up_ref, *refs):
         outs, (gates, ups, sems) = refs[:-3], refs[-3:]
-        copies = []
+        steps = []
         for g, (low, high) in enumerate(spans):
-            for s, (src, dst) in enumerate(((gate_ref, gates), (up_ref, ups))):
-                copies.append(
-                    pltpu.make_async_copy(src.at[:, low:high], dst.at[g, :, : high - low], sems.at[g, s])
-                )
-        for copy in copies:
-            copy.start()
-        for g, (low, high) in enumerate(spans):
-            copies[2 * g].wait()
-            copies[2 * g + 1].wait()
-            gate = gates[g, :, : high - low].astype(jnp.float32)
-            up = ups[g, :, : high - low].astype(jnp.float32)
+            for t in range(2):
+                rows = pl.ds(t * part, part)
+                pair = [
+                    pltpu.make_async_copy(src.at[rows, low:high], dst.at[g, rows, : high - low], sems.at[g, t, s])
+                    for s, (src, dst) in enumerate(((gate_ref, gates), (up_ref, ups)))
+                ]
+                steps.append((g, t, pair))
+        for _, _, pair in steps:
+            for copy in pair:
+                copy.start()
+        for g, t, pair in steps:
+            for copy in pair:
+                copy.wait()
+            low, high = spans[g]
+            rows = slice(t * part, (t + 1) * part)
+            gate = gates[g, rows, : high - low].astype(jnp.float32)
+            up = ups[g, rows, : high - low].astype(jnp.float32)
             turned = (gate / (1.0 + jnp.exp(-gate)) * up).astype(jnp.bfloat16).T
             skip = starts[g] - low
             for k, out in zip(chunks, outs):
-                out[g * SIZES[k] : (g + 1) * SIZES[k], :] = turned[skip : skip + SIZES[k], :]
+                out[g * SIZES[k] : (g + 1) * SIZES[k], rows] = turned[skip : skip + SIZES[k], :]
                 skip += SIZES[k]
 
     block = VMEM((OWNERS, TOKENS, width), jnp.bfloat16)
@@ -94,7 +102,7 @@
         [VMEM((OWNERS * SIZES[k], TOKENS), jnp.bfloat16) for k in chunks],
         [gate, up],
         [HBM, HBM],
-        [block, block, pltpu.SemaphoreType.DMA((OWNERS, 2))],
+        [block, block, pltpu.SemaphoreType.DMA((OWNERS, 2, 2))],
         16 * MIB,
         f"activate{chunks[0]}",
         after,

time: 107 us -> 107 us (level)
  transfers between devices with their start and end apart: 29 -> 29, of which waited for: 11 -> 11; matrix products, arithmetic and copies ran while one was open for 1% -> 1% of each run, Pallas kernels for 27% -> 28%
where the time goes in v5:
time: 107 us
  starting transfers between devices  52.9 us (49%)
  Pallas kernels  31.2 us (29%)
  waiting for transfers between devices  20.7 us (19%)
  other arithmetic  1.66 us (2%)
    pallas_call x26, Pallas kernels, call(): pl.pallas_call(body, in_specs=[pl.BlockSpec(memory_space=s) for s in spac...  31.2 us
    ppermute x11, starting transfers between devices, local(): lax.ppermute(x, axis, [(i, i ^ bit) for i in range(n)])  27.1 us
    ppermute x18, starting transfers between devices, shift(): return lax.ppermute(x, axis, [(i, (i + step) % n) for i in range(n)])  25.8 us
    ppermute x18, waiting for transfers between devices, shift(): return lax.ppermute(x, axis, [(i, (i + step) % n) for i in range(n)])  10.8 us
    ppermute x11, waiting for transfers between devices, local(): lax.ppermute(x, axis, [(i, i ^ bit) for i in range(n)])  9.87 us
  transfers between devices with their start and end apart: 29, of which 11 were waited for; matrix products, arithmetic and copies ran while one was open for 1% of the time, Pallas kernels for 28%

profile of v5, /device:TPU:1, one launch (start us, length us, event | category | flops | bytes accessed | tf_op | source)
XLA Modules:
  0.0 107.0 jit_solution(14131937532315829371)
XLA Ops:
  0.0 2.1 %collective-permute-start.1 = (bf16[256,1024]{1,0:T(8,128)(2,1)}, bf16[256,1024]{1,0:T(8,128)(2,1)S(1)}, u32[]{:S(2)}, u32[]{:S(2)}) collective-permute-start(bf16[256,1024]{1,0:T(8,128)(2,1)} %bitcast.19), channel_id=1, source_target_pairs={{0,2},{1,3},{2,4},{3,5},{4,6},{5,7},{6,0},{7,1},{8,10},{9,11},{10,... | collective-permute-start | bytes 1572872 | tf_op jit(solution)/shard_map/mine/ppermute | solution.py:312
  2.1 1.4 %collective-permute-start.3 = (bf16[256,1024]{1,0:T(8,128)(2,1)}, bf16[256,1024]{1,0:T(8,128)(2,1)S(1)}, u32[]{:S(2)}, u32[]{:S(2)}) collective-permute-start(bf16[256,1024]{1,0:T(8,128)(2,1)} %bitcast.20), channel_id=1, source_target_pairs={{0,6},{1,7},{2,0},{3,1},{4,2},{5,3},{6,4},{7,5},{8,14},{9,15},{10,... | collective-permute-start | bytes 1572872 | tf_op jit(solution)/shard_map/mine/ppermute | solution.py:312
  3.6 1.2 %collective-permute-start = (bf16[256,1024]{1,0:T(8,128)(2,1)}, bf16[256,1024]{1,0:T(8,128)(2,1)S(1)}, u32[]{:S(2)}, u32[]{:S(2)}) collective-permute-start(bf16[256,1024]{1,0:T(8,128)(2,1)} %bitcast.21), channel_id=1, source_target_pairs={{0,1},{1,0},{2,3},{3,2},{4,5},{5,4},{6,7},{7,6},{8,9},{9,8},{10,11... | collective-permute-start | bytes 1572872 | tf_op jit(solution)/shard_map/pair/ppermute | solution.py:318
  4.8 2.3 %activate0.1.refs_2_.refs_1_ = bf16[704,512]{1,0:T(8,128)(2,1)S(1)} custom-call(bf16[512,1792]{1,0:T(8,128)(2,1)} %bitcast.38, bf16[512,1792]{1,0:T(8,128)(2,1)} %bitcast.40), custom_call_target="tpu_custom_call" | custom-call | flops 1000 | bytes 1000 | tf_op jit(solution)/shard_map/activate0/pallas_call | solution.py:51
  7.1 3.8 %collective-permute-start.7 = (bf16[704,512]{1,0:T(8,128)(2,1)S(1)}, bf16[704,512]{1,0:T(8,128)(2,1)S(1)}, u32[]{:S(2)}, u32[]{:S(2)}) collective-permute-start(bf16[704,512]{1,0:T(8,128)(2,1)S(1)} %activate0.1.refs_2_.refs_1_), channel_id=1, source_target_pairs={{0,24},{8,0},{16,8},{24,16},{1,25},{9,1},{17,9},{25,17},{2,26},{10... | collective-permute-start | bytes 2162696 | tf_op jit(solution)/shard_map/ring0/ppermute | solution.py:312
  10.9 0.0 collective-permute-start.6
  11.0 2.7 %activate1.1 = (bf16[640,512]{1,0:T(8,128)(2,1)S(1)}, bf16[448,512]{1,0:T(8,128)(2,1)S(1)}) custom-call(bf16[512,1792]{1,0:T(8,128)(2,1)} %bitcast.39, bf16[512,1792]{1,0:T(8,128)(2,1)} %bitcast.41, bf16[704,512]{1,0:T(8,128)(2,1)S(1)} %activate0.1.refs_2_.refs_1_), custom_call_target="tpu_custom_call" | custom-call | flops 1000 | bytes 1000 | tf_op jit(solution)/shard_map/activate1/pallas_call | solution.py:51
  13.6 1.6 %collective-permute-done.1.refs_4_.refs_2_ = bf16[256,1024]{1,0:T(8,128)(2,1)S(1)} collective-permute-done((bf16[256,1024]{1,0:T(8,128)(2,1)}, bf16[256,1024]{1,0:T(8,128)(2,1)S(1)}, u32[]{:S(2)}, u32[]{:S(2)}) %collective-permute-start.1) | collective-permute-done | bytes 524320 | tf_op jit(solution)/shard_map/mine/ppermute | solution.py:312
  15.3 0.0 collective-permute-start.5
  15.3 0.0 collective-permute-done.3.refs_5_.refs_4_
  15.3 1.1 %collective-permute-start.2 = (bf16[256,1024]{1,0:T(8,128)(2,1)S(1)}, bf16[256,1024]{1,0:T(8,128)(2,1)S(1)}, u32[]{:S(2)}, u32[]{:S(2)}) collective-permute-start(bf16[256,1024]{1,0:T(8,128)(2,1)S(1)} %collective-permute-done.1.refs_4_.refs_2_), channel_id=1, source_target_pairs={{0,1},{1,0},{2,3},{3,2},{4,5},{5,4},{6,7},{7,6},{8,9},{9,8},{10,11... | collective-permute-start | bytes 1572872 | tf_op jit(solution)/shard_map/cross/ppermute | solution.py:318
  16.4 2.7 %collective-permute-start.4 = (bf16[256,1024]{1,0:T(8,128)(2,1)S(1)}, bf16[256,1024]{1,0:T(8,128)(2,1)S(1)}, u32[]{:S(2)}, u32[]{:S(2)}) collective-permute-start(bf16[256,1024]{1,0:T(8,128)(2,1)S(1)} %collective-permute-done.refs_3_.refs_1_), channel_id=1, source_target_pairs={{0,6},{1,7},{2,0},{3,1},{4,2},{5,3},{6,4},{7,5},{8,14},{9,15},{10,... | collective-permute-start | bytes 1572872 | tf_op jit(solution)/shard_map/down/ppermute | solution.py:312
  19.1 3.2 %load0.1 = (bf16[4,176,1024]{2,1,0:T(8,128)(2,1)S(1)}, bf16[4,176,1024]{2,1,0:T(8,128)(2,1)S(1)}, f32[4,176,1024]{2,1,0:T(8,128)S(1)}, f32[176,1024]{1,0:T(8,128)S(1)}, f32[176,1024]{1,0:T(8,128)S(1)}) custom-call(bf16[1792,1024]{1,0:T(8,128)(2,1)} %bitcast.26, bf16[1792,1024]{1,0:T(8,128)(2,1)} %bitcast.29, f32[1792,1024]{1,0:T(8,128)} %bitcast.23, ...), custom_call_target="tpu_custom_call" | custom-call | flops 8000001024 | bytes 1000 | tf_op jit(solution)/shard_map/load0/pallas_call | solution.py:51
  22.2 3.0 %load1.1 = (bf16[4,160,1024]{2,1,0:T(8,128)(2,1)S(1)}, bf16[4,160,1024]{2,1,0:T(8,128)(2,1)S(1)}, f32[4,160,1024]{2,1,0:T(8,128)S(1)}, f32[160,1024]{1,0:T(8,128)S(1)}, f32[160,1024]{1,0:T(8,128)S(1)}) custom-call(bf16[1792,1024]{1,0:T(8,128)(2,1)} %bitcast.27, bf16[1792,1024]{1,0:T(8,128)(2,1)} %bitcast.30, f32[1792,1024]{1,0:T(8,128)} %bitcast.24, ...), custom_call_target="tpu_custom_call" | custom-call | flops 1000 | bytes 1000 | tf_op jit(solution)/shard_map/load1/pallas_call | solution.py:51
  25.2 0.0 collective-permute-done.7.refs_1_.refs_3_
  25.3 2.8 %collective-permute-done.6.refs_0_.refs_2_ = bf16[704,512]{1,0:T(8,128)(2,1)S(1)} collective-permute-done((bf16[704,512]{1,0:T(8,128)(2,1)S(1)}, bf16[704,512]{1,0:T(8,128)(2,1)S(1)}, u32[]{:S(2)}, u32[]{:S(2)}) %collective-permute-start.6) | collective-permute-done | bytes 720928 | tf_op jit(solution)/shard_map/ring0/ppermute | solution.py:312
  28.1 1.1 collective-permute-start.11
  29.2 0.5 collective-permute-start.10
  29.6 0.0 collective-permute-done.5.refs_3_.refs_6_
  29.7 2.1 %collective-permute-start.9 = (bf16[128,1024]{1,0:T(8,128)(2,1)S(1)}, bf16[128,1024]{1,0:T(8,128)(2,1)S(1)}, u32[]{:S(2)}, u32[]{:S(2)}) collective-permute-start(bf16[128,1024]{1,0:T(8,128)(2,1)S(1)} %get-tuple-element.45), channel_id=1, source_target_pairs={{0,6},{1,7},{2,0},{3,1},{4,2},{5,3},{6,4},{7,5},{8,14},{9,15},{10,... | collective-permute-start | bytes 786440 | tf_op jit(solution)/shard_map/last/ppermute | solution.py:312
  31.8 3.8 %collective-permute-start.13 = (bf16[640,512]{1,0:T(8,128)(2,1)S(1)}, bf16[640,512]{1,0:T(8,128)(2,1)S(1)}, u32[]{:S(2)}, u32[]{:S(2)}) collective-permute-start(bf16[640,512]{1,0:T(8,128)(2,1)S(1)} %gap_ring1.1.refs_1_), channel_id=1, source_target_pairs={{0,24},{8,0},{16,8},{24,16},{1,25},{9,1},{17,9},{25,17},{2,26},{10... | collective-permute-start | bytes 1966088 | tf_op jit(solution)/shard_map/ring1/ppermute | solution.py:312
  35.5 1.2 %collective-permute-start.12 = (bf16[640,512]{1,0:T(8,128)(2,1)S(1)}, bf16[640,512]{1,0:T(8,128)(2,1)S(1)}, u32[]{:S(2)}, u32[]{:S(2)}) collective-permute-start(bf16[640,512]{1,0:T(8,128)(2,1)S(1)} %gap_ring1.1.refs_1_), channel_id=1, source_target_pairs={{0,8},{8,16},{16,24},{24,0},{1,9},{9,17},{17,25},{25,1},{2,10},{10... | collective-permute-start | bytes 1966088 | tf_op jit(solution)/shard_map/ring1/ppermute | solution.py:312
  36.7 1.8 %collective-permute-done.8.refs_7_ = bf16[128,1024]{1,0:T(8,128)(2,1)S(1)} collective-permute-done((bf16[128,1024]{1,0:T(8,128)(2,1)S(1)}, bf16[128,1024]{1,0:T(8,128)(2,1)S(1)}, u32[]{:S(2)}, u32[]{:S(2)}) %collective-permute-start.8) | collective-permute-done | bytes 262176 | tf_op jit(solution)/shard_map/last/ppermute | solution.py:312
  38.5 0.3 assemble.1.refs_0_
  38.8 4.9 %inner0.1 = (f32[2,176,1024]{2,1,0:T(8,128)S(1)}, f32[2,176,1024]{2,1,0:T(8,128)S(1)}) custom-call(bf16[2048,1024]{1,0:T(8,128)(2,1)S(1)} %assemble.1.refs_0_, bf16[704,512]{1,0:T(8,128)(2,1)S(1)} %activate0.1.refs_2_.refs_1_, bf16[704,512]{1,0:T(8,128)(2,1)S(1)} %collective-permute-done.6.refs_0_.refs_2_, ...), custom_call_target="tpu_custom_call" | custom-call | flops 1000 | bytes 1000 | tf_op jit(solution)/shard_map/inner0/pallas_call | solution.py:51
  43.7 0.1 convert_element_type.64
  43.8 4.2 %collective-permute-start.14 = (f16[2,176,1024]{2,1,0:T(8,128)(2,1)S(1)}, f16[2,176,1024]{2,1,0:T(8,128)(2,1)S(1)}, u32[]{:S(2)}, u32[]{:S(2)}) collective-permute-start(f16[2,176,1024]{2,1,0:T(8,128)(2,1)S(1)} %convert_element_type.64), channel_id=1, source_target_pairs={{0,32},{32,0},{64,96},{96,64},{1,33},{33,1},{65,97},{97,65},{2,34}... | collective-permute-start | bytes 2162696 | tf_op jit(solution)/shard_map/cores0/ppermute | solution.py:318
  48.0 1.5 %collective-permute-done.13.refs_1_.refs_3_ = bf16[640,512]{1,0:T(8,128)(2,1)S(1)} collective-permute-done((bf16[640,512]{1,0:T(8,128)(2,1)S(1)}, bf16[640,512]{1,0:T(8,128)(2,1)S(1)}, u32[]{:S(2)}, u32[]{:S(2)}) %collective-permute-start.13) | collective-permute-done | bytes 655392 | tf_op jit(solution)/shard_map/ring1/ppermute | solution.py:312
  49.5 2.0 %collective-permute-done.12.refs_0_.refs_2_ = bf16[640,512]{1,0:T(8,128)(2,1)S(1)} collective-permute-done((bf16[640,512]{1,0:T(8,128)(2,1)S(1)}, bf16[640,512]{1,0:T(8,128)(2,1)S(1)}, u32[]{:S(2)}, u32[]{:S(2)}) %collective-permute-start.12) | collective-permute-done | bytes 655392 | tf_op jit(solution)/shard_map/ring1/ppermute | solution.py:312
  51.6 0.2 add_convert_fusion.1
  51.8 2.5 %collective-permute-start.19 = (f16[2,176,1024]{2,1,0:T(8,128)(2,1)S(1)}, f16[2,176,1024]{2,1,0:T(8,128)(2,1)S(1)}, u32[]{:S(2)}, u32[]{:S(2)}) collective-permute-start(f16[2,176,1024]{2,1,0:T(8,128)(2,1)S(1)} %add_convert_fusion.1), channel_id=1, source_target_pairs={{0,64},{32,96},{64,0},{96,32},{1,65},{33,97},{65,1},{97,33},{2,66}... | collective-permute-start | bytes 2162696 | tf_op jit(solution)/shard_map/chips0/ppermute | solution.py:318
  54.3 2.7 %collective-permute-start.18 = (bf16[320,512]{1,0:T(8,128)(2,1)S(1)}, bf16[320,512]{1,0:T(8,128)(2,1)S(1)}, u32[]{:S(2)}, u32[]{:S(2)}) collective-permute-start(bf16[320,512]{1,0:T(8,128)(2,1)S(1)} %get-tuple-element.55), channel_id=1, source_target_pairs={{0,24},{8,0},{16,8},{24,16},{1,25},{9,1},{17,9},{25,17},{2,26},{10... | collective-permute-start | bytes 983048 | tf_op jit(solution)/shard_map/on1/ppermute | solution.py:312
  57.0 0.8 collective-permute-start.16
  57.8 0.7 collective-permute-start.15
  58.5 2.2 %near1.1.refs_0_.refs_1_ = f32[640,1024]{1,0:T(8,128)S(1)} custom-call(bf16[2048,1024]{1,0:T(8,128)(2,1)S(1)} %assemble.1.refs_0_, bf16[640,512]{1,0:T(8,128)(2,1)S(1)} %gap_ring1.1.refs_1_, bf16[640,512]{1,0:T(8,128)(2,1)S(1)} %collective-permute-done.12.refs_0_.refs_2_, bf16[640,512]{1,0:T(8,128)(2,1)S(1)} %collective-permute-done.13.refs_1_.refs_3_, ...), custom_call_target="tpu_custom_call" | custom-call | flops 1000 | bytes 1000 | tf_op jit(solution)/shard_map/near1/pallas_call | solution.py:51
  60.7 0.3 collective-permute-done.18.refs_1_.refs_3_
  61.0 0.7 collective-permute-done.17.refs_0_.refs_2_
  61.8 2.4 %inner1.1 = (f32[2,160,1024]{2,1,0:T(8,128)S(1)}, f32[2,160,1024]{2,1,0:T(8,128)S(1)}) custom-call(bf16[2048,1024]{1,0:T(8,128)(2,1)S(1)} %assemble.1.refs_0_, f32[640,1024]{1,0:T(8,128)S(1)} %near1.1.refs_0_.refs_1_, bf16[320,512]{1,0:T(8,128)(2,1)S(1)} %collective-permute-done.17.refs_0_.refs_2_, ...), custom_call_target="tpu_custom_call" | custom-call | flops 1000 | bytes 1000 | tf_op jit(solution)/shard_map/inner1/pallas_call | solution.py:51
  64.1 0.1 convert_element_type.72
  64.2 8.5 %collective-permute-start.20 = (f16[2,160,1024]{2,1,0:T(8,128)(2,1)S(1)}, f16[2,160,1024]{2,1,0:T(8,128)(2,1)S(1)}, u32[]{:S(2)}, u32[]{:S(2)}) collective-permute-start(f16[2,160,1024]{2,1,0:T(8,128)(2,1)S(1)} %convert_element_type.72), channel_id=1, source_target_pairs={{0,32},{32,0},{64,96},{96,64},{1,33},{33,1},{65,97},{97,65},{2,34}... | collective-permute-start | bytes 1966088 | tf_op jit(solution)/shard_map/cores1/ppermute | solution.py:318
  72.8 0.3 add_convert_fusion.refs_3_.refs_0_
  73.2 0.1 collective-permute-start.21
  73.3 1.2 %collective-permute-done.20 = f16[2,160,1024]{2,1,0:T(8,128)(2,1)S(1)} collective-permute-done((f16[2,160,1024]{2,1,0:T(8,128)(2,1)S(1)}, f16[2,160,1024]{2,1,0:T(8,128)(2,1)S(1)}, u32[]{:S(2)}, u32[]{:S(2)}) %collective-permute-start.20) | collective-permute-done | bytes 655392 | tf_op jit(solution)/shard_map/cores1/ppermute | solution.py:318
  74.5 0.2 add_convert_fusion.3
  74.8 0.6 collective-permute-start.27
  75.4 3.0 %collective-permute-start.22 = (bf16[224,512]{1,0:T(8,128)(2,1)S(1)}, bf16[224,512]{1,0:T(8,128)(2,1)S(1)}, u32[]{:S(2)}, u32[]{:S(2)}) collective-permute-start(bf16[224,512]{1,0:T(8,128)(2,1)S(1)} %get-tuple-element.64), channel_id=1, source_target_pairs={{0,24},{8,0},{16,8},{24,16},{1,25},{9,1},{17,9},{25,17},{2,26},{10... | collective-permute-start | bytes 688136 | tf_op jit(solution)/shard_map/on2/ppermute | solution.py:312
  78.3 2.5 %load2.1 = (bf16[4,112,1024]{2,1,0:T(8,128)(2,1)S(1)}, bf16[4,112,1024]{2,1,0:T(8,128)(2,1)S(1)}, f32[4,112,1024]{2,1,0:T(8,128)S(1)}, f32[112,1024]{1,0:T(8,128)S(1)}, f32[112,1024]{1,0:T(8,128)S(1)}) custom-call(bf16[1792,1024]{1,0:T(8,128)(2,1)} %bitcast.28, bf16[1792,1024]{1,0:T(8,128)(2,1)} %bitcast.31, f32[1792,1024]{1,0:T(8,128)} %bitcast.25, ...), custom_call_target="tpu_custom_call" | custom-call | flops 4000001024 | bytes 1000 | tf_op jit(solution)/shard_map/load2/pallas_call | solution.py:51
  80.9 1.7 %collective-permute-start.23 = (bf16[2,176,1024]{2,1,0:T(8,128)(2,1)S(1)}, bf16[2,176,1024]{2,1,0:T(8,128)(2,1)S(1)}, u32[]{:S(2)}, u32[]{:S(2)}) collective-permute-start(bf16[2,176,1024]{2,1,0:T(8,128)(2,1)S(1)} %gap3.1.refs_0_), channel_id=1, source_target_pairs={{0,32},{32,0},{64,96},{96,64},{1,33},{33,1},{65,97},{97,65},{2,34}... | collective-permute-start | bytes 2162696 | tf_op jit(solution)/shard_map/share0/ppermute | solution.py:318
  82.6 1.6 %near2.1.refs_1_ = f32[448,1024]{1,0:T(8,128)S(1)} custom-call(bf16[2048,1024]{1,0:T(8,128)(2,1)S(1)} %assemble.1.refs_0_, bf16[448,512]{1,0:T(8,128)(2,1)S(1)} %gap_ring2.1.refs_4_.refs_1_, bf16[448,512]{1,0:T(8,128)(2,1)S(1)} %collective-permute-done.15.refs_0_.refs_2_, bf16[448,512]{1,0:T(8,128)(2,1)S(1)} %collective-permute-done.16.refs_1_.refs_3_, ...), custom_call_target="tpu_custom_call" | custom-call | flops 8000001024 | bytes 1000 | tf_op jit(solution)/shard_map/near2/pallas_call | solution.py:51
  84.2 1.7 %inner2.1 = (f32[2,112,1024]{2,1,0:T(8,128)S(1)}, f32[2,112,1024]{2,1,0:T(8,128)S(1)}) custom-call(bf16[2048,1024]{1,0:T(8,128)(2,1)S(1)} %assemble.1.refs_0_, f32[448,1024]{1,0:T(8,128)S(1)} %near2.1.refs_1_, bf16[224,512]{1,0:T(8,128)(2,1)S(1)} %collective-permute-done.21.refs_2_, bf16[224,512]{1,0:T(8,128)(2,1)S(1)} %collective-permute-done.22.refs_3_, ...), custom_call_target="tpu_custom_call" | custom-call | flops 1000 | bytes 1000 | tf_op jit(solution)/shard_map/inner2/pallas_call | solution.py:51
  85.9 0.1 convert_element_type.77
  86.0 0.1 collective-permute-start.24
  86.1 1.1 %place0.1 = (bf16[4,448,1024]{2,1,0:T(8,128)(2,1)}, f32[8,128]{1,0:T(8,128)S(1)}) custom-call(bf16[2,176,1024]{2,1,0:T(8,128)(2,1)S(1)} %gap3.1.refs_0_, bf16[2,176,1024]{2,1,0:T(8,128)(2,1)S(1)} %collective-permute-done.23.refs_1_), custom_call_target="tpu_custom_call" | custom-call | flops 1000 | bytes 1000 | tf_op jit(solution)/shard_map/place0/pallas_call | solution.py:51
  87.3 0.6 collective-permute-done.24
  87.9 0.1 add_convert_fusion.5
  88.1 2.5 %collective-permute-start.25 = (f16[2,112,1024]{2,1,0:T(8,128)(2,1)S(1)}, f16[2,112,1024]{2,1,0:T(8,128)(2,1)S(1)}, u32[]{:S(2)}, u32[]{:S(2)}) collective-permute-start(f16[2,112,1024]{2,1,0:T(8,128)(2,1)S(1)} %add_convert_fusion.5), channel_id=1, source_target_pairs={{0,64},{32,96},{64,0},{96,32},{1,65},{33,97},{65,1},{97,33},{2,66}... | collective-permute-start | bytes 1376264 | tf_op jit(solution)/shard_map/chips2/ppermute | solution.py:318
  90.6 0.3 collective-permute-done.27
  90.9 0.3 add_convert_fusion.2.refs_0_
  91.2 3.4 %collective-permute-start.28 = (bf16[2,160,1024]{2,1,0:T(8,128)(2,1)S(1)}, bf16[2,160,1024]{2,1,0:T(8,128)(2,1)S(1)}, u32[]{:S(2)}, u32[]{:S(2)}) collective-permute-start(bf16[2,160,1024]{2,1,0:T(8,128)(2,1)S(1)} %add_convert_fusion.2.refs_0_), channel_id=1, source_target_pairs={{0,32},{32,0},{64,96},{96,64},{1,33},{33,1},{65,97},{97,65},{2,34}... | collective-permute-start | bytes 1966088 | tf_op jit(solution)/shard_map/share1/ppermute | solution.py:318
  94.6 7.7 %collective-permute-done.25 = f16[2,112,1024]{2,1,0:T(8,128)(2,1)S(1)} collective-permute-done((f16[2,112,1024]{2,1,0:T(8,128)(2,1)S(1)}, f16[2,112,1024]{2,1,0:T(8,128)(2,1)S(1)}, u32[]{:S(2)}, u32[]{:S(2)}) %collective-permute-start.25) | collective-permute-done | bytes 458784 | tf_op jit(solution)/shard_map/chips2/ppermute | solution.py:318
  102.2 0.2 add_convert_fusion.4.refs_2_
  102.4 1.2 %collective-permute-start.26 = (bf16[2,112,1024]{2,1,0:T(8,128)(2,1)S(1)}, bf16[2,112,1024]{2,1,0:T(8,128)(2,1)S(1)}, u32[]{:S(2)}, u32[]{:S(2)}) collective-permute-start(bf16[2,112,1024]{2,1,0:T(8,128)(2,1)S(1)} %add_convert_fusion.4.refs_2_), channel_id=1, source_target_pairs={{0,32},{32,0},{64,96},{96,64},{1,33},{33,1},{65,97},{97,65},{2,34}... | collective-permute-start | bytes 1376264 | tf_op jit(solution)/shard_map/share2/ppermute | solution.py:318
  103.6 1.8 %place1.1 = (bf16[4,448,1024]{2,1,0:T(8,128)(2,1)}, f32[8,128]{1,0:T(8,128)}) custom-call(bf16[2,160,1024]{2,1,0:T(8,128)(2,1)S(1)} %add_convert_fusion.2.refs_0_, bf16[2,160,1024]{2,1,0:T(8,128)(2,1)S(1)} %collective-permute-done.28.refs_1_, bf16[2,112,1024]{2,1,0:T(8,128)(2,1)S(1)} %add_convert_fusion.4.refs_2_, ...), custom_call_target="tpu_custom_call", output_to_operand_aliasing={{0}: (3, {})} | custom-call | flops 1000 | bytes 1000 | tf_op jit(solution)/shard_map/place1/pallas_call | solution.py:51
  105.5 1.4 %place2.1 = (bf16[4,448,1024]{2,1,0:T(8,128)(2,1)}, f32[8,128]{1,0:T(8,128)}) custom-call(bf16[2,112,1024]{2,1,0:T(8,128)(2,1)S(1)} %collective-permute-done.26.refs_0_, bf16[4,448,1024]{2,1,0:T(8,128)(2,1)} %get-tuple-element.73.refs_1_), custom_call_target="tpu_custom_call", output_to_operand_aliasing={{0}: (1, {})} | custom-call | flops 1000 | bytes 1000 | tf_op jit(solution)/shard_map/place2/pallas_call | solution.py:51
  (33 shorter events, 0.2 us)
Async XLA Ops:
  0.0 15.3 %collective-permute-start.1 = (bf16[256,1024]{1,0:T(8,128)(2,1)}, bf16[256,1024]{1,0:T(8,128)(2,1)S(1)}, u32[]{:S(2)}, u32[]{:S(2)}) collective-permute-start(bf16[256,1024]{1,0:T(8,128)(2,1)} %bitcast.19), channel_id=1, source_target_pairs={{0,2},{1,3},{2,4},{3,5},{4,6},{5,7},{6,0},{7,1},{8,10},{9,11},{10,... | collective-permute-start | bytes 1572872 | tf_op jit(solution)/shard_map/mine/ppermute | solution.py:312
  2.1 13.1 %collective-permute-start.3 = (bf16[256,1024]{1,0:T(8,128)(2,1)}, bf16[256,1024]{1,0:T(8,128)(2,1)S(1)}, u32[]{:S(2)}, u32[]{:S(2)}) collective-permute-start(bf16[256,1024]{1,0:T(8,128)(2,1)} %bitcast.20), channel_id=1, source_target_pairs={{0,6},{1,7},{2,0},{3,1},{4,2},{5,3},{6,4},{7,5},{8,14},{9,15},{10,... | collective-permute-start | bytes 1572872 | tf_op jit(solution)/shard_map/mine/ppermute | solution.py:312
  3.6 12.8 %collective-permute-start = (bf16[256,1024]{1,0:T(8,128)(2,1)}, bf16[256,1024]{1,0:T(8,128)(2,1)S(1)}, u32[]{:S(2)}, u32[]{:S(2)}) collective-permute-start(bf16[256,1024]{1,0:T(8,128)(2,1)} %bitcast.21), channel_id=1, source_target_pairs={{0,1},{1,0},{2,3},{3,2},{4,5},{5,4},{6,7},{7,6},{8,9},{9,8},{10,11... | collective-permute-start | bytes 1572872 | tf_op jit(solution)/shard_map/pair/ppermute | solution.py:318
  7.1 18.1 %collective-permute-start.7 = (bf16[704,512]{1,0:T(8,128)(2,1)S(1)}, bf16[704,512]{1,0:T(8,128)(2,1)S(1)}, u32[]{:S(2)}, u32[]{:S(2)}) collective-permute-start(bf16[704,512]{1,0:T(8,128)(2,1)S(1)} %activate0.1.refs_2_.refs_1_), channel_id=1, source_target_pairs={{0,24},{8,0},{16,8},{24,16},{1,25},{9,1},{17,9},{25,17},{2,26},{10... | collective-permute-start | bytes 2162696 | tf_op jit(solution)/shard_map/ring0/ppermute | solution.py:312
  10.9 17.1 %collective-permute-start.6 = (bf16[704,512]{1,0:T(8,128)(2,1)S(1)}, bf16[704,512]{1,0:T(8,128)(2,1)S(1)}, u32[]{:S(2)}, u32[]{:S(2)}) collective-permute-start(bf16[704,512]{1,0:T(8,128)(2,1)S(1)} %activate0.1.refs_2_.refs_1_), channel_id=1, source_target_pairs={{0,8},{8,16},{16,24},{24,0},{1,9},{9,17},{17,25},{25,1},{2,10},{10... | collective-permute-start | bytes 2162696 | tf_op jit(solution)/shard_map/ring0/ppermute | solution.py:312
  15.3 14.4 %collective-permute-start.5 = (bf16[256,1024]{1,0:T(8,128)(2,1)S(1)}, bf16[256,1024]{1,0:T(8,128)(2,1)S(1)}, u32[]{:S(2)}, u32[]{:S(2)}) collective-permute-start(bf16[256,1024]{1,0:T(8,128)(2,1)S(1)} %collective-permute-done.1.refs_4_.refs_2_), channel_id=1, source_target_pairs={{0,2},{1,3},{2,4},{3,5},{4,6},{5,7},{6,0},{7,1},{8,10},{9,11},{10,... | collective-permute-start | bytes 1572872 | tf_op jit(solution)/shard_map/far/ppermute | solution.py:312
  15.3 14.4 %collective-permute-start.2 = (bf16[256,1024]{1,0:T(8,128)(2,1)S(1)}, bf16[256,1024]{1,0:T(8,128)(2,1)S(1)}, u32[]{:S(2)}, u32[]{:S(2)}) collective-permute-start(bf16[256,1024]{1,0:T(8,128)(2,1)S(1)} %collective-permute-done.1.refs_4_.refs_2_), channel_id=1, source_target_pairs={{0,1},{1,0},{2,3},{3,2},{4,5},{5,4},{6,7},{7,6},{8,9},{9,8},{10,11... | collective-permute-start | bytes 1572872 | tf_op jit(solution)/shard_map/cross/ppermute | solution.py:318
  16.4 13.3 %collective-permute-start.4 = (bf16[256,1024]{1,0:T(8,128)(2,1)S(1)}, bf16[256,1024]{1,0:T(8,128)(2,1)S(1)}, u32[]{:S(2)}, u32[]{:S(2)}) collective-permute-start(bf16[256,1024]{1,0:T(8,128)(2,1)S(1)} %collective-permute-done.refs_3_.refs_1_), channel_id=1, source_target_pairs={{0,6},{1,7},{2,0},{3,1},{4,2},{5,3},{6,4},{7,5},{8,14},{9,15},{10,... | collective-permute-start | bytes 1572872 | tf_op jit(solution)/shard_map/down/ppermute | solution.py:312
  28.1 10.7 %collective-permute-start.11 = (bf16[352,512]{1,0:T(8,128)(2,1)S(1)}, bf16[352,512]{1,0:T(8,128)(2,1)S(1)}, u32[]{:S(2)}, u32[]{:S(2)}) collective-permute-start(bf16[352,512]{1,0:T(8,128)(2,1)S(1)} %get-tuple-element.47), channel_id=1, source_target_pairs={{0,24},{8,0},{16,8},{24,16},{1,25},{9,1},{17,9},{25,17},{2,26},{10... | collective-permute-start | bytes 1081352 | tf_op jit(solution)/shard_map/on0/ppermute | solution.py:312
  29.2 9.3 %copy-start = (bf16[1,256,1024]{2,1,0:T(8,128)(2,1)S(1)}, bf16[1,256,1024]{2,1,0:T(8,128)(2,1)}, u32[]{:S(2)}) copy-start(bf16[1,256,1024]{2,1,0:T(8,128)(2,1)} %param.10) | copy-start | bytes 1572868
  29.2 9.7 %collective-permute-start.10 = (bf16[352,512]{1,0:T(8,128)(2,1)S(1)}, bf16[352,512]{1,0:T(8,128)(2,1)S(1)}, u32[]{:S(2)}, u32[]{:S(2)}) collective-permute-start(bf16[352,512]{1,0:T(8,128)(2,1)S(1)} %get-tuple-element.43.refs_2_), channel_id=1, source_target_pairs={{0,8},{8,16},{16,24},{24,0},{1,9},{9,17},{17,25},{25,1},{2,10},{10... | collective-permute-start | bytes 1081352 | tf_op jit(solution)/shard_map/on0/ppermute | solution.py:312
  29.7 5.8 %collective-permute-start.9 = (bf16[128,1024]{1,0:T(8,128)(2,1)S(1)}, bf16[128,1024]{1,0:T(8,128)(2,1)S(1)}, u32[]{:S(2)}, u32[]{:S(2)}) collective-permute-start(bf16[128,1024]{1,0:T(8,128)(2,1)S(1)} %get-tuple-element.45), channel_id=1, source_target_pairs={{0,6},{1,7},{2,0},{3,1},{4,2},{5,3},{6,4},{7,5},{8,14},{9,15},{10,... | collective-permute-start | bytes 786440 | tf_op jit(solution)/shard_map/last/ppermute | solution.py:312
  31.8 6.7 %collective-permute-start.8 = (bf16[128,1024]{1,0:T(8,128)(2,1)S(1)}, bf16[128,1024]{1,0:T(8,128)(2,1)S(1)}, u32[]{:S(2)}, u32[]{:S(2)}) collective-permute-start(bf16[128,1024]{1,0:T(8,128)(2,1)S(1)} %get-tuple-element.44.refs_1_), channel_id=1, source_target_pairs={{0,2},{1,3},{2,4},{3,5},{4,6},{5,7},{6,0},{7,1},{8,10},{9,11},{10,... | collective-permute-start | bytes 786440 | tf_op jit(solution)/shard_map/last/ppermute | solution.py:312
  31.8 17.7 %collective-permute-start.13 = (bf16[640,512]{1,0:T(8,128)(2,1)S(1)}, bf16[640,512]{1,0:T(8,128)(2,1)S(1)}, u32[]{:S(2)}, u32[]{:S(2)}) collective-permute-start(bf16[640,512]{1,0:T(8,128)(2,1)S(1)} %gap_ring1.1.refs_1_), channel_id=1, source_target_pairs={{0,24},{8,0},{16,8},{24,16},{1,25},{9,1},{17,9},{25,17},{2,26},{10... | collective-permute-start | bytes 1966088 | tf_op jit(solution)/shard_map/ring1/ppermute | solution.py:312
  35.5 16.0 %collective-permute-start.12 = (bf16[640,512]{1,0:T(8,128)(2,1)S(1)}, bf16[640,512]{1,0:T(8,128)(2,1)S(1)}, u32[]{:S(2)}, u32[]{:S(2)}) collective-permute-start(bf16[640,512]{1,0:T(8,128)(2,1)S(1)} %gap_ring1.1.refs_1_), channel_id=1, source_target_pairs={{0,8},{8,16},{16,24},{24,0},{1,9},{9,17},{17,25},{25,1},{2,10},{10... | collective-permute-start | bytes 1966088 | tf_op jit(solution)/shard_map/ring1/ppermute | solution.py:312
  43.8 7.8 %collective-permute-start.14 = (f16[2,176,1024]{2,1,0:T(8,128)(2,1)S(1)}, f16[2,176,1024]{2,1,0:T(8,128)(2,1)S(1)}, u32[]{:S(2)}, u32[]{:S(2)}) collective-permute-start(f16[2,176,1024]{2,1,0:T(8,128)(2,1)S(1)} %convert_element_type.64), channel_id=1, source_target_pairs={{0,32},{32,0},{64,96},{96,64},{1,33},{33,1},{65,97},{97,65},{2,34}... | collective-permute-start | bytes 2162696 | tf_op jit(solution)/shard_map/cores0/ppermute | solution.py:318
  51.8 21.0 %collective-permute-start.19 = (f16[2,176,1024]{2,1,0:T(8,128)(2,1)S(1)}, f16[2,176,1024]{2,1,0:T(8,128)(2,1)S(1)}, u32[]{:S(2)}, u32[]{:S(2)}) collective-permute-start(f16[2,176,1024]{2,1,0:T(8,128)(2,1)S(1)} %add_convert_fusion.1), channel_id=1, source_target_pairs={{0,64},{32,96},{64,0},{96,32},{1,65},{33,97},{65,1},{97,33},{2,66}... | collective-permute-start | bytes 2162696 | tf_op jit(solution)/shard_map/chips0/ppermute | solution.py:318
  54.3 7.4 %collective-permute-start.17 = (bf16[320,512]{1,0:T(8,128)(2,1)S(1)}, bf16[320,512]{1,0:T(8,128)(2,1)S(1)}, u32[]{:S(2)}, u32[]{:S(2)}) collective-permute-start(bf16[320,512]{1,0:T(8,128)(2,1)S(1)} %get-tuple-element.53.refs_1_), channel_id=1, source_target_pairs={{0,8},{8,16},{16,24},{24,0},{1,9},{9,17},{17,25},{25,1},{2,10},{10... | collective-permute-start | bytes 983048 | tf_op jit(solution)/shard_map/on1/ppermute | solution.py:312
  54.3 6.7 %collective-permute-start.18 = (bf16[320,512]{1,0:T(8,128)(2,1)S(1)}, bf16[320,512]{1,0:T(8,128)(2,1)S(1)}, u32[]{:S(2)}, u32[]{:S(2)}) collective-permute-start(bf16[320,512]{1,0:T(8,128)(2,1)S(1)} %get-tuple-element.55), channel_id=1, source_target_pairs={{0,24},{8,0},{16,8},{24,16},{1,25},{9,1},{17,9},{25,17},{2,26},{10... | collective-permute-start | bytes 983048 | tf_op jit(solution)/shard_map/on1/ppermute | solution.py:312
  57.0 16.1 %collective-permute-start.16 = (bf16[448,512]{1,0:T(8,128)(2,1)S(1)}, bf16[448,512]{1,0:T(8,128)(2,1)S(1)}, u32[]{:S(2)}, u32[]{:S(2)}) collective-permute-start(bf16[448,512]{1,0:T(8,128)(2,1)S(1)} %gap_ring2.1.refs_4_.refs_1_), channel_id=1, source_target_pairs={{0,24},{8,0},{16,8},{24,16},{1,25},{9,1},{17,9},{25,17},{2,26},{10... | collective-permute-start | bytes 1376264 | tf_op jit(solution)/shard_map/ring2/ppermute | solution.py:312
  57.8 15.3 %collective-permute-start.15 = (bf16[448,512]{1,0:T(8,128)(2,1)S(1)}, bf16[448,512]{1,0:T(8,128)(2,1)S(1)}, u32[]{:S(2)}, u32[]{:S(2)}) collective-permute-start(bf16[448,512]{1,0:T(8,128)(2,1)S(1)} %gap_ring2.1.refs_4_.refs_1_), channel_id=1, source_target_pairs={{0,8},{8,16},{16,24},{24,0},{1,9},{9,17},{17,25},{25,1},{2,10},{10... | collective-permute-start | bytes 1376264 | tf_op jit(solution)/shard_map/ring2/ppermute | solution.py:312
  64.2 10.3 %collective-permute-start.20 = (f16[2,160,1024]{2,1,0:T(8,128)(2,1)S(1)}, f16[2,160,1024]{2,1,0:T(8,128)(2,1)S(1)}, u32[]{:S(2)}, u32[]{:S(2)}) collective-permute-start(f16[2,160,1024]{2,1,0:T(8,128)(2,1)S(1)} %convert_element_type.72), channel_id=1, source_target_pairs={{0,32},{32,0},{64,96},{96,64},{1,33},{33,1},{65,97},{97,65},{2,34}... | collective-permute-start | bytes 1966088 | tf_op jit(solution)/shard_map/cores1/ppermute | solution.py:318
  73.2 11.0 %collective-permute-start.21 = (bf16[224,512]{1,0:T(8,128)(2,1)S(1)}, bf16[224,512]{1,0:T(8,128)(2,1)S(1)}, u32[]{:S(2)}, u32[]{:S(2)}) collective-permute-start(bf16[224,512]{1,0:T(8,128)(2,1)S(1)} %get-tuple-element.61.refs_1_), channel_id=1, source_target_pairs={{0,8},{8,16},{16,24},{24,0},{1,9},{9,17},{17,25},{25,1},{2,10},{10... | collective-permute-start | bytes 688136 | tf_op jit(solution)/shard_map/on2/ppermute | solution.py:312
  74.8 16.1 %collective-permute-start.27 = (f16[2,160,1024]{2,1,0:T(8,128)(2,1)S(1)}, f16[2,160,1024]{2,1,0:T(8,128)(2,1)S(1)}, u32[]{:S(2)}, u32[]{:S(2)}) collective-permute-start(f16[2,160,1024]{2,1,0:T(8,128)(2,1)S(1)} %add_convert_fusion.3), channel_id=1, source_target_pairs={{0,64},{32,96},{64,0},{96,32},{1,65},{33,97},{65,1},{97,33},{2,66}... | collective-permute-start | bytes 1966088 | tf_op jit(solution)/shard_map/chips1/ppermute | solution.py:318
  75.4 8.8 %collective-permute-start.22 = (bf16[224,512]{1,0:T(8,128)(2,1)S(1)}, bf16[224,512]{1,0:T(8,128)(2,1)S(1)}, u32[]{:S(2)}, u32[]{:S(2)}) collective-permute-start(bf16[224,512]{1,0:T(8,128)(2,1)S(1)} %get-tuple-element.64), channel_id=1, source_target_pairs={{0,24},{8,0},{16,8},{24,16},{1,25},{9,1},{17,9},{25,17},{2,26},{10... | collective-permute-start | bytes 688136 | tf_op jit(solution)/shard_map/on2/ppermute | solution.py:312
  80.9 5.3 %collective-permute-start.23 = (bf16[2,176,1024]{2,1,0:T(8,128)(2,1)S(1)}, bf16[2,176,1024]{2,1,0:T(8,128)(2,1)S(1)}, u32[]{:S(2)}, u32[]{:S(2)}) collective-permute-start(bf16[2,176,1024]{2,1,0:T(8,128)(2,1)S(1)} %gap3.1.refs_0_), channel_id=1, source_target_pairs={{0,32},{32,0},{64,96},{96,64},{1,33},{33,1},{65,97},{97,65},{2,34}... | collective-permute-start | bytes 2162696 | tf_op jit(solution)/shard_map/share0/ppermute | solution.py:318
  86.0 1.9 %collective-permute-start.24 = (f16[2,112,1024]{2,1,0:T(8,128)(2,1)S(1)}, f16[2,112,1024]{2,1,0:T(8,128)(2,1)S(1)}, u32[]{:S(2)}, u32[]{:S(2)}) collective-permute-start(f16[2,112,1024]{2,1,0:T(8,128)(2,1)S(1)} %convert_element_type.77), channel_id=1, source_target_pairs={{0,32},{32,0},{64,96},{96,64},{1,33},{33,1},{65,97},{97,65},{2,34}... | collective-permute-start | bytes 1376264 | tf_op jit(solution)/shard_map/cores2/ppermute | solution.py:318
  88.1 14.2 %collective-permute-start.25 = (f16[2,112,1024]{2,1,0:T(8,128)(2,1)S(1)}, f16[2,112,1024]{2,1,0:T(8,128)(2,1)S(1)}, u32[]{:S(2)}, u32[]{:S(2)}) collective-permute-start(f16[2,112,1024]{2,1,0:T(8,128)(2,1)S(1)} %add_convert_fusion.5), channel_id=1, source_target_pairs={{0,64},{32,96},{64,0},{96,32},{1,65},{33,97},{65,1},{97,33},{2,66}... | collective-permute-start | bytes 1376264 | tf_op jit(solution)/shard_map/chips2/ppermute | solution.py:318
  91.2 12.4 %collective-permute-start.28 = (bf16[2,160,1024]{2,1,0:T(8,128)(2,1)S(1)}, bf16[2,160,1024]{2,1,0:T(8,128)(2,1)S(1)}, u32[]{:S(2)}, u32[]{:S(2)}) collective-permute-start(bf16[2,160,1024]{2,1,0:T(8,128)(2,1)S(1)} %add_convert_fusion.2.refs_0_), channel_id=1, source_target_pairs={{0,32},{32,0},{64,96},{96,64},{1,33},{33,1},{65,97},{97,65},{2,34}... | collective-permute-start | bytes 1966088 | tf_op jit(solution)/shard_map/share1/ppermute | solution.py:318
  102.4 3.0 %collective-permute-start.26 = (bf16[2,112,1024]{2,1,0:T(8,128)(2,1)S(1)}, bf16[2,112,1024]{2,1,0:T(8,128)(2,1)S(1)}, u32[]{:S(2)}, u32[]{:S(2)}) collective-permute-start(bf16[2,112,1024]{2,1,0:T(8,128)(2,1)S(1)} %add_convert_fusion.4.refs_2_), channel_id=1, source_target_pairs={{0,32},{32,0},{64,96},{96,64},{1,33},{33,1},{65,97},{97,65},{2,34}... | collective-permute-start | bytes 1376264 | tf_op jit(solution)/shard_map/share2/ppermute | solution.py:318
